TPU v7x, 128 devices: a whole 4x4x4 slice. The times are simulated.
128 devices in a mesh: seq: 16 (over y_lo, z, core), head: 8 (over x, y_hi).
Axes of the slice: x: 4, y: 4 (y_hi: 2, y_lo: 2; y = y_hi * 2 + y_lo), z: 4, core: 2. Of those that a mesh axis runs over, the one named last changes fastest.
Arguments:
- hidden_states: bfloat16 [16384, 2048], P('seq'), may hold values from -6 to 6
- norm_gain: float32 [2048], replicated, may hold values from 0.1 to 1.9
- qkv_weight: bfloat16 [3, 2048, 2048], P(None, None, 'head'), may hold values from -1 to 1
- out_weight: bfloat16 [2048, 2048], P('head'), may hold values from -0.125 to 0.125
- selected_tiles: int32 [256, 32], P('seq'), may hold values from 0 to 255, as said below
- selected_count: int32 [256], P('seq'), may hold values from 1 to 32, as said below
Outputs:
- attended: bfloat16 [16384, 2048], P('seq', 'head')
Inputs may be any that keep to these rules, and one draw needn't show every extreme that they name: `selected_tiles`: entries 0 to 4 of a query tile's list are the tile itself and the tiles one before, one after, two before and two after it, clamped to the first and last tile; later entries may name any tile and may repeat. Only the first selected_count entries of a list are used; in every draw some tiles use all 32 entries.
All inputs are finite; a program needn't handle non-finite values.
Results may differ from a plain program's by a relative error of at most 0.0055.
The roundings to bfloat16 on the way count: a program that leaves them out, or rounds other values in their place, can miss the bound.
Values may be sent and summed in bfloat16 or wider, within the bound.
No kernel may reach another device: no remote copies, remote signals or barrier semaphores. Data moves between devices by JAX's collectives and lax.ppermute only.
A program may use at most 128 MiB of HBM per device.

v0:
```python
import jax
import jax.numpy as jnp
from jax import lax
from jax.sharding import PartitionSpec as P

HD = 128
TILE = 64
SEL = 32


EPSILON = 1e-06
NEGATIVE = -1e30


def normalize(hidden_states, norm_gain):
    values = hidden_states.astype(jnp.float32)
    spread = jnp.mean(values * values, axis=-1, keepdims=True)
    return (values * lax.rsqrt(spread + EPSILON) * norm_gain).astype(jnp.bfloat16)


def finish(summed, totals):
    return (summed / jnp.swapaxes(totals, -1, -2)[..., None]).astype(jnp.bfloat16)


def per_device(hidden_states, norm_gain, qkv_weight, out_weight, selected_tiles, selected_count):
    normed = normalize(hidden_states, norm_gain)
    projected = jnp.einsum(
        "td,mdc->mtc", normed, qkv_weight, preferred_element_type=jnp.float32
    ).astype(jnp.bfloat16)
    token_count = hidden_states.shape[0]
    columns = qkv_weight.shape[2]
    local_heads = columns // HD
    tile_local = token_count // TILE
    tile_total = tile_local * lax.axis_size("seq")
    block_tiles = max(512 // TILE, 1)
    block_count = tile_local // block_tiles
    queries = projected[0].reshape(block_count, block_tiles, TILE, local_heads, HD)
    everything = lax.all_gather(projected[1:], "seq", axis=1, tiled=True)
    key_tiles = everything[0].reshape(tile_total, TILE, local_heads, HD)
    value_tiles = everything[1].reshape(tile_total, TILE, local_heads, HD)
    list_blocks = selected_tiles.reshape(block_count, block_tiles, SEL)
    length_blocks = selected_count.reshape(block_count, block_tiles)

    def attend(operands):
        query_block, chosen, lengths = operands
        keyset = key_tiles[chosen].reshape(block_tiles, SEL * TILE, local_heads, HD)
        valueset = value_tiles[chosen].reshape(block_tiles, SEL * TILE, local_heads, HD)
        scores = jnp.einsum(
            "bqhd,bkhd->bhqk", query_block, keyset, preferred_element_type=jnp.float32
        ) * HD ** (-0.5)
        usable = jnp.repeat(
            jnp.arange(SEL, dtype=jnp.int32)[None, :] < lengths[:, None], TILE, axis=1
        )[:, None, None, :]
        scores = jnp.where(usable, scores, NEGATIVE)
        highest = jnp.max(scores, axis=-1, keepdims=True)
        expo = jnp.where(usable, jnp.exp(scores - highest), 0.0)
        totals = jnp.sum(expo, axis=-1)
        rounded = expo.astype(jnp.bfloat16)
        summed = jnp.einsum(
            "bhqk,bkhd->bqhd", rounded, valueset, preferred_element_type=jnp.float32
        )
        return finish(summed, totals)

    context = lax.map(attend, (queries, list_blocks, length_blocks))
    context = context.reshape(token_count, columns)
    partial_terms = jnp.dot(context, out_weight, preferred_element_type=jnp.float32)
    attended = lax.psum_scatter(partial_terms, "head", scatter_dimension=1, tiled=True)
    return attended.astype(jnp.bfloat16)


def solution(mesh):
    return jax.shard_map(
        per_device,
        mesh=mesh,
        in_specs=(
            P("seq", None),
            P(),
            P(None, None, "head"),
            P("head", None),
            P("seq", None),
            P("seq"),
        ),
        out_specs=P("seq", "head"),
        check_vma=False,
    )
```

profile of v0, /device:TPU:6, one launch (start us, length us, event | category | flops | bytes accessed | tf_op | source)
XLA Modules:
  0.0 416.7 jit_solution(210099622318272469)
XLA Ops:
  6.5 3.2 fusion.33
  9.8 5.7 %fusion.44 = bf16[3,1024,256]{2,1,0:T(8,128)(2,1)S(1)} fusion(bf16[3,2048,256]{2,1,0:T(8,128)(2,1)S(1)} %copy-done, bf16[1024,2048]{1,0:T(8,128)(2,1)} %param.8, f32[2048]{0:T(1024)} %param.9, f32[1024]{0:T(1024)S(1)} %add_rsqrt_fusion), kind=kOutput, calls=%fused_computation.38 | convolution fusion | flops 3230400512 | bytes 8925184 | tf_op jit(solution)/shard_map/td,mdc->mtc/dot_general | solution.py:27
  15.5 1.2 copy-done.2
  16.6 1.0 slice.20
  17.7 0.2 reduce-scatter.2.cloned.1.call-start
  17.9 1.1 slice.22
  19.1 0.1 reshape_squeeze.10
  19.2 92.6 %all-gather.2.cloned.1.call-done = bf16[2,16384,256]{2,1,0:T(8,128)(2,1)} async-done(((bf16[2,1024,256]{2,1,0:T(8,128)(2,1)}), bf16[2,16384,256]{2,1,0:T(8,128)(2,1)}) %all-gather.2.cloned.1.call-update) | async-done | bytes 16777232 | tf_op jit(solution)/shard_map/all_gather | solution.py:38
  111.8 11.3 %fusion.51 = (bf16[1,16384,256]{2,1,0:T(8,128)(2,1)}, bf16[1,16384,256]{2,1,0:T(8,128)(2,1)}) fusion(bf16[2,16384,256]{2,1,0:T(8,128)(2,1)} %all-gather.2.cloned.1.call-done), kind=kLoop, calls=%fused_computation.44 | loop fusion | bytes 33554432 | tf_op jit(solution)/shard_map/slice | solution.py:39
  123.1 12.5 %reshape_squeeze.11 = bf16[256,64,2,128]{3,2,1,0:T(2,128)(2,1)} reshape(bf16[1,16384,256]{2,1,0:T(8,128)(2,1)} %get-tuple-element.73) | data formatting | bytes 16777216 | tf_op jit(solution)/shard_map/reshape;squeeze | solution.py:39
  135.7 12.6 %reshape_squeeze.9 = bf16[256,64,2,128]{3,2,1,0:T(2,128)(2,1)} reshape(bf16[1,16384,256]{2,1,0:T(8,128)(2,1)} %get-tuple-element.74) | data formatting | bytes 16777216 | tf_op jit(solution)/shard_map/reshape;squeeze | solution.py:40
  148.3 139.1 %while.10 = (s32[]{:T(128)}, bf16[2,8,64,2,128]{4,3,2,1,0:T(2,128)(2,1)}, s32[2,8,32]{2,1,0:T(8,128)S(1)}, bf16[256,64,2,128]{3,2,1,0:T(2,128)(2,1)}, s32[2,8]{1...) while((s32[]{:T(128)}, ...), condition=%wide.region_4.5_spmd, body=%wide.region_1.4_spmd.sunk | while | flops 1090785280 | bytes 77156040 | solution.py:64
  148.4 0.1 broadcast_in_dim.60
  148.5 0.1 broadcast_in_dim.61
  148.7 0.2 constant_dynamic-slice_fusion.3
  148.9 25.4 %gather_fusion.1 = bf16[256,64,2,128]{3,2,1,0:T(2,128)(2,1)} fusion(bf16[256,64,2,128]{3,2,1,0:T(2,128)(2,1)} %get-tuple-element.146, s32[1024]{0:T(1024)S(1)} %pad_clamp_fusion.2), kind=kCustom, calls=%fused_computation.1.clone.1 | custom fusion | bytes 16778240 | tf_op jit(solution)/shard_map/while/body/eval_jaxpr/gather | solution.py:46
  174.2 6.4 %fusion.65 = f32[8,2,64,2048]{3,2,1,0:T(8,128)S(1)} fusion(bf16[8,2048,2,128]{3,2,1,0:T(2,128)(2,1)} %bitcast.58, bf16[1,8,64,2,128]{4,3,2,1,0:T(2,128)(2,1)S(1)} %constant_dynamic-slice_fusion.3), kind=kOutput, calls=%fused_computation.5.clone.1 | convolution fusion | flops 536870912 | bytes 17039360 | tf_op jit(solution)/shard_map/while/body/eval_jaxpr/bqhd,bkhd->bhqk/dot_general | solution.py:48
  180.6 4.8 %fusion.67 = (f32[8,2,64]{2,1,0:T(2,128)S(1)}, bf16[8,2,64,2048]{3,2,1,0:T(8,128)(2,1)}) fusion(f32[8,2,64,2048]{3,2,1,0:T(8,128)S(1)} %fusion.65, pred[8,2048]{1,0:T(8,128)(4,1)S(1)} %broadcast_in_dim.61), kind=kOutput, calls=%fused_computation.43.clone.1 | output fusion | flops 16779264 | bytes 12603392 | tf_op jit(solution)/shard_map/while/body/eval_jaxpr/sub | solution.py:56
  185.4 25.4 %gather_fusion = bf16[256,64,2,128]{3,2,1,0:T(2,128)(2,1)} fusion(bf16[256,64,2,128]{3,2,1,0:T(2,128)(2,1)} %get-tuple-element.143, s32[1024]{0:T(1024)S(1)} %pad_clamp_fusion.2), kind=kCustom, calls=%fused_computation.clone.1 | custom fusion | bytes 16778240 | tf_op jit(solution)/shard_map/while/body/eval_jaxpr/gather | solution.py:47
  210.7 6.1 %fusion.68 = bf16[1,8,64,2,128]{4,2,3,1,0:T(8,128)(2,1)S(1)} fusion(bf16[8,2048,2,128]{3,2,1,0:T(2,128)(2,1)} %bitcast.59, bf16[8,2,64,2048]{3,2,1,0:T(8,128)(2,1)} %get-tuple-element.122, f32[8,64,2]{1,2,0:T(2,128)S(1)} %bitcast.61), kind=kOutput, calls=%fused_computation.17.clone.1 | convolution fusion | flops 537133056 | bytes 12849152 | tf_op jit(solution)/shard_map/while/body/eval_jaxpr/bhqk,bkhd->bqhd/dot_general | solution.py:59
  216.8 1.0 copy_dynamic-update-slice_fusion.2
  218.1 0.1 broadcast_in_dim.61
  218.2 0.2 constant_dynamic-slice_fusion.3
  218.4 25.4 %gather_fusion.1 = bf16[256,64,2,128]{3,2,1,0:T(2,128)(2,1)} fusion(bf16[256,64,2,128]{3,2,1,0:T(2,128)(2,1)} %get-tuple-element.146, s32[1024]{0:T(1024)S(1)} %pad_clamp_fusion.2), kind=kCustom, calls=%fused_computation.1.clone.1 | custom fusion | bytes 16778240 | tf_op jit(solution)/shard_map/while/body/eval_jaxpr/gather | solution.py:46
  243.8 6.4 %fusion.65 = f32[8,2,64,2048]{3,2,1,0:T(8,128)S(1)} fusion(bf16[8,2048,2,128]{3,2,1,0:T(2,128)(2,1)} %bitcast.58, bf16[1,8,64,2,128]{4,3,2,1,0:T(2,128)(2,1)S(1)} %constant_dynamic-slice_fusion.3), kind=kOutput, calls=%fused_computation.5.clone.1 | convolution fusion | flops 536870912 | bytes 17039360 | tf_op jit(solution)/shard_map/while/body/eval_jaxpr/bqhd,bkhd->bhqk/dot_general | solution.py:48
  250.2 4.8 %fusion.67 = (f32[8,2,64]{2,1,0:T(2,128)S(1)}, bf16[8,2,64,2048]{3,2,1,0:T(8,128)(2,1)}) fusion(f32[8,2,64,2048]{3,2,1,0:T(8,128)S(1)} %fusion.65, pred[8,2048]{1,0:T(8,128)(4,1)S(1)} %broadcast_in_dim.61), kind=kOutput, calls=%fused_computation.43.clone.1 | output fusion | flops 16779264 | bytes 12603392 | tf_op jit(solution)/shard_map/while/body/eval_jaxpr/sub | solution.py:56
  254.9 25.4 %gather_fusion = bf16[256,64,2,128]{3,2,1,0:T(2,128)(2,1)} fusion(bf16[256,64,2,128]{3,2,1,0:T(2,128)(2,1)} %get-tuple-element.143, s32[1024]{0:T(1024)S(1)} %pad_clamp_fusion.2), kind=kCustom, calls=%fused_computation.clone.1 | custom fusion | bytes 16778240 | tf_op jit(solution)/shard_map/while/body/eval_jaxpr/gather | solution.py:47
  280.3 6.1 %fusion.68 = bf16[1,8,64,2,128]{4,2,3,1,0:T(8,128)(2,1)S(1)} fusion(bf16[8,2048,2,128]{3,2,1,0:T(2,128)(2,1)} %bitcast.59, bf16[8,2,64,2048]{3,2,1,0:T(8,128)(2,1)} %get-tuple-element.122, f32[8,64,2]{1,2,0:T(2,128)S(1)} %bitcast.61), kind=kOutput, calls=%fused_computation.17.clone.1 | convolution fusion | flops 537133056 | bytes 12849152 | tf_op jit(solution)/shard_map/while/body/eval_jaxpr/bhqk,bkhd->bqhd/dot_general | solution.py:59
  286.4 1.0 copy_dynamic-update-slice_fusion.2
  287.3 6.0 %fusion.47 = f32[1024,2048]{1,0:T(8,128)} fusion(bf16[256,2048]{1,0:T(8,128)(2,1)} %param.11, bf16[128,8,2,128]{3,2,1,0:T(2,128)(2,1)} %bitcast.13), kind=kOutput, calls=%fused_computation.39 | convolution fusion | flops 1073741824 | bytes 9961472 | tf_op jit(solution)/shard_map/dot_general | solution.py:66
  293.4 114.4 %reduce-scatter.2.cloned.1.call-done = f32[1024,256]{1,0:T(8,128)} async-done(((f32[1024,2048]{1,0:T(8,128)}), f32[1024,256]{1,0:T(8,128)}) %reduce-scatter.2.cloned.1.call-update) | async-done | bytes 1048592 | tf_op jit(solution)/shard_map/reduce_scatter | solution.py:67
  407.8 2.1 convert_element_type.25
  (26 shorter events, 0.6 us)
Async XLA Ops:
  6.5 3.2 copy-start
  6.5 105.3 %all-gather.2.cloned.1.call-start = ((), (), s32[]{:S(2)}) async-start(), calls=%async_computation.1 | async-start | bytes 17825792 | tf_op jit(solution)/shard_map/all_gather | solution.py:38
  9.8 9.2 %copy-start.4 = (s32[16]{0:T(128)S(1)}, s32[16]{0:T(128)}, u32[]{:S(2)}) copy-start(s32[16]{0:T(128)} %param.13) | copy-start | bytes 196
  15.5 1.2 copy-start.2
  17.7 390.1 %reduce-scatter.2.cloned.1.call-start = ((), (), s32[]{:S(2)}) async-start(), calls=%async_computation.2 | async-start | bytes 9437184 | tf_op jit(solution)/shard_map/reduce_scatter | solution.py:67
  135.7 12.6 %copy-start.3 = (s32[16,32]{1,0:T(8,128)S(1)}, s32[16,32]{1,0:T(8,128)}, u32[]{:S(2)}) copy-start(s32[16,32]{1,0:T(8,128)} %param.12) | copy-start | bytes 6148
  287.3 122.5 %copy-start.1 = (bf16[3,2048,256]{2,1,0:T(8,128)(2,1)S(1)}, bf16[3,2048,256]{2,1,0:T(8,128)(2,1)}, u32[]{:S(2)}) copy-start(bf16[3,2048,256]{2,1,0:T(8,128)(2,1)} %param.10) | copy-start | bytes 9437188
Sparse Core Ops, SparseCore 0:
  17.8 93.9 all-gather.1
  293.5 114.2 reduce-scatter.1
where the time goes:
time: 420 us; the launch traced here: 417 us
  waiting for transfers between devices  207 us (49%)
  local copies, waits for them, and re-layouts  144 us (34%)
  matrix products  36.6 us (9%)
  other arithmetic  15 us (4%)
  between operations  13.5 us (3%)
    reduce_scatter x1, waiting for transfers between devices, per_device(): lax.psum_scatter(partial_terms, 'head', scatter_dimension=1, tiled=True)  114 us
    all_gather x1, waiting for transfers between devices, per_device(): everything = lax.all_gather(projected[1:], 'seq', axis=1, tiled=True)  92.6 us
    gather x2, local copies, waits for them, and re-layouts, attend(): keyset = key_tiles[chosen].reshape(block_tiles, SEL * TILE, local_heads, HD)  50.7 us
    gather x2, local copies, waits for them, and re-layouts, attend(): value_tiles[chosen].reshape(block_tiles, SEL * TILE, local_heads, HD)  50.7 us
    dot_general x2, matrix products, attend(): jnp.einsum('bqhd,bkhd->bhqk', query_block, keyset, preferred_element_type...  12.8 us
    another operation x1, local copies, waits for them, and re-layouts, per_device(): value_tiles = everything[1].reshape(tile_total, TILE, local_heads, HD)  12.6 us
    another operation x1, local copies, waits for them, and re-layouts, per_device(): key_tiles = everything[0].reshape(tile_total, TILE, local_heads, HD)  12.5 us
    dot_general x2, matrix products, attend(): jnp.einsum('bhqk,bkhd->bqhd', rounded, valueset, preferred_element_type=j...  12.1 us
  transfers between devices with their start and end apart: 2, of which 2 were waited for; matrix products, arithmetic and copies ran while one was open for 0% of the time, Pallas kernels for 0%

commit v1 on v0

v1 whole, which is shorter than its diff:
```python
import functools

import jax
import jax.numpy as jnp
from jax import lax
from jax.experimental import pallas as pl
from jax.experimental.pallas import tpu as pltpu
from jax.sharding import PartitionSpec as P

HD = 128
TILE = 64
SEL = 32
EPSILON = 1e-06
NEGATIVE = -1e30
EXPONENT = float(HD**-0.5 * 1.4426950408889634)
AXES = ("seq", "head")
GROUP = 4
ROWS = 4
VM = pl.BlockSpec(memory_space=pltpu.VMEM)
SM = pl.BlockSpec(memory_space=pltpu.SMEM)
ANY = pl.BlockSpec(memory_space=pl.ANY)


def coords(i):
    s, h = divmod(i, 8)
    yl, r = divmod(s, 8)
    z, c = divmod(r, 2)
    x, yh = divmod(h, 2)
    return x, yh, yl, z, c


def index(x, yh, yl, z, c):
    return ((yl * 4 + z) * 2 + c) * 8 + x * 2 + yh


def move(array, dx=0, dyh=0, dyl=0, dz=0, dc=0):
    pairs = []
    for i in range(128):
        x, yh, yl, z, c = coords(i)
        pairs.append((i, index((x + dx) % 4, yh ^ dyh, yl ^ dyl, (z + dz) % 4, c ^ dc)))
    return lax.ppermute(array, AXES, pairs)


def project_kernel(half_ref, h_ref, gain_ref, ko, vo, km, vm, qm, qo, kvo_ref, kvm_ref, qm_ref, qo_ref):
    values = h_ref[...].astype(jnp.float32)
    spread = jnp.mean(values * values, axis=-1, keepdims=True)
    normed = (values * lax.rsqrt(spread + EPSILON) * gain_ref[...]).astype(jnp.bfloat16)

    def pair(a, b):
        weight = jnp.concatenate([a[0], b[0]], axis=1)
        return jnp.dot(normed, weight, preferred_element_type=jnp.float32).astype(jnp.bfloat16)

    kvo_ref[...] = pair(ko, vo)
    kvm_ref[...] = pair(km, vm)
    both = pair(qm, qo)
    qm_ref[...] = both[:, :HD]
    qo_ref[...] = both[:, HD:]


def project(hidden, gain, weight, yl):
    rows, width = hidden.shape
    block = 256

    def part(member, flip):
        return pl.BlockSpec(
            (1, width, HD), lambda i, half: (member, 0, half[0] ^ flip)
        )

    out = lambda n: pl.BlockSpec((block, n), lambda i, half: (i, 0))
    return pl.pallas_call(
        project_kernel,
        grid_spec=pltpu.PrefetchScalarGridSpec(
            num_scalar_prefetch=1,
            grid=(rows // block,),
            in_specs=[
                pl.BlockSpec((block, width), lambda i, half: (i, 0)),
                pl.BlockSpec((1, width), lambda i, half: (0, 0)),
                part(1, 1), part(2, 1), part(1, 0), part(2, 0), part(0, 0), part(0, 1),
            ],
            out_specs=[out(256), out(256), out(HD), out(HD)],
        ),
        out_shape=[
            jax.ShapeDtypeStruct((rows, 256), jnp.bfloat16),
            jax.ShapeDtypeStruct((rows, 256), jnp.bfloat16),
            jax.ShapeDtypeStruct((rows, HD), jnp.bfloat16),
            jax.ShapeDtypeStruct((rows, HD), jnp.bfloat16),
        ],
        compiler_params=pltpu.CompilerParams(vmem_limit_bytes=40 * 2**20),
        cost_estimate=pl.CostEstimate(
            flops=2 * rows * width * 768, bytes_accessed=9 * 2**20, transcendentals=0
        ),
        name="project",
    )(jnp.reshape(yl, (1,)).astype(jnp.int32), hidden, gain.reshape(1, width),
      weight, weight, weight, weight, weight, weight)


def gathered(kv, list_ref, tile, group, half):
    parts = []
    for j in range(GROUP):
        row = pl.multiple_of(list_ref[tile, group * GROUP + j] * TILE, TILE)
        parts.append(kv[pl.ds(row, TILE), half * HD : half * HD + HD])
    return jnp.concatenate(parts, axis=0)


def query_rows(tile):
    return pl.ds(pl.multiple_of(tile * TILE, TILE), TILE)


def score_tile(tile, groups, list_ref, count_ref, q_ref, kv):
    q = q_ref[query_rows(tile), :]
    lane = lax.broadcasted_iota(jnp.int32, (TILE, GROUP * TILE), 1)
    out = []
    for g in range(groups):
        s = lax.dot_general(
            q, gathered(kv, list_ref, tile, g, 0), (((1,), (1,)), ((), ())),
            preferred_element_type=jnp.float32,
        )
        out.append(jnp.where(lane < (count_ref[tile] - GROUP * g) * TILE, s, NEGATIVE))
    return out


def highest_of(scores):
    parts = [s[:, k : k + HD] for s in scores for k in range(0, GROUP * TILE, HD)]
    return jnp.max(functools.reduce(jnp.maximum, parts), axis=-1, keepdims=True)


def context_tile(tile, scores, highest, list_ref, kv, o_ref):
    totals = summed = 0.0
    for g, s in enumerate(scores):
        weights = jnp.exp2((s - highest) * EXPONENT)
        for k in range(0, GROUP * TILE, HD):
            totals = totals + weights[:, k : k + HD]
        summed = summed + jnp.dot(
            weights.astype(jnp.bfloat16), gathered(kv, list_ref, tile, g, 1),
            preferred_element_type=jnp.float32,
        )
    totals = jnp.sum(totals, axis=-1, keepdims=True)
    o_ref[query_rows(tile), :] = (summed / totals).astype(jnp.bfloat16)


def attend_kernel(list_ref, count_ref, order_ref, qm_ref, qp_ref, *rest):
    pieces, (o_ref, kv, q_ref, sems) = rest[:16], rest[16:]
    rows = pieces[0].shape[0]
    copies = [
        pltpu.make_async_copy(piece, kv.at[pl.ds(k * rows, rows)], sems.at[k])
        for k, piece in enumerate(pieces)
    ]
    for copy in copies:
        copy.start()
    q_ref[:rows, :] = qm_ref[...]
    q_ref[rows:, :] = qp_ref[...]
    for copy in copies:
        copy.wait()
    tiles = q_ref.shape[0] // TILE

    @pl.loop(0, tiles // ROWS)
    def _(block):
        ids = [order_ref[block * ROWS + j] for j in range(ROWS)]
        longest = functools.reduce(jnp.maximum, [count_ref[t] for t in ids])
        needed = (longest + GROUP - 1) // GROUP
        for groups in range(1, SEL // GROUP + 1):

            @pl.when(needed == groups)
            def _():
                scores = [score_tile(t, groups, list_ref, count_ref, q_ref, kv) for t in ids]
                tops = [highest_of(s) for s in scores]
                for t, s, top in zip(ids, scores, tops):
                    context_tile(t, s, top, list_ref, kv, o_ref)


def attend(lists, counts, order, qm, qp, pieces):
    rows = qm.shape[0]
    return pl.pallas_call(
        attend_kernel,
        out_shape=jax.ShapeDtypeStruct((2 * rows, HD), jnp.bfloat16),
        in_specs=[SM, SM, SM, VM, VM] + [ANY] * 16,
        out_specs=VM,
        scratch_shapes=[
            pltpu.VMEM((16 * rows, 2 * HD), jnp.bfloat16),
            pltpu.VMEM((2 * rows, HD), jnp.bfloat16),
            pltpu.SemaphoreType.DMA((16,)),
        ],
        compiler_params=pltpu.CompilerParams(vmem_limit_bytes=48 * 2**20),
        cost_estimate=pl.CostEstimate(
            flops=4 * 2 * rows * SEL * TILE * HD, bytes_accessed=10 * 2**20,
            transcendentals=2 * rows * SEL * TILE,
        ),
        name="attend",
    )(lists, counts, order, qm, qp, *pieces)


def out_kernel(*refs):
    mine, partner, weights = refs[0:4], refs[4:8], refs[8:12]
    own_ref, swap_yh_ref, swap_yl_ref, swap_both_ref = refs[12:]
    weight = jnp.concatenate([w[...] for w in weights], axis=0)
    half = weight.shape[1] // 2
    m = jnp.dot(
        jnp.concatenate([r[...] for r in mine], axis=1), weight,
        preferred_element_type=jnp.float32,
    )
    own_ref[...] = m[:, :half]
    swap_yh_ref[...] = m[:, half:].astype(jnp.bfloat16)
    p = jnp.dot(
        jnp.concatenate([r[...] for r in partner], axis=1), weight,
        preferred_element_type=jnp.float32,
    )
    swap_yl_ref[...] = p[:, :half].astype(jnp.bfloat16)
    swap_both_ref[...] = p[:, half:].astype(jnp.bfloat16)


def out_project(contexts, weights):
    rows = contexts[0].shape[0] // 2
    block = 256
    steps = rows // block
    lower = pl.BlockSpec((block, HD), lambda i: (i, 0))
    upper = pl.BlockSpec((block, HD), lambda i: (i + steps, 0))
    whole = pl.BlockSpec(weights[0].shape, lambda i: (0, 0))
    out = pl.BlockSpec((block, 256), lambda i: (i, 0))
    return pl.pallas_call(
        out_kernel,
        grid=(steps,),
        in_specs=[lower] * 4 + [upper] * 4 + [whole] * 4,
        out_specs=[out] * 4,
        out_shape=[jax.ShapeDtypeStruct((rows, 256), jnp.float32)]
        + [jax.ShapeDtypeStruct((rows, 256), jnp.bfloat16)] * 3,
        cost_estimate=pl.CostEstimate(
            flops=2 * 2 * rows * 512 * 512, bytes_accessed=6 * 2**20, transcendentals=0
        ),
        name="out_project",
    )(*contexts, *contexts, *weights)


def per_device(hidden_states, norm_gain, qkv_weight, out_weight, selected_tiles, selected_count):
    seq = lax.axis_index("seq")
    head = lax.axis_index("head")
    yl, z, core = seq // 8, (seq % 8) // 2, seq % 2
    yh = head % 2

    def weight_block(x):
        own = lax.dynamic_slice(out_weight, (yl * HD, (x * 2 + yh) * 256), (HD, 256))
        other = lax.dynamic_slice(out_weight, (yl * HD, (x * 2 + 1 - yh) * 256), (HD, 256))
        return jnp.concatenate([own, other], axis=1)

    x = head // 2
    steps = (0, 1, 3, 2)
    out_weights = [
        weight_block(x) if d == 0 else move(weight_block((x + d) % 4), dx=d) for d in steps
    ]

    rows_here = selected_tiles.shape[0]
    packed = jnp.concatenate(
        [selected_tiles, selected_count[:, None], jnp.zeros((rows_here, 95), jnp.int32)], axis=1
    )
    packed = jnp.concatenate([packed, move(packed, dyl=1)], axis=0)
    counts = packed[:, SEL]
    tile = packed[:, :SEL]
    slab = tile // rows_here
    place = (((slab % 8 // 2 - z) % 4) * 2 + ((slab // 8) ^ yl)) * 2 + ((slab % 2) ^ core)
    lists = place * rows_here + tile % rows_here
    n = counts.shape[0]
    ids = jnp.arange(n, dtype=jnp.int32)
    before = (counts[None, :] > counts[:, None]) | (
        (counts[None, :] == counts[:, None]) & (ids[None, :] < ids[:, None])
    )
    rank = jnp.sum(before.astype(jnp.int32), axis=1)
    order = jnp.sum(jnp.where(rank[None, :] == ids[:, None], ids[None, :], 0), axis=1)

    kvo, kvm, qm, qo = project(hidden_states, norm_gain, qkv_weight, yl)

    kvp = move(kvo, dyl=1)
    up_m = move(kvm, dz=1)
    down_m = move(kvm, dz=-1)
    up_p = move(kvp, dz=1)
    down_p = move(kvp, dz=-1)
    far_m = move(up_m, dz=1)
    far_p = move(down_p, dz=-1)
    qp = move(qo, dyl=1)
    pieces = []
    for m, p in ((kvm, kvp), (down_m, down_p), (far_m, far_p), (up_m, up_p)):
        pieces += [m, move(m, dc=1), p, move(p, dc=1)]

    context = attend(lists, counts, order, qm, qp, pieces)

    contexts = [context] + [move(context, dx=d) for d in (1, 3, 2)]
    own, to_yh, to_yl, to_both = out_project(contexts, out_weights)
    total = own
    for block in (move(to_yl, dyl=1), move(to_both, dyl=1, dyh=1), move(to_yh, dyh=1)):
        total = total + block.astype(jnp.float32)
    return total.astype(jnp.bfloat16)


def solution(mesh):
    return jax.shard_map(
        per_device,
        mesh=mesh,
        in_specs=(
            P("seq", None),
            P(),
            P(None, None, "head"),
            P("head", None),
            P("seq", None),
            P("seq"),
        ),
        out_specs=P("seq", "head"),
        check_vma=False,
    )
```

time: 420 us -> 154 us (0.37)
  local copies, waits for them, and re-layouts: 144 us -> 11.2 us
  waiting for transfers between devices: 207 us -> 86.8 us
  matrix products: 36.6 us -> 0 us
  starting transfers between devices: 0.22 us -> 29.2 us
  Pallas kernels: 0 us -> 19.7 us
  between operations: 13.5 us -> 0.21 us
  other arithmetic: 15 us -> 3.46 us
    reduce_scatter x1 -> x0, waiting for transfers between devices: 114 us -> none  [per_device(): lax.psum_scatter(partial_terms, 'head', scatter_dimension=1, tiled=True)]
    gather x4 -> x0, local copies, waits for them, and re-layouts: 101 us -> none  [the longest x2 50.7 us: attend(): keyset = key_tiles[chosen].reshape(block_tiles, SEL * TILE, local_heads, HD)]
    all_gather x1 -> x0, waiting for transfers between devices: 92.6 us -> none  [per_device(): everything = lax.all_gather(projected[1:], 'seq', axis=1, tiled=True)]
    ppermute x0 -> x26, waiting for transfers between devices: none -> 86.8 us  [move(): return lax.ppermute(array, AXES, pairs)]
    dot_general x6 -> x0, matrix products: 36.6 us -> none  [the longest x2 12.8 us: attend(): jnp.einsum('bqhd,bkhd->bhqk', query_block, keyset, preferred_element_type...]
    ppermute x0 -> x26, starting transfers between devices: none -> 29.2 us  [move(): return lax.ppermute(array, AXES, pairs)]
    another operation x3 -> x0, local copies, waits for them, and re-layouts: 25.2 us -> none  [the longest x1 12.6 us: per_device(): value_tiles = everything[1].reshape(tile_total, TILE, local_heads, HD)]
    pallas_call x0 -> x3, Pallas kernels: none -> 19.7 us  [the longest x1 9.42 us: attend(): pl.pallas_call(attend_kernel, out_shape=jax.ShapeDtypeStruct((2 * rows, H...]
  transfers between devices with their start and end apart: 2 -> 26, of which waited for: 2 -> 12; matrix products, arithmetic and copies ran while one was open for 0% -> 1% of each run, Pallas kernels for 0% -> 0%
where the time goes in v1:
time: 154 us; the launch traced here: 151 us
  waiting for transfers between devices  86.8 us (56%)
  starting transfers between devices  29.2 us (19%)
  Pallas kernels  19.7 us (13%)
  local copies, waits for them, and re-layouts  11.2 us (7%)
  other arithmetic  3.46 us (2%)
    ppermute x26, waiting for transfers between devices, move(): return lax.ppermute(array, AXES, pairs)  86.8 us
    ppermute x26, starting transfers between devices, move(): return lax.ppermute(array, AXES, pairs)  29.2 us
    unnamed x42, local copies, waits for them, and re-layouts  10.8 us
    pallas_call x1, Pallas kernels, attend(): pl.pallas_call(attend_kernel, out_shape=jax.ShapeDtypeStruct((2 * rows, H...  9.42 us
    pallas_call x1, Pallas kernels, project(): pl.pallas_call(project_kernel, grid_spec=pltpu.PrefetchScalarGridSpec(num...  5.6 us
    pallas_call x1, Pallas kernels, out_project(): pl.pallas_call(out_kernel, grid=(steps,), in_specs=[lower] * 4 + [upper]...  4.73 us
  transfers between devices with their start and end apart: 26, of which 12 were waited for; matrix products, arithmetic and copies ran while one was open for 1% of the time, Pallas kernels for 0%

profile of v1, /device:TPU:6, one launch (start us, length us, event | category | flops | bytes accessed | tf_op | source)
XLA Modules:
  0.0 150.6 jit_solution(5032857340058406664)
XLA Ops:
  0.0 1.9 %copy-done = bf16[3,2048,256]{2,1,0:T(8,128)(2,1)S(1)} copy-done((bf16[3,2048,256]{2,1,0:T(8,128)(2,1)S(1)}, bf16[3,2048,256]{2,1,0:T(8,128)(2,1)}, u32[]{:S(2)}) %copy-start) | copy-done | bytes 3145752
  1.9 2.2 %copy-done.2 = bf16[1024,2048]{1,0:T(8,128)(2,1)S(1)} copy-done((bf16[1024,2048]{1,0:T(8,128)(2,1)S(1)}, bf16[1024,2048]{1,0:T(8,128)(2,1)}, u32[]{:S(2)}) %copy-start.2) | copy-done | bytes 4194328
  4.8 5.6 %project.1 = (bf16[1024,256]{1,0:T(8,128)(2,1)S(1)}, bf16[1024,256]{1,0:T(8,128)(2,1)S(1)}, bf16[1024,128]{1,0:T(8,128)(2,1)S(1)}, bf16[1024,128]{1,0:T(8,128)(2,1)S(1)}) custom-call(s32[1]{0:T(128)} %bitcast.1.half_ref, bf16[1024,2048]{1,0:T(8,128)(2,1)S(1)} %copy-done.2, f32[1,2048]{1,0:T(1,128)S(1)} %bitcast.3, bf16[3,2048,256]{2,1,0:T(8,128)(2,1)S(1)} %copy-done, ...), custom_call_target="tpu_custom_call" | custom-call | flops 3221225472 | bytes 9437184 | tf_op jit(solution)/shard_map/project/pallas_call | solution.py:70
  10.4 1.6 %collective-permute-start.3 = (bf16[1024,256]{1,0:T(8,128)(2,1)S(1)}, bf16[1024,256]{1,0:T(8,128)(2,1)S(1)}, u32[]{:S(2)}, u32[]{:S(2)}) collective-permute-start(bf16[1024,256]{1,0:T(8,128)(2,1)S(1)} %get-tuple-element.16), channel_id=1, source_target_pairs={{0,64},{1,65},{2,66},{3,67},{4,68},{5,69},{6,70},{7,71},{8,72},{9,... | collective-permute-start | bytes 1572872 | tf_op jit(solution)/shard_map/ppermute | solution.py:41
  12.0 4.0 %collective-permute-start.5 = (bf16[1024,256]{1,0:T(8,128)(2,1)S(1)}, bf16[1024,256]{1,0:T(8,128)(2,1)S(1)}, u32[]{:S(2)}, u32[]{:S(2)}) collective-permute-start(bf16[1024,256]{1,0:T(8,128)(2,1)S(1)} %get-tuple-element.15.rest_0_), channel_id=1, source_target_pairs={{0,48},{1,49},{2,50},{3,51},{4,52},{5,53},{6,54},{7,55},{8,56},{9,... | collective-permute-start | bytes 1572872 | tf_op jit(solution)/shard_map/ppermute | solution.py:41
  16.1 8.0 %collective-permute-done.3.rest_2_ = bf16[1024,256]{1,0:T(8,128)(2,1)S(1)} collective-permute-done((bf16[1024,256]{1,0:T(8,128)(2,1)S(1)}, bf16[1024,256]{1,0:T(8,128)(2,1)S(1)}, u32[]{:S(2)}, u32[]{:S(2)}) %collective-permute-start.3) | collective-permute-done | bytes 524320 | tf_op jit(solution)/shard_map/ppermute | solution.py:41
  24.1 4.1 %collective-permute-start.7 = (bf16[1024,256]{1,0:T(8,128)(2,1)S(1)}, bf16[1024,256]{1,0:T(8,128)(2,1)S(1)}, u32[]{:S(2)}, u32[]{:S(2)}) collective-permute-start(bf16[1024,256]{1,0:T(8,128)(2,1)S(1)} %collective-permute-done.3.rest_2_), channel_id=1, source_target_pairs={{0,48},{1,49},{2,50},{3,51},{4,52},{5,53},{6,54},{7,55},{8,56},{9,... | collective-permute-start | bytes 1572872 | tf_op jit(solution)/shard_map/ppermute | solution.py:41
  28.3 1.6 %collective-permute-start = (s32[16,128]{1,0:T(8,128)S(1)}, s32[16,128]{1,0:T(8,128)S(1)}, u32[]{:S(2)}, u32[]{:S(2)}) collective-permute-start(s32[16,128]{1,0:T(8,128)S(1)} %pad_add_fusion.1), channel_id=1, source_target_pairs={{0,64},{1,65},{2,66},{3,67},{4,68},{5,69},{6,70},{7,71},{8,72},{9,... | collective-permute-start | bytes 24584 | tf_op jit(solution)/shard_map/ppermute | solution.py:41
  29.9 2.1 %collective-permute-done = s32[16,128]{1,0:T(8,128)S(1)} collective-permute-done((s32[16,128]{1,0:T(8,128)S(1)}, s32[16,128]{1,0:T(8,128)S(1)}, u32[]{:S(2)}, u32[]{:S(2)}) %collective-permute-start) | collective-permute-done | bytes 8224 | tf_op jit(solution)/shard_map/ppermute | solution.py:41
  32.0 1.6 %collective-permute-start.1 = (bf16[1024,128]{1,0:T(8,128)(2,1)S(1)}, bf16[1024,128]{1,0:T(8,128)(2,1)S(1)}, u32[]{:S(2)}, u32[]{:S(2)}) collective-permute-start(bf16[1024,128]{1,0:T(8,128)(2,1)S(1)} %get-tuple-element.14), channel_id=1, source_target_pairs={{0,64},{1,65},{2,66},{3,67},{4,68},{5,69},{6,70},{7,71},{8,72},{9,... | collective-permute-start | bytes 786440 | tf_op jit(solution)/shard_map/ppermute | solution.py:41
  33.6 4.8 %collective-permute-done.1.qp_ref = bf16[1024,128]{1,0:T(8,128)(2,1)S(1)} collective-permute-done((bf16[1024,128]{1,0:T(8,128)(2,1)S(1)}, bf16[1024,128]{1,0:T(8,128)(2,1)S(1)}, u32[]{:S(2)}, u32[]{:S(2)}) %collective-permute-start.1) | collective-permute-done | bytes 262176 | tf_op jit(solution)/shard_map/ppermute | solution.py:41
  39.7 3.2 %collective-permute-start.12 = (bf16[1024,256]{1,0:T(8,128)(2,1)S(1)}, bf16[1024,256]{1,0:T(8,128)(2,1)}, u32[]{:S(2)}, u32[]{:S(2)}) collective-permute-start(bf16[1024,256]{1,0:T(8,128)(2,1)S(1)} %collective-permute-done.7.rest_6_), channel_id=1, source_target_pairs={{0,48},{1,49},{2,50},{3,51},{4,52},{5,53},{6,54},{7,55},{8,56},{9,... | collective-permute-start | bytes 1572872 | tf_op jit(solution)/shard_map/ppermute | solution.py:41
  42.9 0.8 copy-done.3
  44.2 11.7 %collective-permute-done.10.rest_8_ = bf16[1024,256]{1,0:T(8,128)(2,1)} collective-permute-done((bf16[1024,256]{1,0:T(8,128)(2,1)}, bf16[1024,256]{1,0:T(8,128)(2,1)}, u32[]{:S(2)}, u32[]{:S(2)}) %collective-permute-start.10) | collective-permute-done | bytes 524320 | tf_op jit(solution)/shard_map/ppermute | solution.py:41
  55.9 10.4 %collective-permute-done.15.rest_14_ = bf16[1024,256]{1,0:T(8,128)(2,1)} collective-permute-done((bf16[1024,256]{1,0:T(8,128)(2,1)S(1)}, bf16[1024,256]{1,0:T(8,128)(2,1)}, u32[]{:S(2)}, u32[]{:S(2)}) %collective-permute-start.15) | collective-permute-done | bytes 524320 | tf_op jit(solution)/shard_map/ppermute | solution.py:41
  67.4 1.0 collective-permute-done.16.rest_15_
  69.9 1.0 copy-done.4
  71.0 0.9 copy-done.6
  71.9 9.4 %attend.1.refs_0_.refs_4_ = bf16[2048,128]{1,0:T(8,128)(2,1)S(1)} custom-call(s32[32,32]{1,0:T(8,128)S(1)} %get-tuple-element.29.list_ref, s32[32]{0:T(128)S(1)} %slice_reduce_fusion.count_ref, s32[32]{0:T(128)S(1)} %get-tuple-element.30.order_ref, bf16[1024,128]{1,0:T(8,128)(2,1)S(1)} %get-tuple-element.13.qm_ref, bf16[1024,128]{1,0:T(8,128)(2,1)S(1)} %copy-done.6, ...), custom_call_target="tpu_custom_call" | custom-call | flops 2147483648 | bytes 10485760 | tf_op jit(solution)/shard_map/attend/pallas_call | solution.py:173
  81.9 1.6 %collective-permute-start.18 = (bf16[2048,128]{1,0:T(8,128)(2,1)S(1)}, bf16[2048,128]{1,0:T(8,128)(2,1)S(1)}, u32[]{:S(2)}, u32[]{:S(2)}) collective-permute-start(bf16[2048,128]{1,0:T(8,128)(2,1)S(1)} %attend.1.refs_0_.refs_4_), channel_id=1, source_target_pairs={{0,6},{1,7},{2,0},{3,1},{4,2},{5,3},{6,4},{7,5},{8,14},{9,15},{10,... | collective-permute-start | bytes 1572872 | tf_op jit(solution)/shard_map/ppermute | solution.py:41
  83.5 1.4 collective-permute-start.19
  85.0 2.1 %collective-permute-start.20 = (bf16[128,512]{1,0:T(8,128)(2,1)S(1)}, bf16[128,512]{1,0:T(8,128)(2,1)S(1)}, u32[]{:S(2)}, u32[]{:S(2)}) collective-permute-start(bf16[128,512]{1,0:T(8,128)(2,1)S(1)} %pad_maximum_fusion.1), channel_id=1, source_target_pairs={{0,2},{1,3},{2,4},{3,5},{4,6},{5,7},{6,0},{7,1},{8,10},{9,11},{10,... | collective-permute-start | bytes 393224 | tf_op jit(solution)/shard_map/ppermute | solution.py:41
  87.2 22.5 %collective-permute-done.20.refs_9_ = bf16[128,512]{1,0:T(8,128)(2,1)S(1)} collective-permute-done((bf16[128,512]{1,0:T(8,128)(2,1)S(1)}, bf16[128,512]{1,0:T(8,128)(2,1)S(1)}, u32[]{:S(2)}, u32[]{:S(2)}) %collective-permute-start.20) | collective-permute-done | bytes 131104 | tf_op jit(solution)/shard_map/ppermute | solution.py:41
  109.7 1.4 collective-permute-start.22
  111.8 4.4 %collective-permute-done.22.refs_11_ = bf16[128,512]{1,0:T(8,128)(2,1)S(1)} collective-permute-done((bf16[128,512]{1,0:T(8,128)(2,1)S(1)}, bf16[128,512]{1,0:T(8,128)(2,1)S(1)}, u32[]{:S(2)}, u32[]{:S(2)}) %collective-permute-start.22) | collective-permute-done | bytes 131104 | tf_op jit(solution)/shard_map/ppermute | solution.py:41
  117.2 0.8 copy-done.10
  118.0 4.7 %out_project.1 = (f32[1024,256]{1,0:T(8,128)}, bf16[1024,256]{1,0:T(8,128)(2,1)}, bf16[1024,256]{1,0:T(8,128)(2,1)}, bf16[1024,256]{1,0:T(8,128)(2,1)}) custom-call(bf16[2048,128]{1,0:T(8,128)(2,1)} %copy-done.1, bf16[2048,128]{1,0:T(8,128)(2,1)} %copy-done.8, bf16[2048,128]{1,0:T(8,128)(2,1)} %copy-done.9, bf16[2048,128]{1,0:T(8,128)(2,1)} %copy-done.10, ...), custom_call_target="tpu_custom_call" | custom-call | flops 1073741824 | bytes 6291456 | tf_op jit(solution)/shard_map/out_project/pallas_call | solution.py:219
  122.7 3.2 %collective-permute-start.25 = (bf16[1024,256]{1,0:T(8,128)(2,1)}, bf16[1024,256]{1,0:T(8,128)(2,1)S(1)}, u32[]{:S(2)}, u32[]{:S(2)}) collective-permute-start(bf16[1024,256]{1,0:T(8,128)(2,1)} %get-tuple-element.20), channel_id=1, source_target_pairs={{0,1},{1,0},{2,3},{3,2},{4,5},{5,4},{6,7},{7,6},{8,9},{9,8},{10,11... | collective-permute-start | bytes 1572872 | tf_op jit(solution)/shard_map/ppermute | solution.py:41
  126.0 1.1 collective-permute-start.24
  127.1 12.4 %collective-permute-done.25 = bf16[1024,256]{1,0:T(8,128)(2,1)S(1)} collective-permute-done((bf16[1024,256]{1,0:T(8,128)(2,1)}, bf16[1024,256]{1,0:T(8,128)(2,1)S(1)}, u32[]{:S(2)}, u32[]{:S(2)}) %collective-permute-start.25) | collective-permute-done | bytes 524320 | tf_op jit(solution)/shard_map/ppermute | solution.py:41
  139.4 8.5 %collective-permute-done.24 = bf16[1024,256]{1,0:T(8,128)(2,1)S(1)} collective-permute-done((bf16[1024,256]{1,0:T(8,128)(2,1)}, bf16[1024,256]{1,0:T(8,128)(2,1)S(1)}, u32[]{:S(2)}, u32[]{:S(2)}) %collective-permute-start.24) | collective-permute-done | bytes 524320 | tf_op jit(solution)/shard_map/ppermute | solution.py:41
  148.3 2.3 %add_convert_fusion = bf16[1024,256]{1,0:T(8,128)(2,1)} fusion(bf16[1024,256]{1,0:T(8,128)(2,1)S(1)} %collective-permute-done.25, bf16[1024,256]{1,0:T(8,128)(2,1)S(1)} %collective-permute-done.24, f32[1024,256]{1,0:T(8,128)} %get-tuple-element.17, bf16[1024,256]{1,0:T(8,128)(2,1)S(1)} %collective-permute-done.23), kind=kLoop, calls=%fused_computation | loop fusion | flops 1835008 | bytes 3145728 | tf_op jit(solution)/shard_map/convert_element_type | solution.py:289
  (78 shorter events, 8.1 us)
Async XLA Ops:
  4.8 23.4 %copy-start.20 = (s32[16]{0:T(128)S(1)}, s32[16]{0:T(128)}, u32[]{:S(2)}) copy-start(s32[16]{0:T(128)} %param.11) | copy-start | bytes 196
  4.8 23.5 %copy-start.19 = (s32[16,32]{1,0:T(8,128)S(1)}, s32[16,32]{1,0:T(8,128)}, u32[]{:S(2)}) copy-start(s32[16,32]{1,0:T(8,128)} %param.10) | copy-start | bytes 6148
  10.4 13.7 %collective-permute-start.3 = (bf16[1024,256]{1,0:T(8,128)(2,1)S(1)}, bf16[1024,256]{1,0:T(8,128)(2,1)S(1)}, u32[]{:S(2)}, u32[]{:S(2)}) collective-permute-start(bf16[1024,256]{1,0:T(8,128)(2,1)S(1)} %get-tuple-element.16), channel_id=1, source_target_pairs={{0,64},{1,65},{2,66},{3,67},{4,68},{5,69},{6,70},{7,71},{8,72},{9,... | collective-permute-start | bytes 1572872 | tf_op jit(solution)/shard_map/ppermute | solution.py:41
  12.0 27.1 %collective-permute-start.5 = (bf16[1024,256]{1,0:T(8,128)(2,1)S(1)}, bf16[1024,256]{1,0:T(8,128)(2,1)S(1)}, u32[]{:S(2)}, u32[]{:S(2)}) collective-permute-start(bf16[1024,256]{1,0:T(8,128)(2,1)S(1)} %get-tuple-element.15.rest_0_), channel_id=1, source_target_pairs={{0,48},{1,49},{2,50},{3,51},{4,52},{5,53},{6,54},{7,55},{8,56},{9,... | collective-permute-start | bytes 1572872 | tf_op jit(solution)/shard_map/ppermute | solution.py:41
  16.0 23.6 %collective-permute-start.9 = (bf16[1024,256]{1,0:T(8,128)(2,1)S(1)}, bf16[1024,256]{1,0:T(8,128)(2,1)}, u32[]{:S(2)}, u32[]{:S(2)}) collective-permute-start(bf16[1024,256]{1,0:T(8,128)(2,1)S(1)} %get-tuple-element.15.rest_0_), channel_id=1, source_target_pairs={{0,16},{1,17},{2,18},{3,19},{4,20},{5,21},{6,22},{7,23},{8,24},{9,... | collective-permute-start | bytes 1572872 | tf_op jit(solution)/shard_map/ppermute | solution.py:41
  16.1 23.6 %collective-permute-start.2 = (bf16[1024,256]{1,0:T(8,128)(2,1)S(1)}, bf16[1024,256]{1,0:T(8,128)(2,1)S(1)}, u32[]{:S(2)}, u32[]{:S(2)}) collective-permute-start(bf16[1024,256]{1,0:T(8,128)(2,1)S(1)} %get-tuple-element.15.rest_0_), channel_id=1, source_target_pairs={{0,8},{1,9},{2,10},{3,11},{4,12},{5,13},{6,14},{7,15},{8,0},{9,1},... | collective-permute-start | bytes 1572872 | tf_op jit(solution)/shard_map/ppermute | solution.py:41
  24.1 15.6 %collective-permute-start.7 = (bf16[1024,256]{1,0:T(8,128)(2,1)S(1)}, bf16[1024,256]{1,0:T(8,128)(2,1)S(1)}, u32[]{:S(2)}, u32[]{:S(2)}) collective-permute-start(bf16[1024,256]{1,0:T(8,128)(2,1)S(1)} %collective-permute-done.3.rest_2_), channel_id=1, source_target_pairs={{0,48},{1,49},{2,50},{3,51},{4,52},{5,53},{6,54},{7,55},{8,56},{9,... | collective-permute-start | bytes 1572872 | tf_op jit(solution)/shard_map/ppermute | solution.py:41
  28.3 3.7 %collective-permute-start = (s32[16,128]{1,0:T(8,128)S(1)}, s32[16,128]{1,0:T(8,128)S(1)}, u32[]{:S(2)}, u32[]{:S(2)}) collective-permute-start(s32[16,128]{1,0:T(8,128)S(1)} %pad_add_fusion.1), channel_id=1, source_target_pairs={{0,64},{1,65},{2,66},{3,67},{4,68},{5,69},{6,70},{7,71},{8,72},{9,... | collective-permute-start | bytes 24584 | tf_op jit(solution)/shard_map/ppermute | solution.py:41
  32.0 6.4 %collective-permute-start.1 = (bf16[1024,128]{1,0:T(8,128)(2,1)S(1)}, bf16[1024,128]{1,0:T(8,128)(2,1)S(1)}, u32[]{:S(2)}, u32[]{:S(2)}) collective-permute-start(bf16[1024,128]{1,0:T(8,128)(2,1)S(1)} %get-tuple-element.14), channel_id=1, source_target_pairs={{0,64},{1,65},{2,66},{3,67},{4,68},{5,69},{6,70},{7,71},{8,72},{9,... | collective-permute-start | bytes 786440 | tf_op jit(solution)/shard_map/ppermute | solution.py:41
  39.1 3.8 %collective-permute-start.4 = (bf16[1024,256]{1,0:T(8,128)(2,1)S(1)}, bf16[1024,256]{1,0:T(8,128)(2,1)S(1)}, u32[]{:S(2)}, u32[]{:S(2)}) collective-permute-start(bf16[1024,256]{1,0:T(8,128)(2,1)S(1)} %collective-permute-done.3.rest_2_), channel_id=1, source_target_pairs={{0,8},{1,9},{2,10},{3,11},{4,12},{5,13},{6,14},{7,15},{8,0},{9,1},... | collective-permute-start | bytes 1572872 | tf_op jit(solution)/shard_map/ppermute | solution.py:41
  39.1 4.6 %collective-permute-start.6 = (bf16[1024,256]{1,0:T(8,128)(2,1)S(1)}, bf16[1024,256]{1,0:T(8,128)(2,1)}, u32[]{:S(2)}, u32[]{:S(2)}) collective-permute-start(bf16[1024,256]{1,0:T(8,128)(2,1)S(1)} %collective-permute-done.5.rest_4_), channel_id=1, source_target_pairs={{0,8},{1,9},{2,10},{3,11},{4,12},{5,13},{6,14},{7,15},{8,0},{9,1},... | collective-permute-start | bytes 1572872 | tf_op jit(solution)/shard_map/ppermute | solution.py:41
  39.6 16.3 %collective-permute-start.10 = (bf16[1024,256]{1,0:T(8,128)(2,1)}, bf16[1024,256]{1,0:T(8,128)(2,1)}, u32[]{:S(2)}, u32[]{:S(2)}) collective-permute-start(bf16[1024,256]{1,0:T(8,128)(2,1)} %collective-permute-done.9.rest_12_), channel_id=1, source_target_pairs={{0,16},{1,17},{2,18},{3,19},{4,20},{5,21},{6,22},{7,23},{8,24},{9,... | collective-permute-start | bytes 1572872 | tf_op jit(solution)/shard_map/ppermute | solution.py:41
  39.6 26.7 %collective-permute-start.15 = (bf16[1024,256]{1,0:T(8,128)(2,1)S(1)}, bf16[1024,256]{1,0:T(8,128)(2,1)}, u32[]{:S(2)}, u32[]{:S(2)}) collective-permute-start(bf16[1024,256]{1,0:T(8,128)(2,1)S(1)} %collective-permute-done.3.rest_2_), channel_id=1, source_target_pairs={{0,16},{1,17},{2,18},{3,19},{4,20},{5,21},{6,22},{7,23},{8,24},{9,... | collective-permute-start | bytes 1572872 | tf_op jit(solution)/shard_map/ppermute | solution.py:41
  39.7 26.6 %collective-permute-start.12 = (bf16[1024,256]{1,0:T(8,128)(2,1)S(1)}, bf16[1024,256]{1,0:T(8,128)(2,1)}, u32[]{:S(2)}, u32[]{:S(2)}) collective-permute-start(bf16[1024,256]{1,0:T(8,128)(2,1)S(1)} %collective-permute-done.7.rest_6_), channel_id=1, source_target_pairs={{0,48},{1,49},{2,50},{3,51},{4,52},{5,53},{6,54},{7,55},{8,56},{9,... | collective-permute-start | bytes 1572872 | tf_op jit(solution)/shard_map/ppermute | solution.py:41
  43.7 23.7 %collective-permute-start.14 = (bf16[1024,256]{1,0:T(8,128)(2,1)}, bf16[1024,256]{1,0:T(8,128)(2,1)S(1)}, u32[]{:S(2)}, u32[]{:S(2)}) collective-permute-start(bf16[1024,256]{1,0:T(8,128)(2,1)} %collective-permute-done.9.rest_12_), channel_id=1, source_target_pairs={{0,8},{1,9},{2,10},{3,11},{4,12},{5,13},{6,14},{7,15},{8,0},{9,1},... | collective-permute-start | bytes 1572872 | tf_op jit(solution)/shard_map/ppermute | solution.py:41
  43.7 23.7 %collective-permute-start.8 = (bf16[1024,256]{1,0:T(8,128)(2,1)S(1)}, bf16[1024,256]{1,0:T(8,128)(2,1)S(1)}, u32[]{:S(2)}, u32[]{:S(2)}) collective-permute-start(bf16[1024,256]{1,0:T(8,128)(2,1)S(1)} %collective-permute-done.7.rest_6_), channel_id=1, source_target_pairs={{0,8},{1,9},{2,10},{3,11},{4,12},{5,13},{6,14},{7,15},{8,0},{9,1},... | collective-permute-start | bytes 1572872 | tf_op jit(solution)/shard_map/ppermute | solution.py:41
  55.9 11.5 %collective-permute-start.11 = (bf16[1024,256]{1,0:T(8,128)(2,1)}, bf16[1024,256]{1,0:T(8,128)(2,1)S(1)}, u32[]{:S(2)}, u32[]{:S(2)}) collective-permute-start(bf16[1024,256]{1,0:T(8,128)(2,1)} %collective-permute-done.10.rest_8_), channel_id=1, source_target_pairs={{0,8},{1,9},{2,10},{3,11},{4,12},{5,13},{6,14},{7,15},{8,0},{9,1},... | collective-permute-start | bytes 1572872 | tf_op jit(solution)/shard_map/ppermute | solution.py:41
  66.3 2.1 %collective-permute-start.16 = (bf16[1024,256]{1,0:T(8,128)(2,1)}, bf16[1024,256]{1,0:T(8,128)(2,1)S(1)}, u32[]{:S(2)}, u32[]{:S(2)}) collective-permute-start(bf16[1024,256]{1,0:T(8,128)(2,1)} %collective-permute-done.15.rest_14_), channel_id=1, source_target_pairs={{0,8},{1,9},{2,10},{3,11},{4,12},{5,13},{6,14},{7,15},{8,0},{9,1},... | collective-permute-start | bytes 1572872 | tf_op jit(solution)/shard_map/ppermute | solution.py:41
  66.3 2.9 %collective-permute-start.13 = (bf16[1024,256]{1,0:T(8,128)(2,1)}, bf16[1024,256]{1,0:T(8,128)(2,1)S(1)}, u32[]{:S(2)}, u32[]{:S(2)}) collective-permute-start(bf16[1024,256]{1,0:T(8,128)(2,1)} %collective-permute-done.12.rest_10_), channel_id=1, source_target_pairs={{0,8},{1,9},{2,10},{3,11},{4,12},{5,13},{6,14},{7,15},{8,0},{9,1},... | collective-permute-start | bytes 1572872 | tf_op jit(solution)/shard_map/ppermute | solution.py:41
  71.9 13.0 %copy-start.15 = (bf16[256,2048]{1,0:T(8,128)(2,1)S(1)}, bf16[256,2048]{1,0:T(8,128)(2,1)}, u32[]{:S(2)}) copy-start(bf16[256,2048]{1,0:T(8,128)(2,1)} %param.9) | copy-start | bytes 3145732
  81.4 34.8 %copy-start.1 = (bf16[2048,128]{1,0:T(8,128)(2,1)}, bf16[2048,128]{1,0:T(8,128)(2,1)S(1)}, u32[]{:S(2)}) copy-start(bf16[2048,128]{1,0:T(8,128)(2,1)S(1)} %attend.1.refs_0_.refs_4_) | copy-start | bytes 1572868
  81.4 34.8 %collective-permute-start.17 = (bf16[2048,128]{1,0:T(8,128)(2,1)S(1)}, bf16[2048,128]{1,0:T(8,128)(2,1)S(1)}, u32[]{:S(2)}, u32[]{:S(2)}) collective-permute-start(bf16[2048,128]{1,0:T(8,128)(2,1)S(1)} %attend.1.refs_0_.refs_4_), channel_id=1, source_target_pairs={{0,2},{1,3},{2,4},{3,5},{4,6},{5,7},{6,0},{7,1},{8,10},{9,11},{10,... | collective-permute-start | bytes 1572872 | tf_op jit(solution)/shard_map/ppermute | solution.py:41
  81.9 34.3 %collective-permute-start.18 = (bf16[2048,128]{1,0:T(8,128)(2,1)S(1)}, bf16[2048,128]{1,0:T(8,128)(2,1)S(1)}, u32[]{:S(2)}, u32[]{:S(2)}) collective-permute-start(bf16[2048,128]{1,0:T(8,128)(2,1)S(1)} %attend.1.refs_0_.refs_4_), channel_id=1, source_target_pairs={{0,6},{1,7},{2,0},{3,1},{4,2},{5,3},{6,4},{7,5},{8,14},{9,15},{10,... | collective-permute-start | bytes 1572872 | tf_op jit(solution)/shard_map/ppermute | solution.py:41
  83.5 32.7 %collective-permute-start.19 = (bf16[2048,128]{1,0:T(8,128)(2,1)S(1)}, bf16[2048,128]{1,0:T(8,128)(2,1)S(1)}, u32[]{:S(2)}, u32[]{:S(2)}) collective-permute-start(bf16[2048,128]{1,0:T(8,128)(2,1)S(1)} %attend.1.refs_0_.refs_4_), channel_id=1, source_target_pairs={{0,4},{1,5},{2,6},{3,7},{4,0},{5,1},{6,2},{7,3},{8,12},{9,13},{10,... | collective-permute-start | bytes 1572872 | tf_op jit(solution)/shard_map/ppermute | solution.py:41
  85.0 24.7 %collective-permute-start.20 = (bf16[128,512]{1,0:T(8,128)(2,1)S(1)}, bf16[128,512]{1,0:T(8,128)(2,1)S(1)}, u32[]{:S(2)}, u32[]{:S(2)}) collective-permute-start(bf16[128,512]{1,0:T(8,128)(2,1)S(1)} %pad_maximum_fusion.1), channel_id=1, source_target_pairs={{0,2},{1,3},{2,4},{3,5},{4,6},{5,7},{6,0},{7,1},{8,10},{9,11},{10,... | collective-permute-start | bytes 393224 | tf_op jit(solution)/shard_map/ppermute | solution.py:41
  87.1 24.6 %collective-permute-start.21 = (bf16[128,512]{1,0:T(8,128)(2,1)S(1)}, bf16[128,512]{1,0:T(8,128)(2,1)S(1)}, u32[]{:S(2)}, u32[]{:S(2)}) collective-permute-start(bf16[128,512]{1,0:T(8,128)(2,1)S(1)} %pad_maximum_fusion.2), channel_id=1, source_target_pairs={{0,6},{1,7},{2,0},{3,1},{4,2},{5,3},{6,4},{7,5},{8,14},{9,15},{10,... | collective-permute-start | bytes 393224 | tf_op jit(solution)/shard_map/ppermute | solution.py:41
  109.7 6.5 %copy-start.16 = (bf16[128,512]{1,0:T(8,128)(2,1)}, bf16[128,512]{1,0:T(8,128)(2,1)S(1)}, u32[]{:S(2)}) copy-start(bf16[128,512]{1,0:T(8,128)(2,1)S(1)} %collective-permute-done.20.refs_9_) | copy-start | bytes 393220
  109.7 6.5 %collective-permute-start.22 = (bf16[128,512]{1,0:T(8,128)(2,1)S(1)}, bf16[128,512]{1,0:T(8,128)(2,1)S(1)}, u32[]{:S(2)}, u32[]{:S(2)}) collective-permute-start(bf16[128,512]{1,0:T(8,128)(2,1)S(1)} %pad_maximum_fusion.3), channel_id=1, source_target_pairs={{0,4},{1,5},{2,6},{3,7},{4,0},{5,1},{6,2},{7,3},{8,12},{9,13},{10,... | collective-permute-start | bytes 393224 | tf_op jit(solution)/shard_map/ppermute | solution.py:41
  111.8 4.5 %copy-start.17 = (bf16[128,512]{1,0:T(8,128)(2,1)}, bf16[128,512]{1,0:T(8,128)(2,1)S(1)}, u32[]{:S(2)}) copy-start(bf16[128,512]{1,0:T(8,128)(2,1)S(1)} %collective-permute-done.21.refs_10_) | copy-start | bytes 393220
  122.7 16.7 %collective-permute-start.25 = (bf16[1024,256]{1,0:T(8,128)(2,1)}, bf16[1024,256]{1,0:T(8,128)(2,1)S(1)}, u32[]{:S(2)}, u32[]{:S(2)}) collective-permute-start(bf16[1024,256]{1,0:T(8,128)(2,1)} %get-tuple-element.20), channel_id=1, source_target_pairs={{0,1},{1,0},{2,3},{3,2},{4,5},{5,4},{6,7},{7,6},{8,9},{9,8},{10,11... | collective-permute-start | bytes 1572872 | tf_op jit(solution)/shard_map/ppermute | solution.py:41
  126.0 22.0 %collective-permute-start.24 = (bf16[1024,256]{1,0:T(8,128)(2,1)}, bf16[1024,256]{1,0:T(8,128)(2,1)S(1)}, u32[]{:S(2)}, u32[]{:S(2)}) collective-permute-start(bf16[1024,256]{1,0:T(8,128)(2,1)} %get-tuple-element.19), channel_id=1, source_target_pairs={{0,65},{1,64},{2,67},{3,66},{4,69},{5,68},{6,71},{7,70},{8,73},{9,... | collective-permute-start | bytes 1572872 | tf_op jit(solution)/shard_map/ppermute | solution.py:41
  127.0 21.3 %collective-permute-start.23 = (bf16[1024,256]{1,0:T(8,128)(2,1)}, bf16[1024,256]{1,0:T(8,128)(2,1)S(1)}, u32[]{:S(2)}, u32[]{:S(2)}) collective-permute-start(bf16[1024,256]{1,0:T(8,128)(2,1)} %get-tuple-element.18), channel_id=1, source_target_pairs={{0,64},{1,65},{2,66},{3,67},{4,68},{5,69},{6,70},{7,71},{8,72},{9,... | collective-permute-start | bytes 1572872 | tf_op jit(solution)/shard_map/ppermute | solution.py:41
  (15 other events, 16.6 us)

commit v2 on v1

v2 whole, which is shorter than its diff:
```python
import functools

import jax
import jax.numpy as jnp
from jax import lax
from jax.experimental import pallas as pl
from jax.experimental.pallas import tpu as pltpu
from jax.sharding import PartitionSpec as P

D = 2048
HD = 128
TILE = 64
SEL = 32
EPSILON = 1e-06
NEGATIVE = -1e30
EXPONENT = float(HD**-0.5 * 1.4426950408889634)
AXES = ("seq", "head")
GROUP = 4
ROWS = 4
VM = pl.BlockSpec(memory_space=pltpu.VMEM)
SM = pl.BlockSpec(memory_space=pltpu.SMEM)
ANY = pl.BlockSpec(memory_space=pl.ANY)
PROJECT_VMEM = 60 * 2**20
ATTEND_VMEM = 24 * 2**20
OUT_VMEM = 12 * 2**20
CHUNKS = 2


def coords(i):
    s, h = divmod(i, 8)
    yl, r = divmod(s, 8)
    z, c = divmod(r, 2)
    x, yh = divmod(h, 2)
    return x, yh, yl, z, c


def index(x, yh, yl, z, c):
    return ((yl * 4 + z) * 2 + c) * 8 + x * 2 + yh


def move(array, dx=0, dyh=0, dyl=0, dz=0, dc=0):
    pairs = []
    for i in range(128):
        x, yh, yl, z, c = coords(i)
        pairs.append((i, index((x + dx) % 4, yh ^ dyh, yl ^ dyl, (z + dz) % 4, c ^ dc)))
    return lax.ppermute(array, AXES, pairs)


def first_kernel(half_ref, h_ref, gain_ref, ko, vo, km, vm, normed_ref, kvo_ref, kvm_ref):
    values = h_ref[...].astype(jnp.float32)
    spread = jnp.mean(values * values, axis=-1, keepdims=True)
    normed = (values * lax.rsqrt(spread + EPSILON) * gain_ref[...]).astype(jnp.bfloat16)
    normed_ref[...] = normed
    for k_ref, v_ref, out_ref in ((ko, vo, kvo_ref), (km, vm, kvm_ref)):
        weight = jnp.concatenate([k_ref[0], v_ref[0]], axis=1)
        both = jnp.dot(normed, weight, preferred_element_type=jnp.float32)
        out_ref[...] = both.astype(jnp.bfloat16)


def second_kernel(half_ref, normed_ref, qm, qo, qm_ref, qo_ref):
    weight = jnp.concatenate([qm[0], qo[0]], axis=1)
    both = jnp.dot(normed_ref[...], weight, preferred_element_type=jnp.float32)
    both = both.astype(jnp.bfloat16)
    qm_ref[...] = both[:, :HD]
    qo_ref[...] = both[:, HD:]


def project(kernel, operands, weight, half, parts, outs):
    rows, width = operands[0].shape
    block = 512

    def part(member, flip):
        return pl.BlockSpec((1, width, HD), lambda i, half: (member, 0, half[0] ^ flip))

    def rows_of(n):
        return pl.BlockSpec((block, n), lambda i, half: (i, 0))

    return pl.pallas_call(
        kernel,
        grid_spec=pltpu.PrefetchScalarGridSpec(
            num_scalar_prefetch=1,
            grid=(rows // block,),
            in_specs=[rows_of(width)]
            + [pl.BlockSpec((1, width), lambda i, half: (0, 0))] * (len(operands) - 1)
            + [part(*p) for p in parts],
            out_specs=[rows_of(n) for n in outs],
        ),
        out_shape=[jax.ShapeDtypeStruct((rows, n), jnp.bfloat16) for n in outs],
        compiler_params=pltpu.CompilerParams(vmem_limit_bytes=PROJECT_VMEM),
        cost_estimate=pl.CostEstimate(
            flops=2 * rows * width * HD * len(parts), bytes_accessed=9 * 2**20, transcendentals=0
        ),
        name="project",
    )(half, *operands, *[weight] * len(parts))


def gathered(kv_ref, list_ref, tile, group, half):
    parts = []
    for j in range(GROUP):
        row = pl.multiple_of(list_ref[tile, group * GROUP + j] * TILE, TILE)
        parts.append(kv_ref[pl.ds(row, TILE), half * HD : half * HD + HD])
    return jnp.concatenate(parts, axis=0)


def query_rows(tile):
    return pl.ds(pl.multiple_of(tile * TILE, TILE), TILE)


def score_tile(tile, groups, list_ref, count_ref, q_ref, kv_ref):
    q = q_ref[query_rows(tile), :]
    lane = lax.broadcasted_iota(jnp.int32, (TILE, GROUP * TILE), 1)
    out = []
    for g in range(groups):
        s = lax.dot_general(
            q, gathered(kv_ref, list_ref, tile, g, 0), (((1,), (1,)), ((), ())),
            preferred_element_type=jnp.float32,
        )
        out.append(jnp.where(lane < (count_ref[tile] - GROUP * g) * TILE, s, NEGATIVE))
    return out


def highest_of(scores):
    parts = [s[:, k : k + HD] for s in scores for k in range(0, GROUP * TILE, HD)]
    return jnp.max(functools.reduce(jnp.maximum, parts), axis=-1, keepdims=True)


def context_tile(tile, scores, highest, list_ref, kv_ref, o_ref):
    totals = summed = 0.0
    for g, s in enumerate(scores):
        weights = jnp.exp2((s - highest) * EXPONENT)
        for k in range(0, GROUP * TILE, HD):
            totals = totals + weights[:, k : k + HD]
        summed = summed + jnp.dot(
            weights.astype(jnp.bfloat16), gathered(kv_ref, list_ref, tile, g, 1),
            preferred_element_type=jnp.float32,
        )
    totals = jnp.sum(totals, axis=-1, keepdims=True)
    o_ref[query_rows(tile), :] = (summed / totals).astype(jnp.bfloat16)


def attend_kernel(list_ref, count_ref, order_ref, qm_ref, qp_ref, *rest):
    pieces, rest = rest[:16], rest[16:]
    outs, (kv_ref, q_ref, o_ref, sems) = rest[: 2 * CHUNKS], rest[2 * CHUNKS :]
    rows = pieces[0].shape[0]
    copies = [
        pltpu.make_async_copy(piece, kv_ref.at[pl.ds(k * rows, rows)], sems.at[k])
        for k, piece in enumerate(pieces)
    ]
    for copy in copies:
        copy.start()
    q_ref[:rows, :] = qm_ref[...]
    q_ref[rows:, :] = qp_ref[...]
    for copy in copies:
        copy.wait()
    tiles = q_ref.shape[0] // TILE

    @pl.loop(0, tiles // ROWS)
    def _(block):
        ids = [order_ref[block * ROWS + j] for j in range(ROWS)]
        longest = functools.reduce(jnp.maximum, [count_ref[t] for t in ids])
        needed = (longest + GROUP - 1) // GROUP
        for groups in range(1, SEL // GROUP + 1):

            @pl.when(needed == groups)
            def _():
                scores = [score_tile(t, groups, list_ref, count_ref, q_ref, kv_ref) for t in ids]
                tops = [highest_of(s) for s in scores]
                for t, s, top in zip(ids, scores, tops):
                    context_tile(t, s, top, list_ref, kv_ref, o_ref)


    part = outs[0].shape[0]
    for k, out in enumerate(outs):
        out[...] = o_ref[k * part : (k + 1) * part, :]


def attend(lists, counts, order, qm, qp, pieces):
    rows = qm.shape[0]
    part = jax.ShapeDtypeStruct((rows // CHUNKS, HD), jnp.bfloat16)
    return pl.pallas_call(
        attend_kernel,
        out_shape=[part] * (2 * CHUNKS),
        in_specs=[SM, SM, SM, VM, VM] + [ANY] * 16,
        out_specs=[VM] * (2 * CHUNKS),
        scratch_shapes=[
            pltpu.VMEM((16 * rows, 2 * HD), jnp.bfloat16),
            pltpu.VMEM((2 * rows, HD), jnp.bfloat16),
            pltpu.VMEM((2 * rows, HD), jnp.bfloat16),
            pltpu.SemaphoreType.DMA((16,)),
        ],
        compiler_params=pltpu.CompilerParams(vmem_limit_bytes=ATTEND_VMEM),
        cost_estimate=pl.CostEstimate(
            flops=4 * 2 * rows * SEL * TILE * HD, bytes_accessed=10 * 2**20,
            transcendentals=2 * rows * SEL * TILE,
        ),
        name="attend",
    )(lists, counts, order, qm, qp, *pieces)


def out_kernel(c0, c1, c2, c3, upper_ref, lower_ref, own_ref, *outs):
    context = jnp.concatenate([c0[...], c1[...], c2[...], c3[...]], axis=1)
    weight = jnp.concatenate([upper_ref[...], lower_ref[...]], axis=0)
    own_ref[...] = jnp.dot(context, weight[:, :256], preferred_element_type=jnp.float32)
    for k, out in enumerate(outs):
        part = weight[:, 256 * (k + 1) : 256 * (k + 2)]
        out[...] = jnp.dot(context, part, preferred_element_type=jnp.float32).astype(out.dtype)


def out_project(contexts, weights):
    rows = contexts[0].shape[0]
    return pl.pallas_call(
        out_kernel,
        in_specs=[VM] * 6,
        out_specs=[VM] * 4,
        out_shape=[jax.ShapeDtypeStruct((rows, 256), jnp.float32)]
        + [jax.ShapeDtypeStruct((rows, 256), jnp.bfloat16)] * 3,
        compiler_params=pltpu.CompilerParams(vmem_limit_bytes=OUT_VMEM),
        cost_estimate=pl.CostEstimate(
            flops=2 * rows * 512 * 1024, bytes_accessed=3 * 2**20, transcendentals=0
        ),
        name="out_project",
    )(*contexts, *weights)


def sum_kernel(*refs):
    own_ref, blocks, out_ref = refs[0], refs[1:4], refs[-1]
    total = own_ref[...]
    for block in blocks:
        total = total + block[...].astype(jnp.float32)
    out_ref[...] = total.astype(out_ref.dtype)


def sum_part(own, blocks, part, before):
    rows, columns = own.shape
    whole = pl.BlockSpec((rows, columns), lambda i: (0, 0))
    return pl.pallas_call(
        sum_kernel,
        grid=(1,),
        in_specs=[whole] * 4 + [ANY] * len(before),
        out_specs=pl.BlockSpec((rows, columns), lambda i: (part, 0)),
        out_shape=jax.ShapeDtypeStruct((rows * CHUNKS, columns), jnp.bfloat16),
        input_output_aliases={4: 0} if before else {},
        compiler_params=pltpu.CompilerParams(vmem_limit_bytes=OUT_VMEM),
        name="sum_part",
    )(own, *blocks, *before)


def per_device(hidden_states, norm_gain, qkv_weight, out_weight, selected_tiles, selected_count):
    seq = lax.axis_index("seq")
    head = lax.axis_index("head")
    yl, z, core = seq // 8, (seq % 8) // 2, seq % 2
    yh = head % 2

    x = head // 2

    def weight_rows(flip):
        columns = []
        for d in (0, 1, 3, 2):
            start = ((x + d) % 4 * 2 + (yh ^ flip)) * 256
            columns.append(lax.dynamic_slice(out_weight, (0, start), (256, 256)))
        both = jnp.concatenate(columns, axis=1)
        return jnp.where(yl == 0, both, jnp.roll(both, HD, axis=0))

    own_weight = weight_rows(0)
    sent_weight = weight_rows(1)

    rows_here = selected_tiles.shape[0]
    packed = jnp.concatenate(
        [selected_tiles, selected_count[:, None], jnp.zeros((rows_here, 95), jnp.int32)], axis=1
    )
    packed = jnp.concatenate([packed, move(packed, dyl=1)], axis=0)
    counts = packed[:, SEL]
    tile = packed[:, :SEL]
    slab = tile // rows_here
    place = (((slab % 8 // 2 - z) % 4) * 2 + ((slab // 8) ^ yl)) * 2 + ((slab % 2) ^ core)
    lists = place * rows_here + tile % rows_here
    n = counts.shape[0]
    ids = jnp.arange(n, dtype=jnp.int32)
    before = (counts[None, :] > counts[:, None]) | (
        (counts[None, :] == counts[:, None]) & (ids[None, :] < ids[:, None])
    )
    rank = jnp.sum(before.astype(jnp.int32), axis=1)
    order = jnp.sum(jnp.where(rank[None, :] == ids[:, None], ids[None, :], 0), axis=1)

    barrier = lax.optimization_barrier
    half = jnp.reshape(yl, (1,)).astype(jnp.int32)
    gain = norm_gain.reshape(1, -1)
    normed, kvo, kvm = project(
        first_kernel, (hidden_states, gain), qkv_weight, half,
        ((1, 1), (2, 1), (1, 0), (2, 0)), (D, 2 * HD, 2 * HD),
    )
    qm, qo = project(second_kernel, (normed,), qkv_weight, half, ((0, 0), (0, 1)), (HD, HD))

    kvp = move(kvo, dyl=1)
    up_m, down_m, core_m = move(kvm, dz=1), move(kvm, dz=-1), move(kvm, dc=1)
    kvp, sent_weight, lists, counts, order = barrier((kvp, sent_weight, lists, counts, order))
    up_p, down_p = move(kvp, dz=1), move(kvp, dz=-1)
    core_up_m, core_down_m = move(up_m, dc=1), move(down_m, dc=1)
    other_weight = move(sent_weight, dyh=1)
    up_m, down_m, up_p, down_p, kvp, qo, core_m, core_up_m, core_down_m, other_weight = barrier(
        (up_m, down_m, up_p, down_p, kvp, qo, core_m, core_up_m, core_down_m, other_weight)
    )
    far_m, far_p = move(up_m, dz=1), move(down_p, dz=-1)
    qp = move(qo, dyl=1)
    core_up_p, core_down_p, core_p = move(up_p, dc=1), move(down_p, dc=1), move(kvp, dc=1)
    far_m, far_p, qp, core_up_p, core_down_p, core_p = barrier(
        (far_m, far_p, qp, core_up_p, core_down_p, core_p)
    )
    core_far_m, core_far_p = move(far_m, dc=1), move(far_p, dc=1)
    parts = attend(
        lists, counts, order, qm, qp,
        (kvm, core_m, kvp, core_p, down_m, core_down_m, down_p, core_down_p,
         far_m, core_far_m, far_p, core_far_p, up_m, core_up_m, up_p, core_up_p),
    )

    weights = (own_weight, other_weight)
    before = ()
    for k, (mine, partner) in enumerate(zip(parts[:CHUNKS], parts[CHUNKS:])):
        contexts = (
            mine, move(partner, dyl=1), move(mine, dyh=1), move(partner, dyl=1, dyh=1)
        )
        own, *sent = out_project(contexts, weights)
        blocks = [move(block, dx=d) for d, block in zip((1, 3, 2), sent)]
        before = (sum_part(own, blocks, k, before),)
    return before[0]


def solution(mesh):
    return jax.shard_map(
        per_device,
        mesh=mesh,
        in_specs=(
            P("seq", None),
            P(),
            P(None, None, "head"),
            P("head", None),
            P("seq", None),
            P("seq"),
        ),
        out_specs=P("seq", "head"),
        check_vma=False,
    )
```

time: 154 us -> 118 us (0.77)
  the two profiles are of different devices: /device:TPU:6 before, /device:TPU:34 now
where the time goes in v2:
time: 118 us; the launch traced here: 119 us
  waiting for transfers between devices  55.7 us (47%)
  starting transfers between devices  31.1 us (26%)
  Pallas kernels  26.5 us (22%)
  local copies, waits for them, and re-layouts  2.67 us (2%)
  other arithmetic  2.51 us (2%)
    ppermute x30, waiting for transfers between devices, move(): return lax.ppermute(array, AXES, pairs)  55.7 us
    ppermute x30, starting transfers between devices, move(): return lax.ppermute(array, AXES, pairs)  31.1 us
    pallas_call x1, Pallas kernels, attend(): pl.pallas_call(attend_kernel, out_shape=[part] * (2 * CHUNKS), in_specs=[...  10.9 us
    pallas_call x2, Pallas kernels, project(): pl.pallas_call(kernel, grid_spec=pltpu.PrefetchScalarGridSpec(num_scalar_...  10.5 us
    pallas_call x2, Pallas kernels, out_project(): pl.pallas_call(out_kernel, in_specs=[VM] * 6, out_specs=[VM] * 4, out_sha...  3.5 us
  transfers between devices with their start and end apart: 30, of which 14 were waited for; matrix products, arithmetic and copies ran while one was open for 4% of the time, Pallas kernels for 6%

profile of v2, /device:TPU:34, one launch (start us, length us, event | category | flops | bytes accessed | tf_op | source)
XLA Modules:
  0.0 118.6 jit_solution(7156813203679370919)
XLA Ops:
  0.0 6.4 %project.2 = (bf16[1024,2048]{1,0:T(8,128)(2,1)}, bf16[1024,256]{1,0:T(8,128)(2,1)}, bf16[1024,256]{1,0:T(8,128)(2,1)}) custom-call(s32[1]{0:T(128)} %bitcast.half_ref, bf16[1024,2048]{1,0:T(8,128)(2,1)} %h_ref.1, f32[1,2048]{1,0:T(1,128)} %bitcast.3, bf16[3,2048,256]{2,1,0:T(8,128)(2,1)} %qo.1, bf16[3,2048,256]{2,1,0:T(8,128)(2,1)} %qo.1, ...), custom_call_target="tpu_custom_call" | custom-call | flops 2147483648 | bytes 9437184 | tf_op jit(solution)/shard_map/project/pallas_call | solution.py:78
  6.6 1.9 %collective-permute-start.2 = (bf16[1024,256]{1,0:T(8,128)(2,1)}, bf16[1024,256]{1,0:T(8,128)(2,1)S(1)}, u32[]{:S(2)}, u32[]{:S(2)}) collective-permute-start(bf16[1024,256]{1,0:T(8,128)(2,1)} %get-tuple-element.49.rest_0_), channel_id=1, source_target_pairs={{0,16},{1,17},{2,18},{3,19},{4,20},{5,21},{6,22},{7,23},{8,24},{9,... | collective-permute-start | bytes 1572872 | tf_op jit(solution)/shard_map/ppermute | solution.py:46
  8.7 1.6 %collective-permute-start.1 = (s32[16,128]{1,0:T(8,128)S(1)}, s32[16,128]{1,0:T(8,128)S(1)}, u32[]{:S(2)}, u32[]{:S(2)}) collective-permute-start(s32[16,128]{1,0:T(8,128)S(1)} %pad_add_fusion.1), channel_id=1, source_target_pairs={{0,64},{1,65},{2,66},{3,67},{4,68},{5,69},{6,70},{7,71},{8,72},{9,... | collective-permute-start | bytes 24584 | tf_op jit(solution)/shard_map/ppermute | solution.py:46
  10.7 1.4 %constant_dynamic-slice_fusion.3 = (bf16[256,256]{1,0:T(8,128)(2,1)S(1)}, bf16[256,256]{1,0:T(8,128)(2,1)S(1)}, bf16[256,256]{1,0:T(8,128)(2,1)S(1)}, bf16[256,2...) fusion(bf16[256,2048]{1,0:T(8,128)(2,1)} %param.9, ...), kind=kLoop, calls=%fused_computation.54 | loop fusion | bytes 2097184 | tf_op jit(solution)/shard_map/dynamic_slice | solution.py:260
  14.6 9.5 %collective-permute-done.rest_2_ = bf16[1024,256]{1,0:T(8,128)(2,1)S(1)} collective-permute-done((bf16[1024,256]{1,0:T(8,128)(2,1)}, bf16[1024,256]{1,0:T(8,128)(2,1)S(1)}, u32[]{:S(2)}, u32[]{:S(2)}) %collective-permute-start) | collective-permute-done | bytes 524320 | tf_op jit(solution)/shard_map/ppermute | solution.py:46
  24.1 2.2 %collective-permute-start.5 = (bf16[1024,256]{1,0:T(8,128)(2,1)S(1)}, bf16[1024,256]{1,0:T(8,128)(2,1)S(1)}, u32[]{:S(2)}, u32[]{:S(2)}) collective-permute-start(bf16[1024,256]{1,0:T(8,128)(2,1)S(1)} %collective-permute-done.rest_2_), channel_id=1, source_target_pairs={{0,48},{1,49},{2,50},{3,51},{4,52},{5,53},{6,54},{7,55},{8,56},{9,... | collective-permute-start | bytes 1572872 | tf_op jit(solution)/shard_map/ppermute | solution.py:46
  26.4 2.9 %collective-permute-start.9 = (bf16[256,1024]{1,0:T(8,128)(2,1)}, bf16[256,1024]{1,0:T(8,128)(2,1)}, u32[]{:S(2)}, u32[]{:S(2)}) collective-permute-start(bf16[256,1024]{1,0:T(8,128)(2,1)} %maximum_select_fusion), channel_id=1, source_target_pairs={{0,1},{1,0},{2,3},{3,2},{4,5},{5,4},{6,7},{7,6},{8,9},{9,8},{10,11... | collective-permute-start | bytes 1572872 | tf_op jit(solution)/shard_map/ppermute | solution.py:46
  29.8 4.0 %project.3 = (bf16[1024,128]{1,0:T(8,128)(2,1)}, bf16[1024,128]{1,0:T(8,128)(2,1)}) custom-call(s32[1]{0:T(128)} %bitcast.half_ref, bf16[1024,2048]{1,0:T(8,128)(2,1)} %get-tuple-element.47.normed_ref, bf16[3,2048,256]{2,1,0:T(8,128)(2,1)} %qo.1, bf16[3,2048,256]{2,1,0:T(8,128)(2,1)} %qo.1), custom_call_target="tpu_custom_call" | custom-call | flops 1073741824 | bytes 9437184 | tf_op jit(solution)/shard_map/project/pallas_call | solution.py:78
  33.8 7.0 %collective-permute-done.9.lower_ref = bf16[256,1024]{1,0:T(8,128)(2,1)} collective-permute-done((bf16[256,1024]{1,0:T(8,128)(2,1)}, bf16[256,1024]{1,0:T(8,128)(2,1)}, u32[]{:S(2)}, u32[]{:S(2)}) %collective-permute-start.9) | collective-permute-done | bytes 524320 | tf_op jit(solution)/shard_map/ppermute | solution.py:46
  41.5 2.0 %collective-permute-start.10 = (bf16[1024,256]{1,0:T(8,128)(2,1)S(1)}, bf16[1024,256]{1,0:T(8,128)(2,1)S(1)}, u32[]{:S(2)}, u32[]{:S(2)}) collective-permute-start(bf16[1024,256]{1,0:T(8,128)(2,1)S(1)} %collective-permute-done.2.rest_12_), channel_id=1, source_target_pairs={{0,16},{1,17},{2,18},{3,19},{4,20},{5,21},{6,22},{7,23},{8,24},{9,... | collective-permute-start | bytes 1572872 | tf_op jit(solution)/shard_map/ppermute | solution.py:46
  44.0 3.4 %collective-permute-done.12.qp_ref = bf16[1024,128]{1,0:T(8,128)(2,1)S(1)} collective-permute-done((bf16[1024,128]{1,0:T(8,128)(2,1)}, bf16[1024,128]{1,0:T(8,128)(2,1)S(1)}, u32[]{:S(2)}, u32[]{:S(2)}) %collective-permute-start.12) | collective-permute-done | bytes 262176 | tf_op jit(solution)/shard_map/ppermute | solution.py:46
  47.5 2.6 %collective-permute-start.11 = (bf16[1024,256]{1,0:T(8,128)(2,1)S(1)}, bf16[1024,256]{1,0:T(8,128)(2,1)S(1)}, u32[]{:S(2)}, u32[]{:S(2)}) collective-permute-start(bf16[1024,256]{1,0:T(8,128)(2,1)S(1)} %collective-permute-done.5.rest_6_), channel_id=1, source_target_pairs={{0,48},{1,49},{2,50},{3,51},{4,52},{5,53},{6,54},{7,55},{8,56},{9,... | collective-permute-start | bytes 1572872 | tf_op jit(solution)/shard_map/ppermute | solution.py:46
  50.1 3.5 %collective-permute-done.10.rest_8_ = bf16[1024,256]{1,0:T(8,128)(2,1)S(1)} collective-permute-done((bf16[1024,256]{1,0:T(8,128)(2,1)S(1)}, bf16[1024,256]{1,0:T(8,128)(2,1)S(1)}, u32[]{:S(2)}, u32[]{:S(2)}) %collective-permute-start.10) | collective-permute-done | bytes 524320 | tf_op jit(solution)/shard_map/ppermute | solution.py:46
  53.6 6.0 %collective-permute-done.11.rest_10_ = bf16[1024,256]{1,0:T(8,128)(2,1)S(1)} collective-permute-done((bf16[1024,256]{1,0:T(8,128)(2,1)S(1)}, bf16[1024,256]{1,0:T(8,128)(2,1)S(1)}, u32[]{:S(2)}, u32[]{:S(2)}) %collective-permute-start.11) | collective-permute-done | bytes 524320 | tf_op jit(solution)/shard_map/ppermute | solution.py:46
  60.1 1.4 %collective-permute-done.16.rest_9_ = bf16[1024,256]{1,0:T(8,128)(2,1)S(1)} collective-permute-done((bf16[1024,256]{1,0:T(8,128)(2,1)S(1)}, bf16[1024,256]{1,0:T(8,128)(2,1)S(1)}, u32[]{:S(2)}, u32[]{:S(2)}) %collective-permute-start.16) | collective-permute-done | bytes 524320 | tf_op jit(solution)/shard_map/ppermute | solution.py:46
  63.2 10.9 %attend.1 = (bf16[512,128]{1,0:T(8,128)(2,1)S(1)}, bf16[512,128]{1,0:T(8,128)(2,1)S(1)}, bf16[512,128]{1,0:T(8,128)(2,1)S(1)}, bf16[512,128]{1,0:T(8,128)(2,1)S(1)}) custom-call(s32[32,32]{1,0:T(8,128)S(1)} %get-tuple-element.44.list_ref, s32[32]{0:T(128)S(1)} %slice_reduce_fusion.count_ref, s32[32]{0:T(128)S(1)} %get-tuple-element.46.order_ref, ...), custom_call_target="tpu_custom_call" | custom-call | flops 2147483648 | bytes 10485760 | tf_op jit(solution)/shard_map/attend/pallas_call | solution.py:180
  74.1 3.2 %collective-permute-start.26 = (bf16[512,128]{1,0:T(8,128)(2,1)S(1)}, bf16[512,128]{1,0:T(8,128)(2,1)S(1)}, u32[]{:S(2)}, u32[]{:S(2)}) collective-permute-start(bf16[512,128]{1,0:T(8,128)(2,1)S(1)} %get-tuple-element.76), channel_id=1, source_target_pairs={{0,65},{1,64},{2,67},{3,66},{4,69},{5,68},{6,71},{7,70},{8,73},{9,... | collective-permute-start | bytes 393224 | tf_op jit(solution)/shard_map/ppermute | solution.py:46
  77.3 1.6 %collective-permute-start.25 = (bf16[512,128]{1,0:T(8,128)(2,1)S(1)}, bf16[512,128]{1,0:T(8,128)(2,1)S(1)}, u32[]{:S(2)}, u32[]{:S(2)}) collective-permute-start(bf16[512,128]{1,0:T(8,128)(2,1)S(1)} %get-tuple-element.75.c0), channel_id=1, source_target_pairs={{0,1},{1,0},{2,3},{3,2},{4,5},{5,4},{6,7},{7,6},{8,9},{9,8},{10,11... | collective-permute-start | bytes 393224 | tf_op jit(solution)/shard_map/ppermute | solution.py:46
  79.1 6.9 %collective-permute-done.25.c2 = bf16[512,128]{1,0:T(8,128)(2,1)S(1)} collective-permute-done((bf16[512,128]{1,0:T(8,128)(2,1)S(1)}, bf16[512,128]{1,0:T(8,128)(2,1)S(1)}, u32[]{:S(2)}, u32[]{:S(2)}) %collective-permute-start.25) | collective-permute-done | bytes 131104 | tf_op jit(solution)/shard_map/ppermute | solution.py:46
  86.1 1.8 %out_project.3 = (f32[512,256]{1,0:T(8,128)S(1)}, bf16[512,256]{1,0:T(8,128)(2,1)S(1)}, bf16[512,256]{1,0:T(8,128)(2,1)S(1)}, bf16[512,256]{1,0:T(8,128)(2,1)S(1)}) custom-call(bf16[512,128]{1,0:T(8,128)(2,1)S(1)} %get-tuple-element.75.c0, bf16[512,128]{1,0:T(8,128)(2,1)S(1)} %collective-permute-done.24.c1, bf16[512,128]{1,0:T(8,128)(2,1)S(1)} %collective-permute-done.25.c2, ...), custom_call_target="tpu_custom_call" | custom-call | flops 536870912 | bytes 3145728 | tf_op jit(solution)/shard_map/out_project/pallas_call | solution.py:211
  87.8 1.6 %collective-permute-start.27 = (bf16[512,256]{1,0:T(8,128)(2,1)S(1)}, bf16[512,256]{1,0:T(8,128)(2,1)S(1)}, u32[]{:S(2)}, u32[]{:S(2)}) collective-permute-start(bf16[512,256]{1,0:T(8,128)(2,1)S(1)} %get-tuple-element.78), channel_id=1, source_target_pairs={{0,2},{1,3},{2,4},{3,5},{4,6},{5,7},{6,0},{7,1},{8,10},{9,11},{10,... | collective-permute-start | bytes 786440 | tf_op jit(solution)/shard_map/ppermute | solution.py:46
  89.4 2.0 %collective-permute-start.19 = (bf16[512,128]{1,0:T(8,128)(2,1)S(1)}, bf16[512,128]{1,0:T(8,128)(2,1)S(1)}, u32[]{:S(2)}, u32[]{:S(2)}) collective-permute-start(bf16[512,128]{1,0:T(8,128)(2,1)S(1)} %get-tuple-element.68.c0), channel_id=1, source_target_pairs={{0,1},{1,0},{2,3},{3,2},{4,5},{5,4},{6,7},{7,6},{8,9},{9,8},{10,11... | collective-permute-start | bytes 393224 | tf_op jit(solution)/shard_map/ppermute | solution.py:46
  91.3 1.4 %collective-permute-start.20 = (bf16[512,128]{1,0:T(8,128)(2,1)S(1)}, bf16[512,128]{1,0:T(8,128)(2,1)S(1)}, u32[]{:S(2)}, u32[]{:S(2)}) collective-permute-start(bf16[512,128]{1,0:T(8,128)(2,1)S(1)} %get-tuple-element.69), channel_id=1, source_target_pairs={{0,65},{1,64},{2,67},{3,66},{4,69},{5,68},{6,71},{7,70},{8,73},{9,... | collective-permute-start | bytes 393224 | tf_op jit(solution)/shard_map/ppermute | solution.py:46
  93.6 2.6 %collective-permute-done.19.c2 = bf16[512,128]{1,0:T(8,128)(2,1)S(1)} collective-permute-done((bf16[512,128]{1,0:T(8,128)(2,1)S(1)}, bf16[512,128]{1,0:T(8,128)(2,1)S(1)}, u32[]{:S(2)}, u32[]{:S(2)}) %collective-permute-start.19) | collective-permute-done | bytes 131104 | tf_op jit(solution)/shard_map/ppermute | solution.py:46
  97.4 1.5 %collective-permute-done.20.c3 = bf16[512,128]{1,0:T(8,128)(2,1)S(1)} collective-permute-done((bf16[512,128]{1,0:T(8,128)(2,1)S(1)}, bf16[512,128]{1,0:T(8,128)(2,1)S(1)}, u32[]{:S(2)}, u32[]{:S(2)}) %collective-permute-start.20) | collective-permute-done | bytes 131104 | tf_op jit(solution)/shard_map/ppermute | solution.py:46
  98.9 1.7 %out_project.2 = (f32[512,256]{1,0:T(8,128)S(1)}, bf16[512,256]{1,0:T(8,128)(2,1)S(1)}, bf16[512,256]{1,0:T(8,128)(2,1)S(1)}, bf16[512,256]{1,0:T(8,128)(2,1)S(1)}) custom-call(bf16[512,128]{1,0:T(8,128)(2,1)S(1)} %get-tuple-element.68.c0, bf16[512,128]{1,0:T(8,128)(2,1)S(1)} %collective-permute-done.18.c1, bf16[512,128]{1,0:T(8,128)(2,1)S(1)} %collective-permute-done.19.c2, ...), custom_call_target="tpu_custom_call" | custom-call | flops 536870912 | bytes 3145728 | tf_op jit(solution)/shard_map/out_project/pallas_call | solution.py:211
  100.7 1.3 %collective-permute-start.21 = (bf16[512,256]{1,0:T(8,128)(2,1)S(1)}, bf16[512,256]{1,0:T(8,128)(2,1)S(1)}, u32[]{:S(2)}, u32[]{:S(2)}) collective-permute-start(bf16[512,256]{1,0:T(8,128)(2,1)S(1)} %get-tuple-element.72), channel_id=1, source_target_pairs={{0,2},{1,3},{2,4},{3,5},{4,6},{5,7},{6,0},{7,1},{8,10},{9,11},{10,... | collective-permute-start | bytes 786440 | tf_op jit(solution)/shard_map/ppermute | solution.py:46
  102.8 1.1 collective-permute-start.23
  103.9 4.4 %collective-permute-done.29.refs_3_ = bf16[512,256]{1,0:T(8,128)(2,1)S(1)} collective-permute-done((bf16[512,256]{1,0:T(8,128)(2,1)S(1)}, bf16[512,256]{1,0:T(8,128)(2,1)S(1)}, u32[]{:S(2)}, u32[]{:S(2)}) %collective-permute-start.29) | collective-permute-done | bytes 262176 | tf_op jit(solution)/shard_map/ppermute | solution.py:46
  109.1 2.2 %collective-permute-done.21.refs_1_ = bf16[512,256]{1,0:T(8,128)(2,1)S(1)} collective-permute-done((bf16[512,256]{1,0:T(8,128)(2,1)S(1)}, bf16[512,256]{1,0:T(8,128)(2,1)S(1)}, u32[]{:S(2)}, u32[]{:S(2)}) %collective-permute-start.21) | collective-permute-done | bytes 262176 | tf_op jit(solution)/shard_map/ppermute | solution.py:46
  111.3 2.6 %collective-permute-done.22.refs_2_ = bf16[512,256]{1,0:T(8,128)(2,1)S(1)} collective-permute-done((bf16[512,256]{1,0:T(8,128)(2,1)S(1)}, bf16[512,256]{1,0:T(8,128)(2,1)S(1)}, u32[]{:S(2)}, u32[]{:S(2)}) %collective-permute-start.22) | collective-permute-done | bytes 262176 | tf_op jit(solution)/shard_map/ppermute | solution.py:46
  113.9 3.9 %collective-permute-done.23.refs_3_ = bf16[512,256]{1,0:T(8,128)(2,1)S(1)} collective-permute-done((bf16[512,256]{1,0:T(8,128)(2,1)S(1)}, bf16[512,256]{1,0:T(8,128)(2,1)S(1)}, u32[]{:S(2)}, u32[]{:S(2)}) %collective-permute-start.23) | collective-permute-done | bytes 262176 | tf_op jit(solution)/shard_map/ppermute | solution.py:46
  (62 shorter events, 11.9 us)
Async XLA Ops:
  6.5 19.9 %collective-permute-start.6 = (bf16[1024,256]{1,0:T(8,128)(2,1)}, bf16[1024,256]{1,0:T(8,128)(2,1)S(1)}, u32[]{:S(2)}, u32[]{:S(2)}) collective-permute-start(bf16[1024,256]{1,0:T(8,128)(2,1)} %get-tuple-element.49.rest_0_), channel_id=1, source_target_pairs={{0,8},{1,9},{2,10},{3,11},{4,12},{5,13},{6,14},{7,15},{8,0},{9,1},... | collective-permute-start | bytes 1572872 | tf_op jit(solution)/shard_map/ppermute | solution.py:46
  6.5 22.8 %collective-permute-start.3 = (bf16[1024,256]{1,0:T(8,128)(2,1)}, bf16[1024,256]{1,0:T(8,128)(2,1)S(1)}, u32[]{:S(2)}, u32[]{:S(2)}) collective-permute-start(bf16[1024,256]{1,0:T(8,128)(2,1)} %get-tuple-element.49.rest_0_), channel_id=1, source_target_pairs={{0,48},{1,49},{2,50},{3,51},{4,52},{5,53},{6,54},{7,55},{8,56},{9,... | collective-permute-start | bytes 1572872 | tf_op jit(solution)/shard_map/ppermute | solution.py:46
  6.6 22.7 %collective-permute-start.2 = (bf16[1024,256]{1,0:T(8,128)(2,1)}, bf16[1024,256]{1,0:T(8,128)(2,1)S(1)}, u32[]{:S(2)}, u32[]{:S(2)}) collective-permute-start(bf16[1024,256]{1,0:T(8,128)(2,1)} %get-tuple-element.49.rest_0_), channel_id=1, source_target_pairs={{0,16},{1,17},{2,18},{3,19},{4,20},{5,21},{6,22},{7,23},{8,24},{9,... | collective-permute-start | bytes 1572872 | tf_op jit(solution)/shard_map/ppermute | solution.py:46
  8.7 5.3 %collective-permute-start.1 = (s32[16,128]{1,0:T(8,128)S(1)}, s32[16,128]{1,0:T(8,128)S(1)}, u32[]{:S(2)}, u32[]{:S(2)}) collective-permute-start(s32[16,128]{1,0:T(8,128)S(1)} %pad_add_fusion.1), channel_id=1, source_target_pairs={{0,64},{1,65},{2,66},{3,67},{4,68},{5,69},{6,70},{7,71},{8,72},{9,... | collective-permute-start | bytes 24584 | tf_op jit(solution)/shard_map/ppermute | solution.py:46
  10.3 13.8 %collective-permute-start = (bf16[1024,256]{1,0:T(8,128)(2,1)}, bf16[1024,256]{1,0:T(8,128)(2,1)S(1)}, u32[]{:S(2)}, u32[]{:S(2)}) collective-permute-start(bf16[1024,256]{1,0:T(8,128)(2,1)} %get-tuple-element.43), channel_id=1, source_target_pairs={{0,64},{1,65},{2,66},{3,67},{4,68},{5,69},{6,70},{7,71},{8,72},{9,... | collective-permute-start | bytes 1572872 | tf_op jit(solution)/shard_map/ppermute | solution.py:46
  24.1 16.6 %collective-permute-start.5 = (bf16[1024,256]{1,0:T(8,128)(2,1)S(1)}, bf16[1024,256]{1,0:T(8,128)(2,1)S(1)}, u32[]{:S(2)}, u32[]{:S(2)}) collective-permute-start(bf16[1024,256]{1,0:T(8,128)(2,1)S(1)} %collective-permute-done.rest_2_), channel_id=1, source_target_pairs={{0,48},{1,49},{2,50},{3,51},{4,52},{5,53},{6,54},{7,55},{8,56},{9,... | collective-permute-start | bytes 1572872 | tf_op jit(solution)/shard_map/ppermute | solution.py:46
  26.4 14.4 %collective-permute-start.4 = (bf16[1024,256]{1,0:T(8,128)(2,1)S(1)}, bf16[1024,256]{1,0:T(8,128)(2,1)S(1)}, u32[]{:S(2)}, u32[]{:S(2)}) collective-permute-start(bf16[1024,256]{1,0:T(8,128)(2,1)S(1)} %collective-permute-done.rest_2_), channel_id=1, source_target_pairs={{0,16},{1,17},{2,18},{3,19},{4,20},{5,21},{6,22},{7,23},{8,24},{9,... | collective-permute-start | bytes 1572872 | tf_op jit(solution)/shard_map/ppermute | solution.py:46
  26.4 14.4 %collective-permute-start.9 = (bf16[256,1024]{1,0:T(8,128)(2,1)}, bf16[256,1024]{1,0:T(8,128)(2,1)}, u32[]{:S(2)}, u32[]{:S(2)}) collective-permute-start(bf16[256,1024]{1,0:T(8,128)(2,1)} %maximum_select_fusion), channel_id=1, source_target_pairs={{0,1},{1,0},{2,3},{3,2},{4,5},{5,4},{6,7},{7,6},{8,9},{9,8},{10,11... | collective-permute-start | bytes 1572872 | tf_op jit(solution)/shard_map/ppermute | solution.py:46
  29.3 11.5 %collective-permute-start.8 = (bf16[1024,256]{1,0:T(8,128)(2,1)S(1)}, bf16[1024,256]{1,0:T(8,128)(2,1)}, u32[]{:S(2)}, u32[]{:S(2)}) collective-permute-start(bf16[1024,256]{1,0:T(8,128)(2,1)S(1)} %collective-permute-done.3.rest_4_), channel_id=1, source_target_pairs={{0,8},{1,9},{2,10},{3,11},{4,12},{5,13},{6,14},{7,15},{8,0},{9,1},... | collective-permute-start | bytes 1572872 | tf_op jit(solution)/shard_map/ppermute | solution.py:46
  29.3 11.5 %collective-permute-start.7 = (bf16[1024,256]{1,0:T(8,128)(2,1)S(1)}, bf16[1024,256]{1,0:T(8,128)(2,1)}, u32[]{:S(2)}, u32[]{:S(2)}) collective-permute-start(bf16[1024,256]{1,0:T(8,128)(2,1)S(1)} %collective-permute-done.2.rest_12_), channel_id=1, source_target_pairs={{0,8},{1,9},{2,10},{3,11},{4,12},{5,13},{6,14},{7,15},{8,0},{9,1},... | collective-permute-start | bytes 1572872 | tf_op jit(solution)/shard_map/ppermute | solution.py:46
  29.8 32.5 %copy-start = (bf16[1024,256]{1,0:T(8,128)(2,1)S(1)}, bf16[1024,256]{1,0:T(8,128)(2,1)}, u32[]{:S(2)}) copy-start(bf16[1024,256]{1,0:T(8,128)(2,1)} %get-tuple-element.49.rest_0_) | copy-start | bytes 1572868
  40.8 6.7 %collective-permute-start.12 = (bf16[1024,128]{1,0:T(8,128)(2,1)}, bf16[1024,128]{1,0:T(8,128)(2,1)S(1)}, u32[]{:S(2)}, u32[]{:S(2)}) collective-permute-start(bf16[1024,128]{1,0:T(8,128)(2,1)} %get-tuple-element.55), channel_id=1, source_target_pairs={{0,64},{1,65},{2,66},{3,67},{4,68},{5,69},{6,70},{7,71},{8,72},{9,... | collective-permute-start | bytes 786440 | tf_op jit(solution)/shard_map/ppermute | solution.py:46
  41.5 12.0 %collective-permute-start.10 = (bf16[1024,256]{1,0:T(8,128)(2,1)S(1)}, bf16[1024,256]{1,0:T(8,128)(2,1)S(1)}, u32[]{:S(2)}, u32[]{:S(2)}) collective-permute-start(bf16[1024,256]{1,0:T(8,128)(2,1)S(1)} %collective-permute-done.2.rest_12_), channel_id=1, source_target_pairs={{0,16},{1,17},{2,18},{3,19},{4,20},{5,21},{6,22},{7,23},{8,24},{9,... | collective-permute-start | bytes 1572872 | tf_op jit(solution)/shard_map/ppermute | solution.py:46
  43.5 10.0 %collective-permute-start.13 = (bf16[1024,256]{1,0:T(8,128)(2,1)S(1)}, bf16[1024,256]{1,0:T(8,128)(2,1)S(1)}, u32[]{:S(2)}, u32[]{:S(2)}) collective-permute-start(bf16[1024,256]{1,0:T(8,128)(2,1)S(1)} %collective-permute-done.4.rest_14_), channel_id=1, source_target_pairs={{0,8},{1,9},{2,10},{3,11},{4,12},{5,13},{6,14},{7,15},{8,0},{9,1},... | collective-permute-start | bytes 1572872 | tf_op jit(solution)/shard_map/ppermute | solution.py:46
  43.5 10.0 %collective-permute-start.15 = (bf16[1024,256]{1,0:T(8,128)(2,1)S(1)}, bf16[1024,256]{1,0:T(8,128)(2,1)S(1)}, u32[]{:S(2)}, u32[]{:S(2)}) collective-permute-start(bf16[1024,256]{1,0:T(8,128)(2,1)S(1)} %collective-permute-done.rest_2_), channel_id=1, source_target_pairs={{0,8},{1,9},{2,10},{3,11},{4,12},{5,13},{6,14},{7,15},{8,0},{9,1},... | collective-permute-start | bytes 1572872 | tf_op jit(solution)/shard_map/ppermute | solution.py:46
  44.0 9.5 %collective-permute-start.14 = (bf16[1024,256]{1,0:T(8,128)(2,1)S(1)}, bf16[1024,256]{1,0:T(8,128)(2,1)S(1)}, u32[]{:S(2)}, u32[]{:S(2)}) collective-permute-start(bf16[1024,256]{1,0:T(8,128)(2,1)S(1)} %collective-permute-done.5.rest_6_), channel_id=1, source_target_pairs={{0,8},{1,9},{2,10},{3,11},{4,12},{5,13},{6,14},{7,15},{8,0},{9,1},... | collective-permute-start | bytes 1572872 | tf_op jit(solution)/shard_map/ppermute | solution.py:46
  47.5 12.1 %collective-permute-start.11 = (bf16[1024,256]{1,0:T(8,128)(2,1)S(1)}, bf16[1024,256]{1,0:T(8,128)(2,1)S(1)}, u32[]{:S(2)}, u32[]{:S(2)}) collective-permute-start(bf16[1024,256]{1,0:T(8,128)(2,1)S(1)} %collective-permute-done.5.rest_6_), channel_id=1, source_target_pairs={{0,48},{1,49},{2,50},{3,51},{4,52},{5,53},{6,54},{7,55},{8,56},{9,... | collective-permute-start | bytes 1572872 | tf_op jit(solution)/shard_map/ppermute | solution.py:46
  59.6 1.9 %collective-permute-start.16 = (bf16[1024,256]{1,0:T(8,128)(2,1)S(1)}, bf16[1024,256]{1,0:T(8,128)(2,1)S(1)}, u32[]{:S(2)}, u32[]{:S(2)}) collective-permute-start(bf16[1024,256]{1,0:T(8,128)(2,1)S(1)} %collective-permute-done.10.rest_8_), channel_id=1, source_target_pairs={{0,8},{1,9},{2,10},{3,11},{4,12},{5,13},{6,14},{7,15},{8,0},{9,1},... | collective-permute-start | bytes 1572872 | tf_op jit(solution)/shard_map/ppermute | solution.py:46
  59.6 2.7 %collective-permute-start.17 = (bf16[1024,256]{1,0:T(8,128)(2,1)S(1)}, bf16[1024,256]{1,0:T(8,128)(2,1)S(1)}, u32[]{:S(2)}, u32[]{:S(2)}) collective-permute-start(bf16[1024,256]{1,0:T(8,128)(2,1)S(1)} %collective-permute-done.11.rest_10_), channel_id=1, source_target_pairs={{0,8},{1,9},{2,10},{3,11},{4,12},{5,13},{6,14},{7,15},{8,0},{9,1},... | collective-permute-start | bytes 1572872 | tf_op jit(solution)/shard_map/ppermute | solution.py:46
  63.2 15.7 %copy-start.4 = (bf16[256,256]{1,0:T(8,128)(2,1)S(1)}, bf16[256,256]{1,0:T(8,128)(2,1)}, u32[]{:S(2)}) copy-start(bf16[256,256]{1,0:T(8,128)(2,1)} %copy-done.3) | copy-start | bytes 393220
  74.1 11.9 %collective-permute-start.26 = (bf16[512,128]{1,0:T(8,128)(2,1)S(1)}, bf16[512,128]{1,0:T(8,128)(2,1)S(1)}, u32[]{:S(2)}, u32[]{:S(2)}) collective-permute-start(bf16[512,128]{1,0:T(8,128)(2,1)S(1)} %get-tuple-element.76), channel_id=1, source_target_pairs={{0,65},{1,64},{2,67},{3,66},{4,69},{5,68},{6,71},{7,70},{8,73},{9,... | collective-permute-start | bytes 393224 | tf_op jit(solution)/shard_map/ppermute | solution.py:46
  77.3 8.7 %collective-permute-start.24 = (bf16[512,128]{1,0:T(8,128)(2,1)S(1)}, bf16[512,128]{1,0:T(8,128)(2,1)S(1)}, u32[]{:S(2)}, u32[]{:S(2)}) collective-permute-start(bf16[512,128]{1,0:T(8,128)(2,1)S(1)} %get-tuple-element.76), channel_id=1, source_target_pairs={{0,64},{1,65},{2,66},{3,67},{4,68},{5,69},{6,70},{7,71},{8,72},{9,... | collective-permute-start | bytes 393224 | tf_op jit(solution)/shard_map/ppermute | solution.py:46
  77.3 8.7 %collective-permute-start.25 = (bf16[512,128]{1,0:T(8,128)(2,1)S(1)}, bf16[512,128]{1,0:T(8,128)(2,1)S(1)}, u32[]{:S(2)}, u32[]{:S(2)}) collective-permute-start(bf16[512,128]{1,0:T(8,128)(2,1)S(1)} %get-tuple-element.75.c0), channel_id=1, source_target_pairs={{0,1},{1,0},{2,3},{3,2},{4,5},{5,4},{6,7},{7,6},{8,9},{9,8},{10,11... | collective-permute-start | bytes 393224 | tf_op jit(solution)/shard_map/ppermute | solution.py:46
  87.8 15.0 %collective-permute-start.27 = (bf16[512,256]{1,0:T(8,128)(2,1)S(1)}, bf16[512,256]{1,0:T(8,128)(2,1)S(1)}, u32[]{:S(2)}, u32[]{:S(2)}) collective-permute-start(bf16[512,256]{1,0:T(8,128)(2,1)S(1)} %get-tuple-element.78), channel_id=1, source_target_pairs={{0,2},{1,3},{2,4},{3,5},{4,6},{5,7},{6,0},{7,1},{8,10},{9,11},{10,... | collective-permute-start | bytes 786440 | tf_op jit(solution)/shard_map/ppermute | solution.py:46
  89.4 6.9 %collective-permute-start.19 = (bf16[512,128]{1,0:T(8,128)(2,1)S(1)}, bf16[512,128]{1,0:T(8,128)(2,1)S(1)}, u32[]{:S(2)}, u32[]{:S(2)}) collective-permute-start(bf16[512,128]{1,0:T(8,128)(2,1)S(1)} %get-tuple-element.68.c0), channel_id=1, source_target_pairs={{0,1},{1,0},{2,3},{3,2},{4,5},{5,4},{6,7},{7,6},{8,9},{9,8},{10,11... | collective-permute-start | bytes 393224 | tf_op jit(solution)/shard_map/ppermute | solution.py:46
  91.3 7.6 %collective-permute-start.20 = (bf16[512,128]{1,0:T(8,128)(2,1)S(1)}, bf16[512,128]{1,0:T(8,128)(2,1)S(1)}, u32[]{:S(2)}, u32[]{:S(2)}) collective-permute-start(bf16[512,128]{1,0:T(8,128)(2,1)S(1)} %get-tuple-element.69), channel_id=1, source_target_pairs={{0,65},{1,64},{2,67},{3,66},{4,69},{5,68},{6,71},{7,70},{8,73},{9,... | collective-permute-start | bytes 393224 | tf_op jit(solution)/shard_map/ppermute | solution.py:46
  92.7 6.2 %collective-permute-start.18 = (bf16[512,128]{1,0:T(8,128)(2,1)S(1)}, bf16[512,128]{1,0:T(8,128)(2,1)S(1)}, u32[]{:S(2)}, u32[]{:S(2)}) collective-permute-start(bf16[512,128]{1,0:T(8,128)(2,1)S(1)} %get-tuple-element.69), channel_id=1, source_target_pairs={{0,64},{1,65},{2,66},{3,67},{4,68},{5,69},{6,70},{7,71},{8,72},{9,... | collective-permute-start | bytes 393224 | tf_op jit(solution)/shard_map/ppermute | solution.py:46
  93.1 10.8 %collective-permute-start.28 = (bf16[512,256]{1,0:T(8,128)(2,1)S(1)}, bf16[512,256]{1,0:T(8,128)(2,1)S(1)}, u32[]{:S(2)}, u32[]{:S(2)}) collective-permute-start(bf16[512,256]{1,0:T(8,128)(2,1)S(1)} %get-tuple-element.79), channel_id=1, source_target_pairs={{0,6},{1,7},{2,0},{3,1},{4,2},{5,3},{6,4},{7,5},{8,14},{9,15},{10,... | collective-permute-start | bytes 786440 | tf_op jit(solution)/shard_map/ppermute | solution.py:46
  96.3 12.0 %collective-permute-start.29 = (bf16[512,256]{1,0:T(8,128)(2,1)S(1)}, bf16[512,256]{1,0:T(8,128)(2,1)S(1)}, u32[]{:S(2)}, u32[]{:S(2)}) collective-permute-start(bf16[512,256]{1,0:T(8,128)(2,1)S(1)} %get-tuple-element.80), channel_id=1, source_target_pairs={{0,4},{1,5},{2,6},{3,7},{4,0},{5,1},{6,2},{7,3},{8,12},{9,13},{10,... | collective-permute-start | bytes 786440 | tf_op jit(solution)/shard_map/ppermute | solution.py:46
  100.7 10.6 %collective-permute-start.21 = (bf16[512,256]{1,0:T(8,128)(2,1)S(1)}, bf16[512,256]{1,0:T(8,128)(2,1)S(1)}, u32[]{:S(2)}, u32[]{:S(2)}) collective-permute-start(bf16[512,256]{1,0:T(8,128)(2,1)S(1)} %get-tuple-element.72), channel_id=1, source_target_pairs={{0,2},{1,3},{2,4},{3,5},{4,6},{5,7},{6,0},{7,1},{8,10},{9,11},{10,... | collective-permute-start | bytes 786440 | tf_op jit(solution)/shard_map/ppermute | solution.py:46
  102.0 12.0 %collective-permute-start.22 = (bf16[512,256]{1,0:T(8,128)(2,1)S(1)}, bf16[512,256]{1,0:T(8,128)(2,1)S(1)}, u32[]{:S(2)}, u32[]{:S(2)}) collective-permute-start(bf16[512,256]{1,0:T(8,128)(2,1)S(1)} %get-tuple-element.73), channel_id=1, source_target_pairs={{0,6},{1,7},{2,0},{3,1},{4,2},{5,3},{6,4},{7,5},{8,14},{9,15},{10,... | collective-permute-start | bytes 786440 | tf_op jit(solution)/shard_map/ppermute | solution.py:46
  102.8 15.0 %collective-permute-start.23 = (bf16[512,256]{1,0:T(8,128)(2,1)S(1)}, bf16[512,256]{1,0:T(8,128)(2,1)S(1)}, u32[]{:S(2)}, u32[]{:S(2)}) collective-permute-start(bf16[512,256]{1,0:T(8,128)(2,1)S(1)} %get-tuple-element.74), channel_id=1, source_target_pairs={{0,4},{1,5},{2,6},{3,7},{4,0},{5,1},{6,2},{7,3},{8,12},{9,13},{10,... | collective-permute-start | bytes 786440 | tf_op jit(solution)/shard_map/ppermute | solution.py:46
  (5 other events, 45.8 us)

commit v3 on v2

--- a/solution.py
+++ b/solution.py
@@ -20,7 +20,7 @@
 VM = pl.BlockSpec(memory_space=pltpu.VMEM)
 SM = pl.BlockSpec(memory_space=pltpu.SMEM)
 ANY = pl.BlockSpec(memory_space=pl.ANY)
-PROJECT_VMEM = 60 * 2**20
+HBM = pl.BlockSpec(memory_space=pltpu.HBM)
 ATTEND_VMEM = 24 * 2**20
 OUT_VMEM = 12 * 2**20
 CHUNKS = 2
@@ -46,26 +46,29 @@
     return lax.ppermute(array, AXES, pairs)
 
 
-def first_kernel(half_ref, h_ref, gain_ref, ko, vo, km, vm, normed_ref, kvo_ref, kvm_ref):
+def normalize(h_ref, gain_ref):
     values = h_ref[...].astype(jnp.float32)
     spread = jnp.mean(values * values, axis=-1, keepdims=True)
-    normed = (values * lax.rsqrt(spread + EPSILON) * gain_ref[...]).astype(jnp.bfloat16)
-    normed_ref[...] = normed
+    return (values * lax.rsqrt(spread + EPSILON) * gain_ref[...]).astype(jnp.bfloat16)
+
+
+def keys_kernel(half_ref, h_ref, gain_ref, ko, vo, km, vm, kvo_ref, kvm_ref):
+    normed = normalize(h_ref, gain_ref)
     for k_ref, v_ref, out_ref in ((ko, vo, kvo_ref), (km, vm, kvm_ref)):
         weight = jnp.concatenate([k_ref[0], v_ref[0]], axis=1)
         both = jnp.dot(normed, weight, preferred_element_type=jnp.float32)
         out_ref[...] = both.astype(jnp.bfloat16)
 
 
-def second_kernel(half_ref, normed_ref, qm, qo, qm_ref, qo_ref):
+def queries_kernel(half_ref, h_ref, gain_ref, qm, qo, qm_ref, qo_ref):
     weight = jnp.concatenate([qm[0], qo[0]], axis=1)
-    both = jnp.dot(normed_ref[...], weight, preferred_element_type=jnp.float32)
+    both = jnp.dot(normalize(h_ref, gain_ref), weight, preferred_element_type=jnp.float32)
     both = both.astype(jnp.bfloat16)
     qm_ref[...] = both[:, :HD]
     qo_ref[...] = both[:, HD:]
 
 
-def project(kernel, operands, weight, half, parts, outs):
+def project(kernel, operands, weight, half, parts, outs, vmem):
     rows, width = operands[0].shape
     block = 512
 
@@ -86,10 +89,8 @@
             out_specs=[rows_of(n) for n in outs],
         ),
         out_shape=[jax.ShapeDtypeStruct((rows, n), jnp.bfloat16) for n in outs],
-        compiler_params=pltpu.CompilerParams(vmem_limit_bytes=PROJECT_VMEM),
-        cost_estimate=pl.CostEstimate(
-            flops=2 * rows * width * HD * len(parts), bytes_accessed=9 * 2**20, transcendentals=0
-        ),
+        compiler_params=pltpu.CompilerParams(vmem_limit_bytes=vmem),
+        cost_estimate=pl.CostEstimate(flops=1024, bytes_accessed=1024, transcendentals=0),
         name="project",
     )(half, *operands, *[weight] * len(parts))
 
@@ -180,7 +181,7 @@
     return pl.pallas_call(
         attend_kernel,
         out_shape=[part] * (2 * CHUNKS),
-        in_specs=[SM, SM, SM, VM, VM] + [ANY] * 16,
+        in_specs=[SM, SM, SM, VM, VM, HBM] + [ANY] * 15,
         out_specs=[VM] * (2 * CHUNKS),
         scratch_shapes=[
             pltpu.VMEM((16 * rows, 2 * HD), jnp.bfloat16),
@@ -197,6 +198,37 @@
     )(lists, counts, order, qm, qp, *pieces)
 
 
+def pack_kernel(spot_ref, own_ref, other_ref, own_out, other_out):
+    own_out[...] = own_ref[...]
+    other_out[...] = other_ref[...]
+
+
+def pack_weight(spot, weight):
+    rows = weight.shape[0]
+
+    def part(flip):
+        def place(r, i, spot):
+            step = jnp.where(i == 2, 3, jnp.where(i == 3, 2, i))
+            return r ^ spot[2], (spot[0] + step) % 4 * 2 + (spot[1] ^ flip)
+
+        return pl.BlockSpec((HD, 256), place)
+
+    out = pl.BlockSpec((HD, 256), lambda r, i, spot: (r, i))
+    return pl.pallas_call(
+        pack_kernel,
+        grid_spec=pltpu.PrefetchScalarGridSpec(
+            num_scalar_prefetch=1,
+            grid=(rows // HD, 4),
+            in_specs=[part(0), part(1)],
+            out_specs=[out, out],
+        ),
+        out_shape=[jax.ShapeDtypeStruct((rows, 1024), weight.dtype)] * 2,
+        compiler_params=pltpu.CompilerParams(vmem_limit_bytes=OUT_VMEM),
+        cost_estimate=pl.CostEstimate(flops=1024, bytes_accessed=1024, transcendentals=0),
+        name="pack_weight",
+    )(spot, weight, weight)
+
+
 def out_kernel(c0, c1, c2, c3, upper_ref, lower_ref, own_ref, *outs):
     context = jnp.concatenate([c0[...], c1[...], c2[...], c3[...]], axis=1)
     weight = jnp.concatenate([upper_ref[...], lower_ref[...]], axis=0)
@@ -245,66 +277,67 @@
     )(own, *blocks, *before)
 
 
+def place_lists(tile, counts, yl, z, core):
+    per_slab = tile.shape[0] // 2
+    slab = tile // per_slab
+    place = (((slab % 8 // 2 - z) % 4) * 2 + ((slab // 8) ^ yl)) * 2 + ((slab % 2) ^ core)
+    lists = place * per_slab + tile % per_slab
+    ids = jnp.arange(counts.shape[0], dtype=jnp.int32)
+    before = (counts[None, :] > counts[:, None]) | (
+        (counts[None, :] == counts[:, None]) & (ids[None, :] < ids[:, None])
+    )
+    rank = jnp.sum(before.astype(jnp.int32), axis=1)
+    order = jnp.sum(jnp.where(rank[None, :] == ids[:, None], ids[None, :], 0), axis=1)
+    return lists, counts, order
+
+
 def per_device(hidden_states, norm_gain, qkv_weight, out_weight, selected_tiles, selected_count):
+    rows_here = selected_tiles.shape[0]
     seq = lax.axis_index("seq")
     head = lax.axis_index("head")
     yl, z, core = seq // 8, (seq % 8) // 2, seq % 2
     yh = head % 2
 
     x = head // 2
-
-    def weight_rows(flip):
-        columns = []
-        for d in (0, 1, 3, 2):
-            start = ((x + d) % 4 * 2 + (yh ^ flip)) * 256
-            columns.append(lax.dynamic_slice(out_weight, (0, start), (256, 256)))
-        both = jnp.concatenate(columns, axis=1)
-        return jnp.where(yl == 0, both, jnp.roll(both, HD, axis=0))
-
-    own_weight = weight_rows(0)
-    sent_weight = weight_rows(1)
-
-    rows_here = selected_tiles.shape[0]
-    packed = jnp.concatenate(
-        [selected_tiles, selected_count[:, None], jnp.zeros((rows_here, 95), jnp.int32)], axis=1
-    )
-    packed = jnp.concatenate([packed, move(packed, dyl=1)], axis=0)
-    counts = packed[:, SEL]
-    tile = packed[:, :SEL]
-    slab = tile // rows_here
-    place = (((slab % 8 // 2 - z) % 4) * 2 + ((slab // 8) ^ yl)) * 2 + ((slab % 2) ^ core)
-    lists = place * rows_here + tile % rows_here
-    n = counts.shape[0]
-    ids = jnp.arange(n, dtype=jnp.int32)
-    before = (counts[None, :] > counts[:, None]) | (
-        (counts[None, :] == counts[:, None]) & (ids[None, :] < ids[:, None])
-    )
-    rank = jnp.sum(before.astype(jnp.int32), axis=1)
-    order = jnp.sum(jnp.where(rank[None, :] == ids[:, None], ids[None, :], 0), axis=1)
+    spot = jnp.stack([x, yh, yl]).astype(jnp.int32)
+    own_weight, sent_weight = pack_weight(spot, out_weight)
 
     barrier = lax.optimization_barrier
     half = jnp.reshape(yl, (1,)).astype(jnp.int32)
     gain = norm_gain.reshape(1, -1)
-    normed, kvo, kvm = project(
-        first_kernel, (hidden_states, gain), qkv_weight, half,
-        ((1, 1), (2, 1), (1, 0), (2, 0)), (D, 2 * HD, 2 * HD),
-    )
-    qm, qo = project(second_kernel, (normed,), qkv_weight, half, ((0, 0), (0, 1)), (HD, HD))
+    kvo, kvm = project(
+        keys_kernel, (hidden_states, gain), qkv_weight, half,
+        ((1, 1), (2, 1), (1, 0), (2, 0)), (2 * HD, 2 * HD), 60 * 2**20,
+    )
+    qm, qo = project(
+        queries_kernel, (hidden_states, gain), qkv_weight, half,
+        ((0, 0), (0, 1)), (HD, HD), 24 * 2**20,
+    )
 
     kvp = move(kvo, dyl=1)
-    up_m, down_m, core_m = move(kvm, dz=1), move(kvm, dz=-1), move(kvm, dc=1)
-    kvp, sent_weight, lists, counts, order = barrier((kvp, sent_weight, lists, counts, order))
+    first, kvo = barrier((selected_count, kvo))
+    kvm, first = barrier((kvm, move(first, dc=1)))
+    up_m, down_m = move(kvm, dz=1), move(kvm, dz=-1)
+    kvp, sent_weight, first = barrier((kvp, sent_weight, first))
     up_p, down_p = move(kvp, dz=1), move(kvp, dz=-1)
+    other_weight = move(sent_weight, dyh=1)
     core_up_m, core_down_m = move(up_m, dc=1), move(down_m, dc=1)
-    other_weight = move(sent_weight, dyh=1)
-    up_m, down_m, up_p, down_p, kvp, qo, core_m, core_up_m, core_down_m, other_weight = barrier(
-        (up_m, down_m, up_p, down_p, kvp, qo, core_m, core_up_m, core_down_m, other_weight)
+    counts = jnp.maximum(selected_count, jnp.minimum(first, 1))
+    packed = jnp.concatenate(
+        [selected_tiles, counts[:, None], jnp.zeros((rows_here, 95), jnp.int32)], axis=1
+    )
+    up_m, down_m, up_p, down_p, qo, packed, core_up_m, core_down_m, other_weight = barrier(
+        (up_m, down_m, up_p, down_p, qo, packed, core_up_m, core_down_m, other_weight)
     )
     far_m, far_p = move(up_m, dz=1), move(down_p, dz=-1)
-    qp = move(qo, dyl=1)
-    core_up_p, core_down_p, core_p = move(up_p, dc=1), move(down_p, dc=1), move(kvp, dc=1)
-    far_m, far_p, qp, core_up_p, core_down_p, core_p = barrier(
-        (far_m, far_p, qp, core_up_p, core_down_p, core_p)
+    qp, packed_p = move(qo, dyl=1), move(packed, dyl=1)
+    qp, packed_p, up_p, down_p, own_m, own_p = barrier((qp, packed_p, up_p, down_p, kvm, kvp))
+    core_m, core_p = move(own_m, dc=1), move(own_p, dc=1)
+    core_up_p, core_down_p = move(up_p, dc=1), move(down_p, dc=1)
+    packed = jnp.concatenate([packed, packed_p], axis=0)
+    lists, counts, order = place_lists(packed[:, :SEL], packed[:, SEL], yl, z, core)
+    far_m, far_p, core_m, core_p, core_up_p, core_down_p, lists, counts, order = barrier(
+        (far_m, far_p, core_m, core_p, core_up_p, core_down_p, lists, counts, order)
     )
     core_far_m, core_far_p = move(far_m, dc=1), move(far_p, dc=1)
     parts = attend(

time: 118 us -> 113 us (0.958)
  the two profiles are of different devices: /device:TPU:34 before, /device:TPU:6 now
where the time goes in v3:
time: 113 us; the launch traced here: 110 us
  waiting for transfers between devices  42.2 us (37%)
  starting transfers between devices  34.7 us (31%)
  Pallas kernels  26.7 us (24%)
  local copies, waits for them, and re-layouts  6.32 us (6%)
    ppermute x31, waiting for transfers between devices, move(): return lax.ppermute(array, AXES, pairs)  42.2 us
    ppermute x31, starting transfers between devices, move(): return lax.ppermute(array, AXES, pairs)  34.7 us
    pallas_call x1, Pallas kernels, attend(): pl.pallas_call(attend_kernel, out_shape=[part] * (2 * CHUNKS), in_specs=[...  9.17 us
    pallas_call x2, Pallas kernels, project(): pl.pallas_call(kernel, grid_spec=pltpu.PrefetchScalarGridSpec(num_scalar_...  8.93 us
    unnamed x21, local copies, waits for them, and re-layouts  5.97 us
    pallas_call x2, Pallas kernels, out_project(): pl.pallas_call(out_kernel, in_specs=[VM] * 6, out_specs=[VM] * 4, out_sha...  3.5 us
    pallas_call x1, Pallas kernels, pack_weight(): pl.pallas_call(pack_kernel, grid_spec=pltpu.PrefetchScalarGridSpec(num_sc...  3.49 us
  transfers between devices with their start and end apart: 31, of which 18 were waited for; matrix products, arithmetic and copies ran while one was open for 1% of the time, Pallas kernels for 8%

profile of v3, /device:TPU:6, one launch (start us, length us, event | category | flops | bytes accessed | tf_op | source)
XLA Modules:
  0.0 110.5 jit_solution(15169335646962831005)
XLA Ops:
  0.0 6.5 %project.2 = (bf16[1024,256]{1,0:T(8,128)(2,1)}, bf16[1024,256]{1,0:T(8,128)(2,1)}) custom-call(s32[1]{0:T(128)} %bitcast.half_ref, bf16[1024,2048]{1,0:T(8,128)(2,1)} %h_ref.3, f32[1,2048]{1,0:T(1,128)} %bitcast.6, bf16[3,2048,256]{2,1,0:T(8,128)(2,1)} %qo.1, bf16[3,2048,256]{2,1,0:T(8,128)(2,1)} %qo.1, bf16[3,2048,256]{2,1,0:T(8,128)(2,1)} %qo.1, ...), custom_call_target="tpu_custom_call" | custom-call | flops 1024 | bytes 1024 | tf_op jit(solution)/shard_map/project/pallas_call | solution.py:81
  6.5 1.6 %collective-permute-start.3 = (bf16[1024,256]{1,0:T(8,128)(2,1)}, bf16[1024,256]{1,0:T(8,128)(2,1)}, u32[]{:S(2)}, u32[]{:S(2)}) collective-permute-start(bf16[1024,256]{1,0:T(8,128)(2,1)} %get-tuple-element.54), channel_id=1, source_target_pairs={{0,64},{1,65},{2,66},{3,67},{4,68},{5,69},{6,70},{7,71},{8,72},{9,... | collective-permute-start | bytes 1572872 | tf_op jit(solution)/shard_map/ppermute | solution.py:46
  9.2 4.0 %collective-permute-start.2 = (bf16[1024,256]{1,0:T(8,128)(2,1)}, bf16[1024,256]{1,0:T(8,128)(2,1)}, u32[]{:S(2)}, u32[]{:S(2)}) collective-permute-start(bf16[1024,256]{1,0:T(8,128)(2,1)} %get-tuple-element.68.rest_0_), channel_id=1, source_target_pairs={{0,48},{1,49},{2,50},{3,51},{4,52},{5,53},{6,54},{7,55},{8,56},{9,... | collective-permute-start | bytes 1572872 | tf_op jit(solution)/shard_map/ppermute | solution.py:46
  14.5 3.5 %pack_weight.1 = (bf16[256,1024]{1,0:T(8,128)(2,1)S(1)}, bf16[256,1024]{1,0:T(8,128)(2,1)}) custom-call(s32[3]{0:T(128)S(1)} %pad_add_fusion.spot_ref, bf16[256,2048]{1,0:T(8,128)(2,1)S(1)} %copy-done.2, bf16[256,2048]{1,0:T(8,128)(2,1)S(1)} %copy-done.2), custom_call_target="tpu_custom_call" | custom-call | flops 1024 | bytes 1024 | tf_op jit(solution)/shard_map/pack_weight/pallas_call | solution.py:217
  18.8 1.6 %collective-permute-done.3.rest_2_ = bf16[1024,256]{1,0:T(8,128)(2,1)} collective-permute-done((bf16[1024,256]{1,0:T(8,128)(2,1)}, bf16[1024,256]{1,0:T(8,128)(2,1)}, u32[]{:S(2)}, u32[]{:S(2)}) %collective-permute-start.3) | collective-permute-done | bytes 524320 | tf_op jit(solution)/shard_map/ppermute | solution.py:46
  20.5 4.0 %collective-permute-start.5 = (bf16[1024,256]{1,0:T(8,128)(2,1)}, bf16[1024,256]{1,0:T(8,128)(2,1)}, u32[]{:S(2)}, u32[]{:S(2)}) collective-permute-start(bf16[1024,256]{1,0:T(8,128)(2,1)} %collective-permute-done.3.rest_2_), channel_id=1, source_target_pairs={{0,48},{1,49},{2,50},{3,51},{4,52},{5,53},{6,54},{7,55},{8,56},{9,... | collective-permute-start | bytes 1572872 | tf_op jit(solution)/shard_map/ppermute | solution.py:46
  24.5 3.2 %collective-permute-start.8 = (bf16[256,1024]{1,0:T(8,128)(2,1)}, bf16[256,1024]{1,0:T(8,128)(2,1)}, u32[]{:S(2)}, u32[]{:S(2)}) collective-permute-start(bf16[256,1024]{1,0:T(8,128)(2,1)} %get-tuple-element.62), channel_id=1, source_target_pairs={{0,1},{1,0},{2,3},{3,2},{4,5},{5,4},{6,7},{7,6},{8,9},{9,8},{10,11... | collective-permute-start | bytes 1572872 | tf_op jit(solution)/shard_map/ppermute | solution.py:46
  27.7 1.8 %collective-permute-done.1.rest_12_ = bf16[1024,256]{1,0:T(8,128)(2,1)} collective-permute-done((bf16[1024,256]{1,0:T(8,128)(2,1)}, bf16[1024,256]{1,0:T(8,128)(2,1)}, u32[]{:S(2)}, u32[]{:S(2)}) %collective-permute-start.1) | collective-permute-done | bytes 524320 | tf_op jit(solution)/shard_map/ppermute | solution.py:46
  29.6 2.2 %copy-done.1 = bf16[1024,2048]{1,0:T(8,128)(2,1)S(1)} copy-done((bf16[1024,2048]{1,0:T(8,128)(2,1)S(1)}, bf16[1024,2048]{1,0:T(8,128)(2,1)}, u32[]{:S(2)}) %copy-start.1) | copy-done | bytes 4194328
  31.7 2.5 %project.3 = (bf16[1024,128]{1,0:T(8,128)(2,1)S(1)}, bf16[1024,128]{1,0:T(8,128)(2,1)S(1)}) custom-call(s32[1]{0:T(128)} %bitcast.half_ref, bf16[1024,2048]{1,0:T(8,128)(2,1)S(1)} %copy-done.1, f32[1,2048]{1,0:T(1,128)S(1)} %bitcast.7, bf16[3,2048,256]{2,1,0:T(8,128)(2,1)S(1)} %copy-done, bf16[3,2048,256]{2,1,0:T(8,128)(2,1)S(1)} %copy-done), custom_call_target="tpu_custom_call" | custom-call | flops 1024 | bytes 1024 | tf_op jit(solution)/shard_map/project/pallas_call | solution.py:81
  35.2 3.6 %collective-permute-done.8.lower_ref = bf16[256,1024]{1,0:T(8,128)(2,1)} collective-permute-done((bf16[256,1024]{1,0:T(8,128)(2,1)}, bf16[256,1024]{1,0:T(8,128)(2,1)}, u32[]{:S(2)}, u32[]{:S(2)}) %collective-permute-start.8) | collective-permute-done | bytes 524320 | tf_op jit(solution)/shard_map/ppermute | solution.py:46
  40.6 1.3 %collective-permute-start.12 = (s32[16,128]{1,0:T(8,128)S(1)}, s32[16,128]{1,0:T(8,128)S(1)}, u32[]{:S(2)}, u32[]{:S(2)}) collective-permute-start(s32[16,128]{1,0:T(8,128)S(1)} %add_add_fusion), channel_id=1, source_target_pairs={{0,64},{1,65},{2,66},{3,67},{4,68},{5,69},{6,70},{7,71},{8,72},{9,... | collective-permute-start | bytes 24584 | tf_op jit(solution)/shard_map/ppermute | solution.py:46
  41.9 3.2 %collective-permute-start.10 = (bf16[1024,256]{1,0:T(8,128)(2,1)}, bf16[1024,256]{1,0:T(8,128)(2,1)S(1)}, u32[]{:S(2)}, u32[]{:S(2)}) collective-permute-start(bf16[1024,256]{1,0:T(8,128)(2,1)} %collective-permute-done.5.rest_6_), channel_id=1, source_target_pairs={{0,48},{1,49},{2,50},{3,51},{4,52},{5,53},{6,54},{7,55},{8,56},{9,... | collective-permute-start | bytes 1572872 | tf_op jit(solution)/shard_map/ppermute | solution.py:46
  45.0 2.4 %collective-permute-done.12 = s32[16,128]{1,0:T(8,128)S(1)} collective-permute-done((s32[16,128]{1,0:T(8,128)S(1)}, s32[16,128]{1,0:T(8,128)S(1)}, u32[]{:S(2)}, u32[]{:S(2)}) %collective-permute-start.12) | collective-permute-done | bytes 8224 | tf_op jit(solution)/shard_map/ppermute | solution.py:46
  47.9 6.0 %collective-permute-done.9.rest_8_ = bf16[1024,256]{1,0:T(8,128)(2,1)S(1)} collective-permute-done((bf16[1024,256]{1,0:T(8,128)(2,1)}, bf16[1024,256]{1,0:T(8,128)(2,1)S(1)}, u32[]{:S(2)}, u32[]{:S(2)}) %collective-permute-start.9) | collective-permute-done | bytes 524320 | tf_op jit(solution)/shard_map/ppermute | solution.py:46
  56.6 1.4 %collective-permute-done.17.rest_9_ = bf16[1024,256]{1,0:T(8,128)(2,1)S(1)} collective-permute-done((bf16[1024,256]{1,0:T(8,128)(2,1)S(1)}, bf16[1024,256]{1,0:T(8,128)(2,1)S(1)}, u32[]{:S(2)}, u32[]{:S(2)}) %collective-permute-start.17) | collective-permute-done | bytes 524320 | tf_op jit(solution)/shard_map/ppermute | solution.py:46
  59.8 9.2 %attend.1 = (bf16[512,128]{1,0:T(8,128)(2,1)S(1)}, bf16[512,128]{1,0:T(8,128)(2,1)S(1)}, bf16[512,128]{1,0:T(8,128)(2,1)S(1)}, bf16[512,128]{1,0:T(8,128)(2,1)S(1)}) custom-call(s32[32,32]{1,0:T(8,128)S(1)} %get-tuple-element.73.list_ref, s32[32]{0:T(128)S(1)} %slice_reduce_fusion.count_ref, s32[32]{0:T(128)S(1)} %get-tuple-element.75.order_ref, ...), custom_call_target="tpu_custom_call" | custom-call | flops 2147483648 | bytes 10485760 | tf_op jit(solution)/shard_map/attend/pallas_call | solution.py:181
  69.0 2.7 %collective-permute-start.26 = (bf16[512,128]{1,0:T(8,128)(2,1)S(1)}, bf16[512,128]{1,0:T(8,128)(2,1)S(1)}, u32[]{:S(2)}, u32[]{:S(2)}) collective-permute-start(bf16[512,128]{1,0:T(8,128)(2,1)S(1)} %get-tuple-element.95.c0), channel_id=1, source_target_pairs={{0,1},{1,0},{2,3},{3,2},{4,5},{5,4},{6,7},{7,6},{8,9},{9,8},{10,11... | collective-permute-start | bytes 393224 | tf_op jit(solution)/shard_map/ppermute | solution.py:46
  72.5 3.6 %collective-permute-done.26.c2 = bf16[512,128]{1,0:T(8,128)(2,1)S(1)} collective-permute-done((bf16[512,128]{1,0:T(8,128)(2,1)S(1)}, bf16[512,128]{1,0:T(8,128)(2,1)S(1)}, u32[]{:S(2)}, u32[]{:S(2)}) %collective-permute-start.26) | collective-permute-done | bytes 131104 | tf_op jit(solution)/shard_map/ppermute | solution.py:46
  76.1 2.7 %collective-permute-done.27.c3 = bf16[512,128]{1,0:T(8,128)(2,1)S(1)} collective-permute-done((bf16[512,128]{1,0:T(8,128)(2,1)S(1)}, bf16[512,128]{1,0:T(8,128)(2,1)S(1)}, u32[]{:S(2)}, u32[]{:S(2)}) %collective-permute-start.27) | collective-permute-done | bytes 131104 | tf_op jit(solution)/shard_map/ppermute | solution.py:46
  78.9 1.8 %out_project.3 = (f32[512,256]{1,0:T(8,128)S(1)}, bf16[512,256]{1,0:T(8,128)(2,1)S(1)}, bf16[512,256]{1,0:T(8,128)(2,1)S(1)}, bf16[512,256]{1,0:T(8,128)(2,1)S(1)}) custom-call(bf16[512,128]{1,0:T(8,128)(2,1)S(1)} %get-tuple-element.95.c0, bf16[512,128]{1,0:T(8,128)(2,1)S(1)} %collective-permute-done.25.c1, bf16[512,128]{1,0:T(8,128)(2,1)S(1)} %collective-permute-done.26.c2, ...), custom_call_target="tpu_custom_call" | custom-call | flops 536870912 | bytes 3145728 | tf_op jit(solution)/shard_map/out_project/pallas_call | solution.py:243
  81.2 1.7 %collective-permute-start.20 = (bf16[512,128]{1,0:T(8,128)(2,1)S(1)}, bf16[512,128]{1,0:T(8,128)(2,1)S(1)}, u32[]{:S(2)}, u32[]{:S(2)}) collective-permute-start(bf16[512,128]{1,0:T(8,128)(2,1)S(1)} %get-tuple-element.87.c0), channel_id=1, source_target_pairs={{0,1},{1,0},{2,3},{3,2},{4,5},{5,4},{6,7},{7,6},{8,9},{9,8},{10,11... | collective-permute-start | bytes 393224 | tf_op jit(solution)/shard_map/ppermute | solution.py:46
  82.9 2.1 %collective-permute-start.21 = (bf16[512,128]{1,0:T(8,128)(2,1)S(1)}, bf16[512,128]{1,0:T(8,128)(2,1)S(1)}, u32[]{:S(2)}, u32[]{:S(2)}) collective-permute-start(bf16[512,128]{1,0:T(8,128)(2,1)S(1)} %get-tuple-element.88), channel_id=1, source_target_pairs={{0,65},{1,64},{2,67},{3,66},{4,69},{5,68},{6,71},{7,70},{8,73},{9,... | collective-permute-start | bytes 393224 | tf_op jit(solution)/shard_map/ppermute | solution.py:46
  85.0 1.5 %collective-permute-start.29 = (bf16[512,256]{1,0:T(8,128)(2,1)S(1)}, bf16[512,256]{1,0:T(8,128)(2,1)S(1)}, u32[]{:S(2)}, u32[]{:S(2)}) collective-permute-start(bf16[512,256]{1,0:T(8,128)(2,1)S(1)} %get-tuple-element.99), channel_id=1, source_target_pairs={{0,6},{1,7},{2,0},{3,1},{4,2},{5,3},{6,4},{7,5},{8,14},{9,15},{10,... | collective-permute-start | bytes 786440 | tf_op jit(solution)/shard_map/ppermute | solution.py:46
  86.5 2.3 %collective-permute-done.20.c2 = bf16[512,128]{1,0:T(8,128)(2,1)S(1)} collective-permute-done((bf16[512,128]{1,0:T(8,128)(2,1)S(1)}, bf16[512,128]{1,0:T(8,128)(2,1)S(1)}, u32[]{:S(2)}, u32[]{:S(2)}) %collective-permute-start.20) | collective-permute-done | bytes 131104 | tf_op jit(solution)/shard_map/ppermute | solution.py:46
  88.8 2.4 %collective-permute-start.30 = (bf16[512,256]{1,0:T(8,128)(2,1)S(1)}, bf16[512,256]{1,0:T(8,128)(2,1)S(1)}, u32[]{:S(2)}, u32[]{:S(2)}) collective-permute-start(bf16[512,256]{1,0:T(8,128)(2,1)S(1)} %get-tuple-element.100), channel_id=1, source_target_pairs={{0,4},{1,5},{2,6},{3,7},{4,0},{5,1},{6,2},{7,3},{8,12},{9,13},{10,... | collective-permute-start | bytes 786440 | tf_op jit(solution)/shard_map/ppermute | solution.py:46
  91.2 1.7 %out_project.2 = (f32[512,256]{1,0:T(8,128)S(1)}, bf16[512,256]{1,0:T(8,128)(2,1)S(1)}, bf16[512,256]{1,0:T(8,128)(2,1)S(1)}, bf16[512,256]{1,0:T(8,128)(2,1)S(1)}) custom-call(bf16[512,128]{1,0:T(8,128)(2,1)S(1)} %get-tuple-element.87.c0, bf16[512,128]{1,0:T(8,128)(2,1)S(1)} %collective-permute-done.19.c1, bf16[512,128]{1,0:T(8,128)(2,1)S(1)} %collective-permute-done.20.c2, ...), custom_call_target="tpu_custom_call" | custom-call | flops 536870912 | bytes 3145728 | tf_op jit(solution)/shard_map/out_project/pallas_call | solution.py:243
  93.0 1.9 %collective-permute-start.22 = (bf16[512,256]{1,0:T(8,128)(2,1)S(1)}, bf16[512,256]{1,0:T(8,128)(2,1)S(1)}, u32[]{:S(2)}, u32[]{:S(2)}) collective-permute-start(bf16[512,256]{1,0:T(8,128)(2,1)S(1)} %get-tuple-element.92), channel_id=1, source_target_pairs={{0,2},{1,3},{2,4},{3,5},{4,6},{5,7},{6,0},{7,1},{8,10},{9,11},{10,... | collective-permute-start | bytes 786440 | tf_op jit(solution)/shard_map/ppermute | solution.py:46
  95.1 1.6 %collective-permute-start.24 = (bf16[512,256]{1,0:T(8,128)(2,1)S(1)}, bf16[512,256]{1,0:T(8,128)(2,1)S(1)}, u32[]{:S(2)}, u32[]{:S(2)}) collective-permute-start(bf16[512,256]{1,0:T(8,128)(2,1)S(1)} %get-tuple-element.94), channel_id=1, source_target_pairs={{0,4},{1,5},{2,6},{3,7},{4,0},{5,1},{6,2},{7,3},{8,12},{9,13},{10,... | collective-permute-start | bytes 786440 | tf_op jit(solution)/shard_map/ppermute | solution.py:46
  97.0 3.0 %collective-permute-done.30.refs_3_ = bf16[512,256]{1,0:T(8,128)(2,1)S(1)} collective-permute-done((bf16[512,256]{1,0:T(8,128)(2,1)S(1)}, bf16[512,256]{1,0:T(8,128)(2,1)S(1)}, u32[]{:S(2)}, u32[]{:S(2)}) %collective-permute-start.30) | collective-permute-done | bytes 262176 | tf_op jit(solution)/shard_map/ppermute | solution.py:46
  100.8 1.6 %collective-permute-done.22.refs_1_ = bf16[512,256]{1,0:T(8,128)(2,1)S(1)} collective-permute-done((bf16[512,256]{1,0:T(8,128)(2,1)S(1)}, bf16[512,256]{1,0:T(8,128)(2,1)S(1)}, u32[]{:S(2)}, u32[]{:S(2)}) %collective-permute-start.22) | collective-permute-done | bytes 262176 | tf_op jit(solution)/shard_map/ppermute | solution.py:46
  102.5 7.2 %collective-permute-done.23.refs_2_ = bf16[512,256]{1,0:T(8,128)(2,1)S(1)} collective-permute-done((bf16[512,256]{1,0:T(8,128)(2,1)S(1)}, bf16[512,256]{1,0:T(8,128)(2,1)S(1)}, u32[]{:S(2)}, u32[]{:S(2)}) %collective-permute-start.23) | collective-permute-done | bytes 262176 | tf_op jit(solution)/shard_map/ppermute | solution.py:46
  (69 shorter events, 14.6 us)
Async XLA Ops:
  0.0 29.5 %copy-start.4 = (f32[2048]{0:T(1024)S(1)}, f32[2048]{0:T(1024)}, u32[]{:S(2)}) copy-start(f32[2048]{0:T(1024)} %param.7) | copy-start | bytes 24580
  6.5 14.0 %collective-permute-start.3 = (bf16[1024,256]{1,0:T(8,128)(2,1)}, bf16[1024,256]{1,0:T(8,128)(2,1)}, u32[]{:S(2)}, u32[]{:S(2)}) collective-permute-start(bf16[1024,256]{1,0:T(8,128)(2,1)} %get-tuple-element.54), channel_id=1, source_target_pairs={{0,64},{1,65},{2,66},{3,67},{4,68},{5,69},{6,70},{7,71},{8,72},{9,... | collective-permute-start | bytes 1572872 | tf_op jit(solution)/shard_map/ppermute | solution.py:46
  8.0 1.1 %collective-permute-start = (s32[16]{0:T(128)S(1)}, s32[16]{0:T(128)S(1)}, u32[]{:S(2)}, u32[]{:S(2)}) collective-permute-start(s32[16]{0:T(128)S(1)} %copy-done.9), channel_id=1, source_target_pairs={{0,8},{1,9},{2,10},{3,11},{4,12},{5,13},{6,14},{7,15},{8,0},{9,1},... | collective-permute-start | bytes 200 | tf_op jit(solution)/shard_map/ppermute | solution.py:46
  9.2 18.5 %collective-permute-start.2 = (bf16[1024,256]{1,0:T(8,128)(2,1)}, bf16[1024,256]{1,0:T(8,128)(2,1)}, u32[]{:S(2)}, u32[]{:S(2)}) collective-permute-start(bf16[1024,256]{1,0:T(8,128)(2,1)} %get-tuple-element.68.rest_0_), channel_id=1, source_target_pairs={{0,48},{1,49},{2,50},{3,51},{4,52},{5,53},{6,54},{7,55},{8,56},{9,... | collective-permute-start | bytes 1572872 | tf_op jit(solution)/shard_map/ppermute | solution.py:46
  13.2 16.3 %collective-permute-start.1 = (bf16[1024,256]{1,0:T(8,128)(2,1)}, bf16[1024,256]{1,0:T(8,128)(2,1)}, u32[]{:S(2)}, u32[]{:S(2)}) collective-permute-start(bf16[1024,256]{1,0:T(8,128)(2,1)} %get-tuple-element.68.rest_0_), channel_id=1, source_target_pairs={{0,16},{1,17},{2,18},{3,19},{4,20},{5,21},{6,22},{7,23},{8,24},{9,... | collective-permute-start | bytes 1572872 | tf_op jit(solution)/shard_map/ppermute | solution.py:46
  20.5 18.4 %collective-permute-start.5 = (bf16[1024,256]{1,0:T(8,128)(2,1)}, bf16[1024,256]{1,0:T(8,128)(2,1)}, u32[]{:S(2)}, u32[]{:S(2)}) collective-permute-start(bf16[1024,256]{1,0:T(8,128)(2,1)} %collective-permute-done.3.rest_2_), channel_id=1, source_target_pairs={{0,48},{1,49},{2,50},{3,51},{4,52},{5,53},{6,54},{7,55},{8,56},{9,... | collective-permute-start | bytes 1572872 | tf_op jit(solution)/shard_map/ppermute | solution.py:46
  24.5 15.2 %collective-permute-start.4 = (bf16[1024,256]{1,0:T(8,128)(2,1)}, bf16[1024,256]{1,0:T(8,128)(2,1)}, u32[]{:S(2)}, u32[]{:S(2)}) collective-permute-start(bf16[1024,256]{1,0:T(8,128)(2,1)} %collective-permute-done.3.rest_2_), channel_id=1, source_target_pairs={{0,16},{1,17},{2,18},{3,19},{4,20},{5,21},{6,22},{7,23},{8,24},{9,... | collective-permute-start | bytes 1572872 | tf_op jit(solution)/shard_map/ppermute | solution.py:46
  24.5 14.3 %collective-permute-start.8 = (bf16[256,1024]{1,0:T(8,128)(2,1)}, bf16[256,1024]{1,0:T(8,128)(2,1)}, u32[]{:S(2)}, u32[]{:S(2)}) collective-permute-start(bf16[256,1024]{1,0:T(8,128)(2,1)} %get-tuple-element.62), channel_id=1, source_target_pairs={{0,1},{1,0},{2,3},{3,2},{4,5},{5,4},{6,7},{7,6},{8,9},{9,8},{10,11... | collective-permute-start | bytes 1572872 | tf_op jit(solution)/shard_map/ppermute | solution.py:46
  27.7 12.0 %collective-permute-start.7 = (bf16[1024,256]{1,0:T(8,128)(2,1)}, bf16[1024,256]{1,0:T(8,128)(2,1)}, u32[]{:S(2)}, u32[]{:S(2)}) collective-permute-start(bf16[1024,256]{1,0:T(8,128)(2,1)} %collective-permute-done.2.rest_4_), channel_id=1, source_target_pairs={{0,8},{1,9},{2,10},{3,11},{4,12},{5,13},{6,14},{7,15},{8,0},{9,1},... | collective-permute-start | bytes 1572872 | tf_op jit(solution)/shard_map/ppermute | solution.py:46
  29.5 10.2 %collective-permute-start.6 = (bf16[1024,256]{1,0:T(8,128)(2,1)}, bf16[1024,256]{1,0:T(8,128)(2,1)}, u32[]{:S(2)}, u32[]{:S(2)}) collective-permute-start(bf16[1024,256]{1,0:T(8,128)(2,1)} %collective-permute-done.1.rest_12_), channel_id=1, source_target_pairs={{0,8},{1,9},{2,10},{3,11},{4,12},{5,13},{6,14},{7,15},{8,0},{9,1},... | collective-permute-start | bytes 1572872 | tf_op jit(solution)/shard_map/ppermute | solution.py:46
  39.7 14.2 %collective-permute-start.9 = (bf16[1024,256]{1,0:T(8,128)(2,1)}, bf16[1024,256]{1,0:T(8,128)(2,1)S(1)}, u32[]{:S(2)}, u32[]{:S(2)}) collective-permute-start(bf16[1024,256]{1,0:T(8,128)(2,1)} %collective-permute-done.1.rest_12_), channel_id=1, source_target_pairs={{0,16},{1,17},{2,18},{3,19},{4,20},{5,21},{6,22},{7,23},{8,24},{9,... | collective-permute-start | bytes 1572872 | tf_op jit(solution)/shard_map/ppermute | solution.py:46
  39.7 7.6 %collective-permute-start.11 = (bf16[1024,128]{1,0:T(8,128)(2,1)}, bf16[1024,128]{1,0:T(8,128)(2,1)S(1)}, u32[]{:S(2)}, u32[]{:S(2)}) collective-permute-start(bf16[1024,128]{1,0:T(8,128)(2,1)} %copy-done.7), channel_id=1, source_target_pairs={{0,64},{1,65},{2,66},{3,67},{4,68},{5,69},{6,70},{7,71},{8,72},{9,... | collective-permute-start | bytes 786440 | tf_op jit(solution)/shard_map/ppermute | solution.py:46
  40.6 6.8 %collective-permute-start.12 = (s32[16,128]{1,0:T(8,128)S(1)}, s32[16,128]{1,0:T(8,128)S(1)}, u32[]{:S(2)}, u32[]{:S(2)}) collective-permute-start(s32[16,128]{1,0:T(8,128)S(1)} %add_add_fusion), channel_id=1, source_target_pairs={{0,64},{1,65},{2,66},{3,67},{4,68},{5,69},{6,70},{7,71},{8,72},{9,... | collective-permute-start | bytes 24584 | tf_op jit(solution)/shard_map/ppermute | solution.py:46
  41.9 12.9 %collective-permute-start.10 = (bf16[1024,256]{1,0:T(8,128)(2,1)}, bf16[1024,256]{1,0:T(8,128)(2,1)S(1)}, u32[]{:S(2)}, u32[]{:S(2)}) collective-permute-start(bf16[1024,256]{1,0:T(8,128)(2,1)} %collective-permute-done.5.rest_6_), channel_id=1, source_target_pairs={{0,48},{1,49},{2,50},{3,51},{4,52},{5,53},{6,54},{7,55},{8,56},{9,... | collective-permute-start | bytes 1572872 | tf_op jit(solution)/shard_map/ppermute | solution.py:46
  47.4 7.4 %collective-permute-start.13 = (bf16[1024,256]{1,0:T(8,128)(2,1)}, bf16[1024,256]{1,0:T(8,128)(2,1)S(1)}, u32[]{:S(2)}, u32[]{:S(2)}) collective-permute-start(bf16[1024,256]{1,0:T(8,128)(2,1)} %get-tuple-element.68.rest_0_), channel_id=1, source_target_pairs={{0,8},{1,9},{2,10},{3,11},{4,12},{5,13},{6,14},{7,15},{8,0},{9,1},... | collective-permute-start | bytes 1572872 | tf_op jit(solution)/shard_map/ppermute | solution.py:46
  47.4 7.4 %collective-permute-start.14 = (bf16[1024,256]{1,0:T(8,128)(2,1)}, bf16[1024,256]{1,0:T(8,128)(2,1)S(1)}, u32[]{:S(2)}, u32[]{:S(2)}) collective-permute-start(bf16[1024,256]{1,0:T(8,128)(2,1)} %collective-permute-done.3.rest_2_), channel_id=1, source_target_pairs={{0,8},{1,9},{2,10},{3,11},{4,12},{5,13},{6,14},{7,15},{8,0},{9,1},... | collective-permute-start | bytes 1572872 | tf_op jit(solution)/shard_map/ppermute | solution.py:46
  47.9 6.9 %collective-permute-start.15 = (bf16[1024,256]{1,0:T(8,128)(2,1)}, bf16[1024,256]{1,0:T(8,128)(2,1)S(1)}, u32[]{:S(2)}, u32[]{:S(2)}) collective-permute-start(bf16[1024,256]{1,0:T(8,128)(2,1)} %collective-permute-done.4.rest_14_), channel_id=1, source_target_pairs={{0,8},{1,9},{2,10},{3,11},{4,12},{5,13},{6,14},{7,15},{8,0},{9,1},... | collective-permute-start | bytes 1572872 | tf_op jit(solution)/shard_map/ppermute | solution.py:46
  54.0 2.1 %collective-permute-start.16 = (bf16[1024,256]{1,0:T(8,128)(2,1)}, bf16[1024,256]{1,0:T(8,128)(2,1)S(1)}, u32[]{:S(2)}, u32[]{:S(2)}) collective-permute-start(bf16[1024,256]{1,0:T(8,128)(2,1)} %collective-permute-done.5.rest_6_), channel_id=1, source_target_pairs={{0,8},{1,9},{2,10},{3,11},{4,12},{5,13},{6,14},{7,15},{8,0},{9,1},... | collective-permute-start | bytes 1572872 | tf_op jit(solution)/shard_map/ppermute | solution.py:46
  56.1 1.9 %collective-permute-start.17 = (bf16[1024,256]{1,0:T(8,128)(2,1)S(1)}, bf16[1024,256]{1,0:T(8,128)(2,1)S(1)}, u32[]{:S(2)}, u32[]{:S(2)}) collective-permute-start(bf16[1024,256]{1,0:T(8,128)(2,1)S(1)} %collective-permute-done.9.rest_8_), channel_id=1, source_target_pairs={{0,8},{1,9},{2,10},{3,11},{4,12},{5,13},{6,14},{7,15},{8,0},{9,1},... | collective-permute-start | bytes 1572872 | tf_op jit(solution)/shard_map/ppermute | solution.py:46
  56.2 2.5 %collective-permute-start.18 = (bf16[1024,256]{1,0:T(8,128)(2,1)S(1)}, bf16[1024,256]{1,0:T(8,128)(2,1)S(1)}, u32[]{:S(2)}, u32[]{:S(2)}) collective-permute-start(bf16[1024,256]{1,0:T(8,128)(2,1)S(1)} %collective-permute-done.10.rest_10_), channel_id=1, source_target_pairs={{0,8},{1,9},{2,10},{3,11},{4,12},{5,13},{6,14},{7,15},{8,0},{9,1},... | collective-permute-start | bytes 1572872 | tf_op jit(solution)/shard_map/ppermute | solution.py:46
  69.0 7.2 %collective-permute-start.26 = (bf16[512,128]{1,0:T(8,128)(2,1)S(1)}, bf16[512,128]{1,0:T(8,128)(2,1)S(1)}, u32[]{:S(2)}, u32[]{:S(2)}) collective-permute-start(bf16[512,128]{1,0:T(8,128)(2,1)S(1)} %get-tuple-element.95.c0), channel_id=1, source_target_pairs={{0,1},{1,0},{2,3},{3,2},{4,5},{5,4},{6,7},{7,6},{8,9},{9,8},{10,11... | collective-permute-start | bytes 393224 | tf_op jit(solution)/shard_map/ppermute | solution.py:46
  71.6 7.2 %collective-permute-start.27 = (bf16[512,128]{1,0:T(8,128)(2,1)S(1)}, bf16[512,128]{1,0:T(8,128)(2,1)S(1)}, u32[]{:S(2)}, u32[]{:S(2)}) collective-permute-start(bf16[512,128]{1,0:T(8,128)(2,1)S(1)} %get-tuple-element.96), channel_id=1, source_target_pairs={{0,65},{1,64},{2,67},{3,66},{4,69},{5,68},{6,71},{7,70},{8,73},{9,... | collective-permute-start | bytes 393224 | tf_op jit(solution)/shard_map/ppermute | solution.py:46
  71.6 7.2 %collective-permute-start.25 = (bf16[512,128]{1,0:T(8,128)(2,1)S(1)}, bf16[512,128]{1,0:T(8,128)(2,1)S(1)}, u32[]{:S(2)}, u32[]{:S(2)}) collective-permute-start(bf16[512,128]{1,0:T(8,128)(2,1)S(1)} %get-tuple-element.96), channel_id=1, source_target_pairs={{0,64},{1,65},{2,66},{3,67},{4,68},{5,69},{6,70},{7,71},{8,72},{9,... | collective-permute-start | bytes 393224 | tf_op jit(solution)/shard_map/ppermute | solution.py:46
  80.6 14.5 %collective-permute-start.28 = (bf16[512,256]{1,0:T(8,128)(2,1)S(1)}, bf16[512,256]{1,0:T(8,128)(2,1)S(1)}, u32[]{:S(2)}, u32[]{:S(2)}) collective-permute-start(bf16[512,256]{1,0:T(8,128)(2,1)S(1)} %get-tuple-element.98), channel_id=1, source_target_pairs={{0,2},{1,3},{2,4},{3,5},{4,6},{5,7},{6,0},{7,1},{8,10},{9,11},{10,... | collective-permute-start | bytes 786440 | tf_op jit(solution)/shard_map/ppermute | solution.py:46
  81.2 7.6 %collective-permute-start.20 = (bf16[512,128]{1,0:T(8,128)(2,1)S(1)}, bf16[512,128]{1,0:T(8,128)(2,1)S(1)}, u32[]{:S(2)}, u32[]{:S(2)}) collective-permute-start(bf16[512,128]{1,0:T(8,128)(2,1)S(1)} %get-tuple-element.87.c0), channel_id=1, source_target_pairs={{0,1},{1,0},{2,3},{3,2},{4,5},{5,4},{6,7},{7,6},{8,9},{9,8},{10,11... | collective-permute-start | bytes 393224 | tf_op jit(solution)/shard_map/ppermute | solution.py:46
  82.9 8.3 %collective-permute-start.21 = (bf16[512,128]{1,0:T(8,128)(2,1)S(1)}, bf16[512,128]{1,0:T(8,128)(2,1)S(1)}, u32[]{:S(2)}, u32[]{:S(2)}) collective-permute-start(bf16[512,128]{1,0:T(8,128)(2,1)S(1)} %get-tuple-element.88), channel_id=1, source_target_pairs={{0,65},{1,64},{2,67},{3,66},{4,69},{5,68},{6,71},{7,70},{8,73},{9,... | collective-permute-start | bytes 393224 | tf_op jit(solution)/shard_map/ppermute | solution.py:46
  85.0 6.2 %collective-permute-start.19 = (bf16[512,128]{1,0:T(8,128)(2,1)S(1)}, bf16[512,128]{1,0:T(8,128)(2,1)S(1)}, u32[]{:S(2)}, u32[]{:S(2)}) collective-permute-start(bf16[512,128]{1,0:T(8,128)(2,1)S(1)} %get-tuple-element.88), channel_id=1, source_target_pairs={{0,64},{1,65},{2,66},{3,67},{4,68},{5,69},{6,70},{7,71},{8,72},{9,... | collective-permute-start | bytes 393224 | tf_op jit(solution)/shard_map/ppermute | solution.py:46
  85.0 12.1 %collective-permute-start.29 = (bf16[512,256]{1,0:T(8,128)(2,1)S(1)}, bf16[512,256]{1,0:T(8,128)(2,1)S(1)}, u32[]{:S(2)}, u32[]{:S(2)}) collective-permute-start(bf16[512,256]{1,0:T(8,128)(2,1)S(1)} %get-tuple-element.99), channel_id=1, source_target_pairs={{0,6},{1,7},{2,0},{3,1},{4,2},{5,3},{6,4},{7,5},{8,14},{9,15},{10,... | collective-permute-start | bytes 786440 | tf_op jit(solution)/shard_map/ppermute | solution.py:46
  88.8 11.2 %collective-permute-start.30 = (bf16[512,256]{1,0:T(8,128)(2,1)S(1)}, bf16[512,256]{1,0:T(8,128)(2,1)S(1)}, u32[]{:S(2)}, u32[]{:S(2)}) collective-permute-start(bf16[512,256]{1,0:T(8,128)(2,1)S(1)} %get-tuple-element.100), channel_id=1, source_target_pairs={{0,4},{1,5},{2,6},{3,7},{4,0},{5,1},{6,2},{7,3},{8,12},{9,13},{10,... | collective-permute-start | bytes 786440 | tf_op jit(solution)/shard_map/ppermute | solution.py:46
  93.0 9.5 %collective-permute-start.22 = (bf16[512,256]{1,0:T(8,128)(2,1)S(1)}, bf16[512,256]{1,0:T(8,128)(2,1)S(1)}, u32[]{:S(2)}, u32[]{:S(2)}) collective-permute-start(bf16[512,256]{1,0:T(8,128)(2,1)S(1)} %get-tuple-element.92), channel_id=1, source_target_pairs={{0,2},{1,3},{2,4},{3,5},{4,6},{5,7},{6,0},{7,1},{8,10},{9,11},{10,... | collective-permute-start | bytes 786440 | tf_op jit(solution)/shard_map/ppermute | solution.py:46
  94.8 14.8 %collective-permute-start.23 = (bf16[512,256]{1,0:T(8,128)(2,1)S(1)}, bf16[512,256]{1,0:T(8,128)(2,1)S(1)}, u32[]{:S(2)}, u32[]{:S(2)}) collective-permute-start(bf16[512,256]{1,0:T(8,128)(2,1)S(1)} %get-tuple-element.93), channel_id=1, source_target_pairs={{0,6},{1,7},{2,0},{3,1},{4,2},{5,3},{6,4},{7,5},{8,14},{9,15},{10,... | collective-permute-start | bytes 786440 | tf_op jit(solution)/shard_map/ppermute | solution.py:46
  95.1 14.6 %collective-permute-start.24 = (bf16[512,256]{1,0:T(8,128)(2,1)S(1)}, bf16[512,256]{1,0:T(8,128)(2,1)S(1)}, u32[]{:S(2)}, u32[]{:S(2)}) collective-permute-start(bf16[512,256]{1,0:T(8,128)(2,1)S(1)} %get-tuple-element.94), channel_id=1, source_target_pairs={{0,4},{1,5},{2,6},{3,7},{4,0},{5,1},{6,2},{7,3},{8,12},{9,13},{10,... | collective-permute-start | bytes 786440 | tf_op jit(solution)/shard_map/ppermute | solution.py:46
  (9 other events, 83.2 us)

commit v4 on v3

--- a/solution.py
+++ b/solution.py
@@ -16,7 +16,7 @@
 EXPONENT = float(HD**-0.5 * 1.4426950408889634)
 AXES = ("seq", "head")
 GROUP = 4
-ROWS = 4
+ROWS = 8
 VM = pl.BlockSpec(memory_space=pltpu.VMEM)
 SM = pl.BlockSpec(memory_space=pltpu.SMEM)
 ANY = pl.BlockSpec(memory_space=pl.ANY)
@@ -198,51 +198,47 @@
     )(lists, counts, order, qm, qp, *pieces)
 
 
-def pack_kernel(spot_ref, own_ref, other_ref, own_out, other_out):
-    own_out[...] = own_ref[...]
-    other_out[...] = other_ref[...]
-
-
-def pack_weight(spot, weight):
+def pack_weight(spot, weight, flip, held=None):
     rows = weight.shape[0]
 
-    def part(flip):
-        def place(r, i, spot):
-            step = jnp.where(i == 2, 3, jnp.where(i == 3, 2, i))
-            return r ^ spot[2], (spot[0] + step) % 4 * 2 + (spot[1] ^ flip)
-
-        return pl.BlockSpec((HD, 256), place)
-
-    out = pl.BlockSpec((HD, 256), lambda r, i, spot: (r, i))
-    return pl.pallas_call(
-        pack_kernel,
-        grid_spec=pltpu.PrefetchScalarGridSpec(
-            num_scalar_prefetch=1,
-            grid=(rows // HD, 4),
-            in_specs=[part(0), part(1)],
-            out_specs=[out, out],
-        ),
-        out_shape=[jax.ShapeDtypeStruct((rows, 1024), weight.dtype)] * 2,
+    def kernel(spot_ref, weight_ref, *refs):
+        out_ref = refs[-1]
+        x, yh, yl = spot_ref[0], spot_ref[1], spot_ref[2]
+        for i, d in enumerate((0, 1, 3, 2)):
+            start = ((x + d) % 4 * 2 + (yh ^ flip)) * 256
+            columns = pl.ds(pl.multiple_of(start, 256), 256)
+            for r in range(rows // HD):
+                taken = pl.ds(pl.multiple_of((r ^ yl) * HD, HD), HD)
+                out_ref[r * HD : (r + 1) * HD, i * 256 : (i + 1) * 256] = weight_ref[taken, columns]
+        if held is not None:
+            out_ref[rows:, :] = refs[0][...]
+
+    extra = [] if held is None else [held]
+    return pl.pallas_call(
+        kernel,
+        in_specs=[SM] + [VM] * (1 + len(extra)),
+        out_specs=VM,
+        out_shape=jax.ShapeDtypeStruct((rows * (1 + len(extra)), 1024), weight.dtype),
         compiler_params=pltpu.CompilerParams(vmem_limit_bytes=OUT_VMEM),
         cost_estimate=pl.CostEstimate(flops=1024, bytes_accessed=1024, transcendentals=0),
         name="pack_weight",
-    )(spot, weight, weight)
-
-
-def out_kernel(c0, c1, c2, c3, upper_ref, lower_ref, own_ref, *outs):
+    )(spot, weight, *extra)
+
+
+def out_kernel(c0, c1, c2, c3, weight_ref, own_ref, *outs):
     context = jnp.concatenate([c0[...], c1[...], c2[...], c3[...]], axis=1)
-    weight = jnp.concatenate([upper_ref[...], lower_ref[...]], axis=0)
+    weight = weight_ref[...]
     own_ref[...] = jnp.dot(context, weight[:, :256], preferred_element_type=jnp.float32)
     for k, out in enumerate(outs):
         part = weight[:, 256 * (k + 1) : 256 * (k + 2)]
         out[...] = jnp.dot(context, part, preferred_element_type=jnp.float32).astype(out.dtype)
 
 
-def out_project(contexts, weights):
+def out_project(contexts, weight):
     rows = contexts[0].shape[0]
     return pl.pallas_call(
         out_kernel,
-        in_specs=[VM] * 6,
+        in_specs=[VM] * 5,
         out_specs=[VM] * 4,
         out_shape=[jax.ShapeDtypeStruct((rows, 256), jnp.float32)]
         + [jax.ShapeDtypeStruct((rows, 256), jnp.bfloat16)] * 3,
@@ -251,7 +247,7 @@
             flops=2 * rows * 512 * 1024, bytes_accessed=3 * 2**20, transcendentals=0
         ),
         name="out_project",
-    )(*contexts, *weights)
+    )(*contexts, weight)
 
 
 def sum_kernel(*refs):
@@ -300,7 +296,7 @@
 
     x = head // 2
     spot = jnp.stack([x, yh, yl]).astype(jnp.int32)
-    own_weight, sent_weight = pack_weight(spot, out_weight)
+    sent_weight = pack_weight(spot, out_weight, 1)
 
     barrier = lax.optimization_barrier
     half = jnp.reshape(yl, (1,)).astype(jnp.int32)
@@ -346,13 +342,14 @@
          far_m, core_far_m, far_p, core_far_p, up_m, core_up_m, up_p, core_up_p),
     )
 
-    weights = (own_weight, other_weight)
+    *parts, out_weight = barrier((*parts, out_weight))
+    weight = pack_weight(spot, out_weight, 0, other_weight)
     before = ()
     for k, (mine, partner) in enumerate(zip(parts[:CHUNKS], parts[CHUNKS:])):
         contexts = (
             mine, move(partner, dyl=1), move(mine, dyh=1), move(partner, dyl=1, dyh=1)
         )
-        own, *sent = out_project(contexts, weights)
+        own, *sent = out_project(contexts, weight)
         blocks = [move(block, dx=d) for d, block in zip((1, 3, 2), sent)]
         before = (sum_part(own, blocks, k, before),)
     return before[0]

time: 113 us -> 110 us (0.973); the launches traced: 110 us -> 109 us
  Pallas kernels: 26.7 us -> 23.8 us
  waiting for transfers between devices: 42.2 us -> 44.6 us
    pallas_call x3 -> x4, Pallas kernels: 6.99 us -> 4.01 us  [the longest x2 2.59 us: pack_weight(): pl.pallas_call(kernel, in_specs=[SM] + [VM] * (1 + len(extra)), out_specs...]
    ppermute x31, waiting for transfers between devices: 42.2 us -> 44.6 us  [move(): return lax.ppermute(array, AXES, pairs)]
    unnamed x21 -> x19, local copies, waits for them, and re-layouts: 5.97 us -> 5.17 us
  transfers between devices with their start and end apart: 31 -> 31, of which waited for: 18 -> 18; matrix products, arithmetic and copies ran while one was open for 1% -> 1% of each run, Pallas kernels for 8% -> 6%
where the time goes in v4:
time: 110 us; the launch traced here: 109 us
  waiting for transfers between devices  44.6 us (41%)
  starting transfers between devices  34.7 us (32%)
  Pallas kernels  23.8 us (22%)
  local copies, waits for them, and re-layouts  5.52 us (5%)
    ppermute x31, waiting for transfers between devices, move(): return lax.ppermute(array, AXES, pairs)  44.6 us
    ppermute x31, starting transfers between devices, move(): return lax.ppermute(array, AXES, pairs)  34.7 us
    pallas_call x1, Pallas kernels, attend(): pl.pallas_call(attend_kernel, out_shape=[part] * (2 * CHUNKS), in_specs=[...  9.21 us
    pallas_call x2, Pallas kernels, project(): pl.pallas_call(kernel, grid_spec=pltpu.PrefetchScalarGridSpec(num_scalar_...  8.94 us
    unnamed x19, local copies, waits for them, and re-layouts  5.17 us
    pallas_call x2, Pallas kernels, pack_weight(): pl.pallas_call(kernel, in_specs=[SM] + [VM] * (1 + len(extra)), out_specs...  2.59 us
  transfers between devices with their start and end apart: 31, of which 18 were waited for; matrix products, arithmetic and copies ran while one was open for 1% of the time, Pallas kernels for 6%

profile of v4, /device:TPU:6, one launch (start us, length us, event | category | flops | bytes accessed | tf_op | source)
XLA Modules:
  0.0 109.2 jit_solution(9706830866672222241)
XLA Ops:
  0.0 6.5 %project.2 = (bf16[1024,256]{1,0:T(8,128)(2,1)}, bf16[1024,256]{1,0:T(8,128)(2,1)}) custom-call(s32[1]{0:T(128)} %bitcast.half_ref, bf16[1024,2048]{1,0:T(8,128)(2,1)} %h_ref.3, f32[1,2048]{1,0:T(1,128)} %bitcast.6, bf16[3,2048,256]{2,1,0:T(8,128)(2,1)} %qo.1, bf16[3,2048,256]{2,1,0:T(8,128)(2,1)} %qo.1, bf16[3,2048,256]{2,1,0:T(8,128)(2,1)} %qo.1, ...), custom_call_target="tpu_custom_call" | custom-call | flops 1024 | bytes 1024 | tf_op jit(solution)/shard_map/project/pallas_call | solution.py:81
  6.5 1.6 %collective-permute-start.3 = (bf16[1024,256]{1,0:T(8,128)(2,1)}, bf16[1024,256]{1,0:T(8,128)(2,1)}, u32[]{:S(2)}, u32[]{:S(2)}) collective-permute-start(bf16[1024,256]{1,0:T(8,128)(2,1)} %get-tuple-element.57), channel_id=1, source_target_pairs={{0,64},{1,65},{2,66},{3,67},{4,68},{5,69},{6,70},{7,71},{8,72},{9,... | collective-permute-start | bytes 1572872 | tf_op jit(solution)/shard_map/ppermute | solution.py:46
  9.2 4.0 %collective-permute-start.2 = (bf16[1024,256]{1,0:T(8,128)(2,1)}, bf16[1024,256]{1,0:T(8,128)(2,1)}, u32[]{:S(2)}, u32[]{:S(2)}) collective-permute-start(bf16[1024,256]{1,0:T(8,128)(2,1)} %get-tuple-element.70.rest_0_), channel_id=1, source_target_pairs={{0,48},{1,49},{2,50},{3,51},{4,52},{5,53},{6,54},{7,55},{8,56},{9,... | collective-permute-start | bytes 1572872 | tf_op jit(solution)/shard_map/ppermute | solution.py:46
  13.3 1.2 %copy-done.2 = bf16[256,2048]{1,0:T(8,128)(2,1)S(1)} copy-done((bf16[256,2048]{1,0:T(8,128)(2,1)S(1)}, bf16[256,2048]{1,0:T(8,128)(2,1)}, u32[]{:S(2)}) %copy-start.2) | copy-done | bytes 1048600
  14.5 1.4 %pack_weight.2 = bf16[256,1024]{1,0:T(8,128)(2,1)} custom-call(s32[3]{0:T(128)S(1)} %pad_add_fusion.spot_ref, bf16[256,2048]{1,0:T(8,128)(2,1)S(1)} %copy-done.2), custom_call_target="tpu_custom_call" | custom-call | flops 1024 | bytes 1024 | tf_op jit(solution)/shard_map/pack_weight/pallas_call | solution.py:217
  16.0 4.5 %collective-permute-done.3.rest_2_ = bf16[1024,256]{1,0:T(8,128)(2,1)} collective-permute-done((bf16[1024,256]{1,0:T(8,128)(2,1)}, bf16[1024,256]{1,0:T(8,128)(2,1)}, u32[]{:S(2)}, u32[]{:S(2)}) %collective-permute-start.3) | collective-permute-done | bytes 524320 | tf_op jit(solution)/shard_map/ppermute | solution.py:46
  20.5 4.0 %collective-permute-start.5 = (bf16[1024,256]{1,0:T(8,128)(2,1)}, bf16[1024,256]{1,0:T(8,128)(2,1)}, u32[]{:S(2)}, u32[]{:S(2)}) collective-permute-start(bf16[1024,256]{1,0:T(8,128)(2,1)} %collective-permute-done.3.rest_2_), channel_id=1, source_target_pairs={{0,48},{1,49},{2,50},{3,51},{4,52},{5,53},{6,54},{7,55},{8,56},{9,... | collective-permute-start | bytes 1572872 | tf_op jit(solution)/shard_map/ppermute | solution.py:46
  24.5 3.2 %collective-permute-start.8 = (bf16[256,1024]{1,0:T(8,128)(2,1)}, bf16[256,1024]{1,0:T(8,128)(2,1)}, u32[]{:S(2)}, u32[]{:S(2)}) collective-permute-start(bf16[256,1024]{1,0:T(8,128)(2,1)} %pack_weight.2), channel_id=1, source_target_pairs={{0,1},{1,0},{2,3},{3,2},{4,5},{5,4},{6,7},{7,6},{8,9},{9,8},{10,11... | collective-permute-start | bytes 1572872 | tf_op jit(solution)/shard_map/ppermute | solution.py:46
  27.7 1.8 %collective-permute-done.1.rest_12_ = bf16[1024,256]{1,0:T(8,128)(2,1)} collective-permute-done((bf16[1024,256]{1,0:T(8,128)(2,1)}, bf16[1024,256]{1,0:T(8,128)(2,1)}, u32[]{:S(2)}, u32[]{:S(2)}) %collective-permute-start.1) | collective-permute-done | bytes 524320 | tf_op jit(solution)/shard_map/ppermute | solution.py:46
  29.6 2.2 %copy-done.1 = bf16[1024,2048]{1,0:T(8,128)(2,1)S(1)} copy-done((bf16[1024,2048]{1,0:T(8,128)(2,1)S(1)}, bf16[1024,2048]{1,0:T(8,128)(2,1)}, u32[]{:S(2)}) %copy-start.1) | copy-done | bytes 4194328
  31.8 2.5 %project.3 = (bf16[1024,128]{1,0:T(8,128)(2,1)S(1)}, bf16[1024,128]{1,0:T(8,128)(2,1)S(1)}) custom-call(s32[1]{0:T(128)} %bitcast.half_ref, bf16[1024,2048]{1,0:T(8,128)(2,1)S(1)} %copy-done.1, f32[1,2048]{1,0:T(1,128)S(1)} %bitcast.7, bf16[3,2048,256]{2,1,0:T(8,128)(2,1)S(1)} %copy-done, bf16[3,2048,256]{2,1,0:T(8,128)(2,1)S(1)} %copy-done), custom_call_target="tpu_custom_call" | custom-call | flops 1024 | bytes 1024 | tf_op jit(solution)/shard_map/project/pallas_call | solution.py:81
  35.2 3.6 %collective-permute-done.8.refs_0_ = bf16[256,1024]{1,0:T(8,128)(2,1)} collective-permute-done((bf16[256,1024]{1,0:T(8,128)(2,1)}, bf16[256,1024]{1,0:T(8,128)(2,1)}, u32[]{:S(2)}, u32[]{:S(2)}) %collective-permute-start.8) | collective-permute-done | bytes 524320 | tf_op jit(solution)/shard_map/ppermute | solution.py:46
  40.6 1.3 %collective-permute-start.12 = (s32[16,128]{1,0:T(8,128)S(1)}, s32[16,128]{1,0:T(8,128)S(1)}, u32[]{:S(2)}, u32[]{:S(2)}) collective-permute-start(s32[16,128]{1,0:T(8,128)S(1)} %add_add_fusion), channel_id=1, source_target_pairs={{0,64},{1,65},{2,66},{3,67},{4,68},{5,69},{6,70},{7,71},{8,72},{9,... | collective-permute-start | bytes 24584 | tf_op jit(solution)/shard_map/ppermute | solution.py:46
  41.9 3.2 %collective-permute-start.10 = (bf16[1024,256]{1,0:T(8,128)(2,1)}, bf16[1024,256]{1,0:T(8,128)(2,1)S(1)}, u32[]{:S(2)}, u32[]{:S(2)}) collective-permute-start(bf16[1024,256]{1,0:T(8,128)(2,1)} %collective-permute-done.5.rest_6_), channel_id=1, source_target_pairs={{0,48},{1,49},{2,50},{3,51},{4,52},{5,53},{6,54},{7,55},{8,56},{9,... | collective-permute-start | bytes 1572872 | tf_op jit(solution)/shard_map/ppermute | solution.py:46
  45.0 2.4 %collective-permute-done.12 = s32[16,128]{1,0:T(8,128)S(1)} collective-permute-done((s32[16,128]{1,0:T(8,128)S(1)}, s32[16,128]{1,0:T(8,128)S(1)}, u32[]{:S(2)}, u32[]{:S(2)}) %collective-permute-start.12) | collective-permute-done | bytes 8224 | tf_op jit(solution)/shard_map/ppermute | solution.py:46
  47.9 6.0 %collective-permute-done.9.rest_8_ = bf16[1024,256]{1,0:T(8,128)(2,1)S(1)} collective-permute-done((bf16[1024,256]{1,0:T(8,128)(2,1)}, bf16[1024,256]{1,0:T(8,128)(2,1)S(1)}, u32[]{:S(2)}, u32[]{:S(2)}) %collective-permute-start.9) | collective-permute-done | bytes 524320 | tf_op jit(solution)/shard_map/ppermute | solution.py:46
  54.8 1.3 %collective-permute-done.16.rest_7_ = bf16[1024,256]{1,0:T(8,128)(2,1)S(1)} collective-permute-done((bf16[1024,256]{1,0:T(8,128)(2,1)}, bf16[1024,256]{1,0:T(8,128)(2,1)S(1)}, u32[]{:S(2)}, u32[]{:S(2)}) %collective-permute-start.16) | collective-permute-done | bytes 524320 | tf_op jit(solution)/shard_map/ppermute | solution.py:46
  56.6 1.4 %collective-permute-done.17.rest_9_ = bf16[1024,256]{1,0:T(8,128)(2,1)S(1)} collective-permute-done((bf16[1024,256]{1,0:T(8,128)(2,1)S(1)}, bf16[1024,256]{1,0:T(8,128)(2,1)S(1)}, u32[]{:S(2)}, u32[]{:S(2)}) %collective-permute-start.17) | collective-permute-done | bytes 524320 | tf_op jit(solution)/shard_map/ppermute | solution.py:46
  59.8 9.2 %attend.1 = (bf16[512,128]{1,0:T(8,128)(2,1)S(1)}, bf16[512,128]{1,0:T(8,128)(2,1)S(1)}, bf16[512,128]{1,0:T(8,128)(2,1)S(1)}, bf16[512,128]{1,0:T(8,128)(2,1)S(1)}) custom-call(s32[32,32]{1,0:T(8,128)S(1)} %get-tuple-element.75.list_ref, s32[32]{0:T(128)S(1)} %slice_reduce_fusion.count_ref, s32[32]{0:T(128)S(1)} %get-tuple-element.77.order_ref, ...), custom_call_target="tpu_custom_call" | custom-call | flops 2147483648 | bytes 10485760 | tf_op jit(solution)/shard_map/attend/pallas_call | solution.py:181
  69.0 2.7 %collective-permute-start.26 = (bf16[512,128]{1,0:T(8,128)(2,1)S(1)}, bf16[512,128]{1,0:T(8,128)(2,1)S(1)}, u32[]{:S(2)}, u32[]{:S(2)}) collective-permute-start(bf16[512,128]{1,0:T(8,128)(2,1)S(1)} %get-tuple-element.101.c0), channel_id=1, source_target_pairs={{0,1},{1,0},{2,3},{3,2},{4,5},{5,4},{6,7},{7,6},{8,9},{9,8},{10,11... | collective-permute-start | bytes 393224 | tf_op jit(solution)/shard_map/ppermute | solution.py:46
  73.7 2.2 %collective-permute-done.26.c2 = bf16[512,128]{1,0:T(8,128)(2,1)S(1)} collective-permute-done((bf16[512,128]{1,0:T(8,128)(2,1)S(1)}, bf16[512,128]{1,0:T(8,128)(2,1)S(1)}, u32[]{:S(2)}, u32[]{:S(2)}) %collective-permute-start.26) | collective-permute-done | bytes 131104 | tf_op jit(solution)/shard_map/ppermute | solution.py:46
  75.9 2.7 %collective-permute-done.27.c3 = bf16[512,128]{1,0:T(8,128)(2,1)S(1)} collective-permute-done((bf16[512,128]{1,0:T(8,128)(2,1)S(1)}, bf16[512,128]{1,0:T(8,128)(2,1)S(1)}, u32[]{:S(2)}, u32[]{:S(2)}) %collective-permute-start.27) | collective-permute-done | bytes 131104 | tf_op jit(solution)/shard_map/ppermute | solution.py:46
  80.1 1.7 %collective-permute-start.20 = (bf16[512,128]{1,0:T(8,128)(2,1)S(1)}, bf16[512,128]{1,0:T(8,128)(2,1)S(1)}, u32[]{:S(2)}, u32[]{:S(2)}) collective-permute-start(bf16[512,128]{1,0:T(8,128)(2,1)S(1)} %get-tuple-element.93.c0), channel_id=1, source_target_pairs={{0,1},{1,0},{2,3},{3,2},{4,5},{5,4},{6,7},{7,6},{8,9},{9,8},{10,11... | collective-permute-start | bytes 393224 | tf_op jit(solution)/shard_map/ppermute | solution.py:46
  81.9 2.1 %collective-permute-start.21 = (bf16[512,128]{1,0:T(8,128)(2,1)S(1)}, bf16[512,128]{1,0:T(8,128)(2,1)S(1)}, u32[]{:S(2)}, u32[]{:S(2)}) collective-permute-start(bf16[512,128]{1,0:T(8,128)(2,1)S(1)} %get-tuple-element.94), channel_id=1, source_target_pairs={{0,65},{1,64},{2,67},{3,66},{4,69},{5,68},{6,71},{7,70},{8,73},{9,... | collective-permute-start | bytes 393224 | tf_op jit(solution)/shard_map/ppermute | solution.py:46
  83.9 1.5 %collective-permute-start.29 = (bf16[512,256]{1,0:T(8,128)(2,1)S(1)}, bf16[512,256]{1,0:T(8,128)(2,1)S(1)}, u32[]{:S(2)}, u32[]{:S(2)}) collective-permute-start(bf16[512,256]{1,0:T(8,128)(2,1)S(1)} %get-tuple-element.105), channel_id=1, source_target_pairs={{0,6},{1,7},{2,0},{3,1},{4,2},{5,3},{6,4},{7,5},{8,14},{9,15},{10,... | collective-permute-start | bytes 786440 | tf_op jit(solution)/shard_map/ppermute | solution.py:46
  85.5 2.5 %collective-permute-done.20.c2 = bf16[512,128]{1,0:T(8,128)(2,1)S(1)} collective-permute-done((bf16[512,128]{1,0:T(8,128)(2,1)S(1)}, bf16[512,128]{1,0:T(8,128)(2,1)S(1)}, u32[]{:S(2)}, u32[]{:S(2)}) %collective-permute-start.20) | collective-permute-done | bytes 131104 | tf_op jit(solution)/shard_map/ppermute | solution.py:46
  88.0 2.4 %collective-permute-start.30 = (bf16[512,256]{1,0:T(8,128)(2,1)S(1)}, bf16[512,256]{1,0:T(8,128)(2,1)S(1)}, u32[]{:S(2)}, u32[]{:S(2)}) collective-permute-start(bf16[512,256]{1,0:T(8,128)(2,1)S(1)} %get-tuple-element.106), channel_id=1, source_target_pairs={{0,4},{1,5},{2,6},{3,7},{4,0},{5,1},{6,2},{7,3},{8,12},{9,13},{10,... | collective-permute-start | bytes 786440 | tf_op jit(solution)/shard_map/ppermute | solution.py:46
  91.1 1.9 %collective-permute-start.22 = (bf16[512,256]{1,0:T(8,128)(2,1)S(1)}, bf16[512,256]{1,0:T(8,128)(2,1)S(1)}, u32[]{:S(2)}, u32[]{:S(2)}) collective-permute-start(bf16[512,256]{1,0:T(8,128)(2,1)S(1)} %get-tuple-element.98), channel_id=1, source_target_pairs={{0,2},{1,3},{2,4},{3,5},{4,6},{5,7},{6,0},{7,1},{8,10},{9,11},{10,... | collective-permute-start | bytes 786440 | tf_op jit(solution)/shard_map/ppermute | solution.py:46
  93.2 1.3 %collective-permute-start.24 = (bf16[512,256]{1,0:T(8,128)(2,1)S(1)}, bf16[512,256]{1,0:T(8,128)(2,1)S(1)}, u32[]{:S(2)}, u32[]{:S(2)}) collective-permute-start(bf16[512,256]{1,0:T(8,128)(2,1)S(1)} %get-tuple-element.100), channel_id=1, source_target_pairs={{0,4},{1,5},{2,6},{3,7},{4,0},{5,1},{6,2},{7,3},{8,12},{9,13},{10,... | collective-permute-start | bytes 786440 | tf_op jit(solution)/shard_map/ppermute | solution.py:46
  95.6 3.7 %collective-permute-done.30.refs_3_ = bf16[512,256]{1,0:T(8,128)(2,1)S(1)} collective-permute-done((bf16[512,256]{1,0:T(8,128)(2,1)S(1)}, bf16[512,256]{1,0:T(8,128)(2,1)S(1)}, u32[]{:S(2)}, u32[]{:S(2)}) %collective-permute-start.30) | collective-permute-done | bytes 262176 | tf_op jit(solution)/shard_map/ppermute | solution.py:46
  100.2 2.0 %collective-permute-done.22.refs_1_ = bf16[512,256]{1,0:T(8,128)(2,1)S(1)} collective-permute-done((bf16[512,256]{1,0:T(8,128)(2,1)S(1)}, bf16[512,256]{1,0:T(8,128)(2,1)S(1)}, u32[]{:S(2)}, u32[]{:S(2)}) %collective-permute-start.22) | collective-permute-done | bytes 262176 | tf_op jit(solution)/shard_map/ppermute | solution.py:46
  102.2 6.2 %collective-permute-done.23.refs_2_ = bf16[512,256]{1,0:T(8,128)(2,1)S(1)} collective-permute-done((bf16[512,256]{1,0:T(8,128)(2,1)S(1)}, bf16[512,256]{1,0:T(8,128)(2,1)S(1)}, u32[]{:S(2)}, u32[]{:S(2)}) %collective-permute-start.23) | collective-permute-done | bytes 262176 | tf_op jit(solution)/shard_map/ppermute | solution.py:46
  (68 shorter events, 14.8 us)
Async XLA Ops:
  0.0 29.6 %copy-start.5 = (f32[2048]{0:T(1024)S(1)}, f32[2048]{0:T(1024)}, u32[]{:S(2)}) copy-start(f32[2048]{0:T(1024)} %param.7) | copy-start | bytes 24580
  6.5 14.0 %collective-permute-start.3 = (bf16[1024,256]{1,0:T(8,128)(2,1)}, bf16[1024,256]{1,0:T(8,128)(2,1)}, u32[]{:S(2)}, u32[]{:S(2)}) collective-permute-start(bf16[1024,256]{1,0:T(8,128)(2,1)} %get-tuple-element.57), channel_id=1, source_target_pairs={{0,64},{1,65},{2,66},{3,67},{4,68},{5,69},{6,70},{7,71},{8,72},{9,... | collective-permute-start | bytes 1572872 | tf_op jit(solution)/shard_map/ppermute | solution.py:46
  8.1 1.1 %collective-permute-start = (s32[16]{0:T(128)S(1)}, s32[16]{0:T(128)S(1)}, u32[]{:S(2)}, u32[]{:S(2)}) collective-permute-start(s32[16]{0:T(128)S(1)} %copy-done.8), channel_id=1, source_target_pairs={{0,8},{1,9},{2,10},{3,11},{4,12},{5,13},{6,14},{7,15},{8,0},{9,1},... | collective-permute-start | bytes 200 | tf_op jit(solution)/shard_map/ppermute | solution.py:46
  9.2 18.5 %collective-permute-start.2 = (bf16[1024,256]{1,0:T(8,128)(2,1)}, bf16[1024,256]{1,0:T(8,128)(2,1)}, u32[]{:S(2)}, u32[]{:S(2)}) collective-permute-start(bf16[1024,256]{1,0:T(8,128)(2,1)} %get-tuple-element.70.rest_0_), channel_id=1, source_target_pairs={{0,48},{1,49},{2,50},{3,51},{4,52},{5,53},{6,54},{7,55},{8,56},{9,... | collective-permute-start | bytes 1572872 | tf_op jit(solution)/shard_map/ppermute | solution.py:46
  13.2 16.3 %collective-permute-start.1 = (bf16[1024,256]{1,0:T(8,128)(2,1)}, bf16[1024,256]{1,0:T(8,128)(2,1)}, u32[]{:S(2)}, u32[]{:S(2)}) collective-permute-start(bf16[1024,256]{1,0:T(8,128)(2,1)} %get-tuple-element.70.rest_0_), channel_id=1, source_target_pairs={{0,16},{1,17},{2,18},{3,19},{4,20},{5,21},{6,22},{7,23},{8,24},{9,... | collective-permute-start | bytes 1572872 | tf_op jit(solution)/shard_map/ppermute | solution.py:46
  20.5 18.4 %collective-permute-start.5 = (bf16[1024,256]{1,0:T(8,128)(2,1)}, bf16[1024,256]{1,0:T(8,128)(2,1)}, u32[]{:S(2)}, u32[]{:S(2)}) collective-permute-start(bf16[1024,256]{1,0:T(8,128)(2,1)} %collective-permute-done.3.rest_2_), channel_id=1, source_target_pairs={{0,48},{1,49},{2,50},{3,51},{4,52},{5,53},{6,54},{7,55},{8,56},{9,... | collective-permute-start | bytes 1572872 | tf_op jit(solution)/shard_map/ppermute | solution.py:46
  24.5 15.2 %collective-permute-start.4 = (bf16[1024,256]{1,0:T(8,128)(2,1)}, bf16[1024,256]{1,0:T(8,128)(2,1)}, u32[]{:S(2)}, u32[]{:S(2)}) collective-permute-start(bf16[1024,256]{1,0:T(8,128)(2,1)} %collective-permute-done.3.rest_2_), channel_id=1, source_target_pairs={{0,16},{1,17},{2,18},{3,19},{4,20},{5,21},{6,22},{7,23},{8,24},{9,... | collective-permute-start | bytes 1572872 | tf_op jit(solution)/shard_map/ppermute | solution.py:46
  24.5 14.3 %collective-permute-start.8 = (bf16[256,1024]{1,0:T(8,128)(2,1)}, bf16[256,1024]{1,0:T(8,128)(2,1)}, u32[]{:S(2)}, u32[]{:S(2)}) collective-permute-start(bf16[256,1024]{1,0:T(8,128)(2,1)} %pack_weight.2), channel_id=1, source_target_pairs={{0,1},{1,0},{2,3},{3,2},{4,5},{5,4},{6,7},{7,6},{8,9},{9,8},{10,11... | collective-permute-start | bytes 1572872 | tf_op jit(solution)/shard_map/ppermute | solution.py:46
  27.7 12.0 %collective-permute-start.7 = (bf16[1024,256]{1,0:T(8,128)(2,1)}, bf16[1024,256]{1,0:T(8,128)(2,1)}, u32[]{:S(2)}, u32[]{:S(2)}) collective-permute-start(bf16[1024,256]{1,0:T(8,128)(2,1)} %collective-permute-done.2.rest_4_), channel_id=1, source_target_pairs={{0,8},{1,9},{2,10},{3,11},{4,12},{5,13},{6,14},{7,15},{8,0},{9,1},... | collective-permute-start | bytes 1572872 | tf_op jit(solution)/shard_map/ppermute | solution.py:46
  29.5 10.2 %collective-permute-start.6 = (bf16[1024,256]{1,0:T(8,128)(2,1)}, bf16[1024,256]{1,0:T(8,128)(2,1)}, u32[]{:S(2)}, u32[]{:S(2)}) collective-permute-start(bf16[1024,256]{1,0:T(8,128)(2,1)} %collective-permute-done.1.rest_12_), channel_id=1, source_target_pairs={{0,8},{1,9},{2,10},{3,11},{4,12},{5,13},{6,14},{7,15},{8,0},{9,1},... | collective-permute-start | bytes 1572872 | tf_op jit(solution)/shard_map/ppermute | solution.py:46
  39.7 14.2 %collective-permute-start.9 = (bf16[1024,256]{1,0:T(8,128)(2,1)}, bf16[1024,256]{1,0:T(8,128)(2,1)S(1)}, u32[]{:S(2)}, u32[]{:S(2)}) collective-permute-start(bf16[1024,256]{1,0:T(8,128)(2,1)} %collective-permute-done.1.rest_12_), channel_id=1, source_target_pairs={{0,16},{1,17},{2,18},{3,19},{4,20},{5,21},{6,22},{7,23},{8,24},{9,... | collective-permute-start | bytes 1572872 | tf_op jit(solution)/shard_map/ppermute | solution.py:46
  39.8 7.6 %collective-permute-start.11 = (bf16[1024,128]{1,0:T(8,128)(2,1)}, bf16[1024,128]{1,0:T(8,128)(2,1)S(1)}, u32[]{:S(2)}, u32[]{:S(2)}) collective-permute-start(bf16[1024,128]{1,0:T(8,128)(2,1)} %copy-done.6), channel_id=1, source_target_pairs={{0,64},{1,65},{2,66},{3,67},{4,68},{5,69},{6,70},{7,71},{8,72},{9,... | collective-permute-start | bytes 786440 | tf_op jit(solution)/shard_map/ppermute | solution.py:46
  40.6 6.8 %collective-permute-start.12 = (s32[16,128]{1,0:T(8,128)S(1)}, s32[16,128]{1,0:T(8,128)S(1)}, u32[]{:S(2)}, u32[]{:S(2)}) collective-permute-start(s32[16,128]{1,0:T(8,128)S(1)} %add_add_fusion), channel_id=1, source_target_pairs={{0,64},{1,65},{2,66},{3,67},{4,68},{5,69},{6,70},{7,71},{8,72},{9,... | collective-permute-start | bytes 24584 | tf_op jit(solution)/shard_map/ppermute | solution.py:46
  41.9 12.9 %collective-permute-start.10 = (bf16[1024,256]{1,0:T(8,128)(2,1)}, bf16[1024,256]{1,0:T(8,128)(2,1)S(1)}, u32[]{:S(2)}, u32[]{:S(2)}) collective-permute-start(bf16[1024,256]{1,0:T(8,128)(2,1)} %collective-permute-done.5.rest_6_), channel_id=1, source_target_pairs={{0,48},{1,49},{2,50},{3,51},{4,52},{5,53},{6,54},{7,55},{8,56},{9,... | collective-permute-start | bytes 1572872 | tf_op jit(solution)/shard_map/ppermute | solution.py:46
  47.4 7.4 %collective-permute-start.13 = (bf16[1024,256]{1,0:T(8,128)(2,1)}, bf16[1024,256]{1,0:T(8,128)(2,1)S(1)}, u32[]{:S(2)}, u32[]{:S(2)}) collective-permute-start(bf16[1024,256]{1,0:T(8,128)(2,1)} %get-tuple-element.70.rest_0_), channel_id=1, source_target_pairs={{0,8},{1,9},{2,10},{3,11},{4,12},{5,13},{6,14},{7,15},{8,0},{9,1},... | collective-permute-start | bytes 1572872 | tf_op jit(solution)/shard_map/ppermute | solution.py:46
  47.4 7.4 %collective-permute-start.14 = (bf16[1024,256]{1,0:T(8,128)(2,1)}, bf16[1024,256]{1,0:T(8,128)(2,1)S(1)}, u32[]{:S(2)}, u32[]{:S(2)}) collective-permute-start(bf16[1024,256]{1,0:T(8,128)(2,1)} %collective-permute-done.3.rest_2_), channel_id=1, source_target_pairs={{0,8},{1,9},{2,10},{3,11},{4,12},{5,13},{6,14},{7,15},{8,0},{9,1},... | collective-permute-start | bytes 1572872 | tf_op jit(solution)/shard_map/ppermute | solution.py:46
  47.9 6.9 %collective-permute-start.15 = (bf16[1024,256]{1,0:T(8,128)(2,1)}, bf16[1024,256]{1,0:T(8,128)(2,1)S(1)}, u32[]{:S(2)}, u32[]{:S(2)}) collective-permute-start(bf16[1024,256]{1,0:T(8,128)(2,1)} %collective-permute-done.4.rest_14_), channel_id=1, source_target_pairs={{0,8},{1,9},{2,10},{3,11},{4,12},{5,13},{6,14},{7,15},{8,0},{9,1},... | collective-permute-start | bytes 1572872 | tf_op jit(solution)/shard_map/ppermute | solution.py:46
  54.0 2.1 %collective-permute-start.16 = (bf16[1024,256]{1,0:T(8,128)(2,1)}, bf16[1024,256]{1,0:T(8,128)(2,1)S(1)}, u32[]{:S(2)}, u32[]{:S(2)}) collective-permute-start(bf16[1024,256]{1,0:T(8,128)(2,1)} %collective-permute-done.5.rest_6_), channel_id=1, source_target_pairs={{0,8},{1,9},{2,10},{3,11},{4,12},{5,13},{6,14},{7,15},{8,0},{9,1},... | collective-permute-start | bytes 1572872 | tf_op jit(solution)/shard_map/ppermute | solution.py:46
  56.1 1.9 %collective-permute-start.17 = (bf16[1024,256]{1,0:T(8,128)(2,1)S(1)}, bf16[1024,256]{1,0:T(8,128)(2,1)S(1)}, u32[]{:S(2)}, u32[]{:S(2)}) collective-permute-start(bf16[1024,256]{1,0:T(8,128)(2,1)S(1)} %collective-permute-done.9.rest_8_), channel_id=1, source_target_pairs={{0,8},{1,9},{2,10},{3,11},{4,12},{5,13},{6,14},{7,15},{8,0},{9,1},... | collective-permute-start | bytes 1572872 | tf_op jit(solution)/shard_map/ppermute | solution.py:46
  56.2 2.5 %collective-permute-start.18 = (bf16[1024,256]{1,0:T(8,128)(2,1)S(1)}, bf16[1024,256]{1,0:T(8,128)(2,1)S(1)}, u32[]{:S(2)}, u32[]{:S(2)}) collective-permute-start(bf16[1024,256]{1,0:T(8,128)(2,1)S(1)} %collective-permute-done.10.rest_10_), channel_id=1, source_target_pairs={{0,8},{1,9},{2,10},{3,11},{4,12},{5,13},{6,14},{7,15},{8,0},{9,1},... | collective-permute-start | bytes 1572872 | tf_op jit(solution)/shard_map/ppermute | solution.py:46
  69.0 6.9 %collective-permute-start.26 = (bf16[512,128]{1,0:T(8,128)(2,1)S(1)}, bf16[512,128]{1,0:T(8,128)(2,1)S(1)}, u32[]{:S(2)}, u32[]{:S(2)}) collective-permute-start(bf16[512,128]{1,0:T(8,128)(2,1)S(1)} %get-tuple-element.101.c0), channel_id=1, source_target_pairs={{0,1},{1,0},{2,3},{3,2},{4,5},{5,4},{6,7},{7,6},{8,9},{9,8},{10,11... | collective-permute-start | bytes 393224 | tf_op jit(solution)/shard_map/ppermute | solution.py:46
  71.7 7.0 %collective-permute-start.27 = (bf16[512,128]{1,0:T(8,128)(2,1)S(1)}, bf16[512,128]{1,0:T(8,128)(2,1)S(1)}, u32[]{:S(2)}, u32[]{:S(2)}) collective-permute-start(bf16[512,128]{1,0:T(8,128)(2,1)S(1)} %get-tuple-element.102), channel_id=1, source_target_pairs={{0,65},{1,64},{2,67},{3,66},{4,69},{5,68},{6,71},{7,70},{8,73},{9,... | collective-permute-start | bytes 393224 | tf_op jit(solution)/shard_map/ppermute | solution.py:46
  71.7 7.0 %collective-permute-start.25 = (bf16[512,128]{1,0:T(8,128)(2,1)S(1)}, bf16[512,128]{1,0:T(8,128)(2,1)S(1)}, u32[]{:S(2)}, u32[]{:S(2)}) collective-permute-start(bf16[512,128]{1,0:T(8,128)(2,1)S(1)} %get-tuple-element.102), channel_id=1, source_target_pairs={{0,64},{1,65},{2,66},{3,67},{4,68},{5,69},{6,70},{7,71},{8,72},{9,... | collective-permute-start | bytes 393224 | tf_op jit(solution)/shard_map/ppermute | solution.py:46
  79.4 13.9 %collective-permute-start.28 = (bf16[512,256]{1,0:T(8,128)(2,1)S(1)}, bf16[512,256]{1,0:T(8,128)(2,1)S(1)}, u32[]{:S(2)}, u32[]{:S(2)}) collective-permute-start(bf16[512,256]{1,0:T(8,128)(2,1)S(1)} %get-tuple-element.104), channel_id=1, source_target_pairs={{0,2},{1,3},{2,4},{3,5},{4,6},{5,7},{6,0},{7,1},{8,10},{9,11},{10,... | collective-permute-start | bytes 786440 | tf_op jit(solution)/shard_map/ppermute | solution.py:46
  80.1 7.9 %collective-permute-start.20 = (bf16[512,128]{1,0:T(8,128)(2,1)S(1)}, bf16[512,128]{1,0:T(8,128)(2,1)S(1)}, u32[]{:S(2)}, u32[]{:S(2)}) collective-permute-start(bf16[512,128]{1,0:T(8,128)(2,1)S(1)} %get-tuple-element.93.c0), channel_id=1, source_target_pairs={{0,1},{1,0},{2,3},{3,2},{4,5},{5,4},{6,7},{7,6},{8,9},{9,8},{10,11... | collective-permute-start | bytes 393224 | tf_op jit(solution)/shard_map/ppermute | solution.py:46
  81.9 8.5 %collective-permute-start.21 = (bf16[512,128]{1,0:T(8,128)(2,1)S(1)}, bf16[512,128]{1,0:T(8,128)(2,1)S(1)}, u32[]{:S(2)}, u32[]{:S(2)}) collective-permute-start(bf16[512,128]{1,0:T(8,128)(2,1)S(1)} %get-tuple-element.94), channel_id=1, source_target_pairs={{0,65},{1,64},{2,67},{3,66},{4,69},{5,68},{6,71},{7,70},{8,73},{9,... | collective-permute-start | bytes 393224 | tf_op jit(solution)/shard_map/ppermute | solution.py:46
  83.9 6.5 %collective-permute-start.19 = (bf16[512,128]{1,0:T(8,128)(2,1)S(1)}, bf16[512,128]{1,0:T(8,128)(2,1)S(1)}, u32[]{:S(2)}, u32[]{:S(2)}) collective-permute-start(bf16[512,128]{1,0:T(8,128)(2,1)S(1)} %get-tuple-element.94), channel_id=1, source_target_pairs={{0,64},{1,65},{2,66},{3,67},{4,68},{5,69},{6,70},{7,71},{8,72},{9,... | collective-permute-start | bytes 393224 | tf_op jit(solution)/shard_map/ppermute | solution.py:46
  83.9 11.7 %collective-permute-start.29 = (bf16[512,256]{1,0:T(8,128)(2,1)S(1)}, bf16[512,256]{1,0:T(8,128)(2,1)S(1)}, u32[]{:S(2)}, u32[]{:S(2)}) collective-permute-start(bf16[512,256]{1,0:T(8,128)(2,1)S(1)} %get-tuple-element.105), channel_id=1, source_target_pairs={{0,6},{1,7},{2,0},{3,1},{4,2},{5,3},{6,4},{7,5},{8,14},{9,15},{10,... | collective-permute-start | bytes 786440 | tf_op jit(solution)/shard_map/ppermute | solution.py:46
  88.0 11.4 %collective-permute-start.30 = (bf16[512,256]{1,0:T(8,128)(2,1)S(1)}, bf16[512,256]{1,0:T(8,128)(2,1)S(1)}, u32[]{:S(2)}, u32[]{:S(2)}) collective-permute-start(bf16[512,256]{1,0:T(8,128)(2,1)S(1)} %get-tuple-element.106), channel_id=1, source_target_pairs={{0,4},{1,5},{2,6},{3,7},{4,0},{5,1},{6,2},{7,3},{8,12},{9,13},{10,... | collective-permute-start | bytes 786440 | tf_op jit(solution)/shard_map/ppermute | solution.py:46
  91.1 11.1 %collective-permute-start.22 = (bf16[512,256]{1,0:T(8,128)(2,1)S(1)}, bf16[512,256]{1,0:T(8,128)(2,1)S(1)}, u32[]{:S(2)}, u32[]{:S(2)}) collective-permute-start(bf16[512,256]{1,0:T(8,128)(2,1)S(1)} %get-tuple-element.98), channel_id=1, source_target_pairs={{0,2},{1,3},{2,4},{3,5},{4,6},{5,7},{6,0},{7,1},{8,10},{9,11},{10,... | collective-permute-start | bytes 786440 | tf_op jit(solution)/shard_map/ppermute | solution.py:46
  93.0 15.4 %collective-permute-start.23 = (bf16[512,256]{1,0:T(8,128)(2,1)S(1)}, bf16[512,256]{1,0:T(8,128)(2,1)S(1)}, u32[]{:S(2)}, u32[]{:S(2)}) collective-permute-start(bf16[512,256]{1,0:T(8,128)(2,1)S(1)} %get-tuple-element.99), channel_id=1, source_target_pairs={{0,6},{1,7},{2,0},{3,1},{4,2},{5,3},{6,4},{7,5},{8,14},{9,15},{10,... | collective-permute-start | bytes 786440 | tf_op jit(solution)/shard_map/ppermute | solution.py:46
  93.2 15.2 %collective-permute-start.24 = (bf16[512,256]{1,0:T(8,128)(2,1)S(1)}, bf16[512,256]{1,0:T(8,128)(2,1)S(1)}, u32[]{:S(2)}, u32[]{:S(2)}) collective-permute-start(bf16[512,256]{1,0:T(8,128)(2,1)S(1)} %get-tuple-element.100), channel_id=1, source_target_pairs={{0,4},{1,5},{2,6},{3,7},{4,0},{5,1},{6,2},{7,3},{8,12},{9,13},{10,... | collective-permute-start | bytes 786440 | tf_op jit(solution)/shard_map/ppermute | solution.py:46
  (8 other events, 76.1 us)

commit v5 on v4

--- a/solution.py
+++ b/solution.py
@@ -225,13 +225,19 @@
     )(spot, weight, *extra)
 
 
-def out_kernel(c0, c1, c2, c3, weight_ref, own_ref, *outs):
+def out_kernel(c0, c1, c2, c3, weight_ref, own_ref, plus_ref, minus_ref, up_ref, down_ref):
     context = jnp.concatenate([c0[...], c1[...], c2[...], c3[...]], axis=1)
-    weight = weight_ref[...]
-    own_ref[...] = jnp.dot(context, weight[:, :256], preferred_element_type=jnp.float32)
-    for k, out in enumerate(outs):
-        part = weight[:, 256 * (k + 1) : 256 * (k + 2)]
-        out[...] = jnp.dot(context, part, preferred_element_type=jnp.float32).astype(out.dtype)
+
+    def product(k):
+        part = weight_ref[:, 256 * k : 256 * (k + 1)]
+        return jnp.dot(context, part, preferred_element_type=jnp.float32)
+
+    far = product(3).astype(up_ref.dtype)
+    half = up_ref.shape[0]
+    up_ref[...] = far[:half]
+    down_ref[...] = far[half:]
+    for k, out in enumerate((own_ref, plus_ref, minus_ref)):
+        out[...] = product(k)
 
 
 def out_project(contexts, weight):
@@ -239,9 +245,9 @@
     return pl.pallas_call(
         out_kernel,
         in_specs=[VM] * 5,
-        out_specs=[VM] * 4,
-        out_shape=[jax.ShapeDtypeStruct((rows, 256), jnp.float32)]
-        + [jax.ShapeDtypeStruct((rows, 256), jnp.bfloat16)] * 3,
+        out_specs=[VM] * 5,
+        out_shape=[jax.ShapeDtypeStruct((rows, 256), jnp.float32)] * 3
+        + [jax.ShapeDtypeStruct((rows // 2, 256), jnp.bfloat16)] * 2,
         compiler_params=pltpu.CompilerParams(vmem_limit_bytes=OUT_VMEM),
         cost_estimate=pl.CostEstimate(
             flops=2 * rows * 512 * 1024, bytes_accessed=3 * 2**20, transcendentals=0
@@ -250,27 +256,48 @@
     )(*contexts, weight)
 
 
-def sum_kernel(*refs):
-    own_ref, blocks, out_ref = refs[0], refs[1:4], refs[-1]
-    total = own_ref[...]
-    for block in blocks:
-        total = total + block[...].astype(jnp.float32)
-    out_ref[...] = total.astype(out_ref.dtype)
-
-
-def sum_part(own, blocks, part, before):
-    rows, columns = own.shape
-    whole = pl.BlockSpec((rows, columns), lambda i: (0, 0))
+def sum_kernel(plus_ref, minus_ref, up_ref, down_ref, plus_out, minus_out):
+    half = up_ref.shape[0]
+    plus, minus = plus_ref[...], minus_ref[...]
+    plus_out[:half, :] = (plus[:half] + up_ref[...].astype(jnp.float32)).astype(plus_out.dtype)
+    plus_out[half:, :] = plus[half:].astype(plus_out.dtype)
+    minus_out[:half, :] = minus[:half].astype(minus_out.dtype)
+    lower = minus[half:] + down_ref[...].astype(jnp.float32)
+    minus_out[half:, :] = lower.astype(minus_out.dtype)
+
+
+def sum_blocks(plus, minus, up, down):
     return pl.pallas_call(
         sum_kernel,
-        grid=(1,),
-        in_specs=[whole] * 4 + [ANY] * len(before),
-        out_specs=pl.BlockSpec((rows, columns), lambda i: (part, 0)),
-        out_shape=jax.ShapeDtypeStruct((rows * CHUNKS, columns), jnp.bfloat16),
-        input_output_aliases={4: 0} if before else {},
+        in_specs=[VM] * 4,
+        out_specs=[VM] * 2,
+        out_shape=[jax.ShapeDtypeStruct(plus.shape, jnp.bfloat16)] * 2,
         compiler_params=pltpu.CompilerParams(vmem_limit_bytes=OUT_VMEM),
-        name="sum_part",
-    )(own, *blocks, *before)
+        name="sum_blocks",
+    )(plus, minus, up, down)
+
+
+def finish_kernel(*refs):
+    out_ref = refs[-1]
+    rows = refs[0].shape[0]
+    for k in range(2):
+        own, *blocks = refs[3 * k : 3 * k + 3]
+        total = own[...]
+        for block in blocks:
+            total = total + block[...].astype(jnp.float32)
+        out_ref[k * rows : (k + 1) * rows, :] = total.astype(out_ref.dtype)
+
+
+def finish(first, second):
+    rows, columns = first[0].shape
+    return pl.pallas_call(
+        finish_kernel,
+        in_specs=[VM] * 6,
+        out_specs=VM,
+        out_shape=jax.ShapeDtypeStruct((2 * rows, columns), jnp.bfloat16),
+        compiler_params=pltpu.CompilerParams(vmem_limit_bytes=OUT_VMEM),
+        name="finish",
+    )(*first, *second)
 
 
 def place_lists(tile, counts, yl, z, core):
@@ -344,15 +371,16 @@
 
     *parts, out_weight = barrier((*parts, out_weight))
     weight = pack_weight(spot, out_weight, 0, other_weight)
-    before = ()
-    for k, (mine, partner) in enumerate(zip(parts[:CHUNKS], parts[CHUNKS:])):
-        contexts = (
-            mine, move(partner, dyl=1), move(mine, dyh=1), move(partner, dyl=1, dyh=1)
-        )
-        own, *sent = out_project(contexts, weight)
-        blocks = [move(block, dx=d) for d, block in zip((1, 3, 2), sent)]
-        before = (sum_part(own, blocks, k, before),)
-    return before[0]
+    contexts = [
+        (mine, move(partner, dyl=1), move(mine, dyh=1), move(partner, dyl=1, dyh=1))
+        for mine, partner in zip(parts[:CHUNKS], parts[CHUNKS:])
+    ]
+    done = []
+    for held in contexts:
+        own, plus, minus, up, down = out_project(held, weight)
+        plus, minus = sum_blocks(plus, minus, move(up, dx=1), move(down, dx=-1))
+        done.append((own, move(plus, dx=1), move(minus, dx=-1)))
+    return finish(*done)
 
 
 def solution(mesh):

time: 110 us -> 107 us (0.973)
  waiting for transfers between devices: 44.6 us -> 41.8 us
    ppermute x31 -> x33, waiting for transfers between devices: 44.6 us -> 41.8 us  [move(): return lax.ppermute(array, AXES, pairs)]
    pallas_call x4 -> x5, Pallas kernels: 3.05 us -> 2.5 us  [the longest x2 1.42 us: out_project(): pl.pallas_call(out_kernel, in_specs=[VM] * 5, out_specs=[VM] * 5, out_sha...]
    ppermute x31 -> x33, starting transfers between devices: 34.7 us -> 34.9 us  [move(): return lax.ppermute(array, AXES, pairs)]
  transfers between devices with their start and end apart: 31 -> 33, of which waited for: 18 -> 20; matrix products, arithmetic and copies ran while one was open for 1% -> 1% of each run, Pallas kernels for 6% -> 6%
where the time goes in v5:
time: 107 us
  waiting for transfers between devices  41.8 us (39%)
  starting transfers between devices  34.9 us (33%)
  Pallas kernels  23.8 us (22%)
  local copies, waits for them, and re-layouts  5.52 us (5%)
    ppermute x33, waiting for transfers between devices, move(): return lax.ppermute(array, AXES, pairs)  41.8 us
    ppermute x33, starting transfers between devices, move(): return lax.ppermute(array, AXES, pairs)  34.9 us
    pallas_call x1, Pallas kernels, attend(): pl.pallas_call(attend_kernel, out_shape=[part] * (2 * CHUNKS), in_specs=[...  9.77 us
    pallas_call x2, Pallas kernels, project(): pl.pallas_call(kernel, grid_spec=pltpu.PrefetchScalarGridSpec(num_scalar_...  8.94 us
    unnamed x19, local copies, waits for them, and re-layouts  5.17 us
    pallas_call x2, Pallas kernels, pack_weight(): pl.pallas_call(kernel, in_specs=[SM] + [VM] * (1 + len(extra)), out_specs...  2.61 us
  transfers between devices with their start and end apart: 33, of which 20 were waited for; matrix products, arithmetic and copies ran while one was open for 1% of the time, Pallas kernels for 6%

profile of v5, /device:TPU:6, one launch (start us, length us, event | category | flops | bytes accessed | tf_op | source)
XLA Modules:
  0.0 106.6 jit_solution(3620093949198387841)
XLA Ops:
  0.0 6.5 %project.2 = (bf16[1024,256]{1,0:T(8,128)(2,1)}, bf16[1024,256]{1,0:T(8,128)(2,1)}) custom-call(s32[1]{0:T(128)} %bitcast.half_ref, bf16[1024,2048]{1,0:T(8,128)(2,1)} %h_ref.3, f32[1,2048]{1,0:T(1,128)} %bitcast.6, bf16[3,2048,256]{2,1,0:T(8,128)(2,1)} %qo.1, bf16[3,2048,256]{2,1,0:T(8,128)(2,1)} %qo.1, bf16[3,2048,256]{2,1,0:T(8,128)(2,1)} %qo.1, ...), custom_call_target="tpu_custom_call" | custom-call | flops 1024 | bytes 1024 | tf_op jit(solution)/shard_map/project/pallas_call | solution.py:81
  6.5 1.6 %collective-permute-start.3 = (bf16[1024,256]{1,0:T(8,128)(2,1)}, bf16[1024,256]{1,0:T(8,128)(2,1)}, u32[]{:S(2)}, u32[]{:S(2)}) collective-permute-start(bf16[1024,256]{1,0:T(8,128)(2,1)} %get-tuple-element.63), channel_id=1, source_target_pairs={{0,64},{1,65},{2,66},{3,67},{4,68},{5,69},{6,70},{7,71},{8,72},{9,... | collective-permute-start | bytes 1572872 | tf_op jit(solution)/shard_map/ppermute | solution.py:46
  9.2 4.0 %collective-permute-start.2 = (bf16[1024,256]{1,0:T(8,128)(2,1)}, bf16[1024,256]{1,0:T(8,128)(2,1)}, u32[]{:S(2)}, u32[]{:S(2)}) collective-permute-start(bf16[1024,256]{1,0:T(8,128)(2,1)} %get-tuple-element.76.rest_0_), channel_id=1, source_target_pairs={{0,48},{1,49},{2,50},{3,51},{4,52},{5,53},{6,54},{7,55},{8,56},{9,... | collective-permute-start | bytes 1572872 | tf_op jit(solution)/shard_map/ppermute | solution.py:46
  13.3 1.2 %copy-done.2 = bf16[256,2048]{1,0:T(8,128)(2,1)S(1)} copy-done((bf16[256,2048]{1,0:T(8,128)(2,1)S(1)}, bf16[256,2048]{1,0:T(8,128)(2,1)}, u32[]{:S(2)}) %copy-start.2) | copy-done | bytes 1048600
  14.5 1.5 %pack_weight.2 = bf16[256,1024]{1,0:T(8,128)(2,1)} custom-call(s32[3]{0:T(128)S(1)} %pad_add_fusion.spot_ref, bf16[256,2048]{1,0:T(8,128)(2,1)S(1)} %copy-done.2), custom_call_target="tpu_custom_call" | custom-call | flops 1024 | bytes 1024 | tf_op jit(solution)/shard_map/pack_weight/pallas_call | solution.py:217
  16.0 4.5 %collective-permute-done.3.rest_2_ = bf16[1024,256]{1,0:T(8,128)(2,1)} collective-permute-done((bf16[1024,256]{1,0:T(8,128)(2,1)}, bf16[1024,256]{1,0:T(8,128)(2,1)}, u32[]{:S(2)}, u32[]{:S(2)}) %collective-permute-start.3) | collective-permute-done | bytes 524320 | tf_op jit(solution)/shard_map/ppermute | solution.py:46
  20.5 4.0 %collective-permute-start.5 = (bf16[1024,256]{1,0:T(8,128)(2,1)}, bf16[1024,256]{1,0:T(8,128)(2,1)}, u32[]{:S(2)}, u32[]{:S(2)}) collective-permute-start(bf16[1024,256]{1,0:T(8,128)(2,1)} %collective-permute-done.3.rest_2_), channel_id=1, source_target_pairs={{0,48},{1,49},{2,50},{3,51},{4,52},{5,53},{6,54},{7,55},{8,56},{9,... | collective-permute-start | bytes 1572872 | tf_op jit(solution)/shard_map/ppermute | solution.py:46
  24.5 3.2 %collective-permute-start.8 = (bf16[256,1024]{1,0:T(8,128)(2,1)}, bf16[256,1024]{1,0:T(8,128)(2,1)}, u32[]{:S(2)}, u32[]{:S(2)}) collective-permute-start(bf16[256,1024]{1,0:T(8,128)(2,1)} %pack_weight.2), channel_id=1, source_target_pairs={{0,1},{1,0},{2,3},{3,2},{4,5},{5,4},{6,7},{7,6},{8,9},{9,8},{10,11... | collective-permute-start | bytes 1572872 | tf_op jit(solution)/shard_map/ppermute | solution.py:46
  27.7 1.8 %collective-permute-done.1.rest_12_ = bf16[1024,256]{1,0:T(8,128)(2,1)} collective-permute-done((bf16[1024,256]{1,0:T(8,128)(2,1)}, bf16[1024,256]{1,0:T(8,128)(2,1)}, u32[]{:S(2)}, u32[]{:S(2)}) %collective-permute-start.1) | collective-permute-done | bytes 524320 | tf_op jit(solution)/shard_map/ppermute | solution.py:46
  29.6 2.2 %copy-done.1 = bf16[1024,2048]{1,0:T(8,128)(2,1)S(1)} copy-done((bf16[1024,2048]{1,0:T(8,128)(2,1)S(1)}, bf16[1024,2048]{1,0:T(8,128)(2,1)}, u32[]{:S(2)}) %copy-start.1) | copy-done | bytes 4194328
  31.7 2.5 %project.3 = (bf16[1024,128]{1,0:T(8,128)(2,1)S(1)}, bf16[1024,128]{1,0:T(8,128)(2,1)S(1)}) custom-call(s32[1]{0:T(128)} %bitcast.half_ref, bf16[1024,2048]{1,0:T(8,128)(2,1)S(1)} %copy-done.1, f32[1,2048]{1,0:T(1,128)S(1)} %bitcast.7, bf16[3,2048,256]{2,1,0:T(8,128)(2,1)S(1)} %copy-done, bf16[3,2048,256]{2,1,0:T(8,128)(2,1)S(1)} %copy-done), custom_call_target="tpu_custom_call" | custom-call | flops 1024 | bytes 1024 | tf_op jit(solution)/shard_map/project/pallas_call | solution.py:81
  35.2 3.6 %collective-permute-done.8.refs_0_ = bf16[256,1024]{1,0:T(8,128)(2,1)} collective-permute-done((bf16[256,1024]{1,0:T(8,128)(2,1)}, bf16[256,1024]{1,0:T(8,128)(2,1)}, u32[]{:S(2)}, u32[]{:S(2)}) %collective-permute-start.8) | collective-permute-done | bytes 524320 | tf_op jit(solution)/shard_map/ppermute | solution.py:46
  40.6 1.3 %collective-permute-start.12 = (s32[16,128]{1,0:T(8,128)S(1)}, s32[16,128]{1,0:T(8,128)S(1)}, u32[]{:S(2)}, u32[]{:S(2)}) collective-permute-start(s32[16,128]{1,0:T(8,128)S(1)} %add_add_fusion), channel_id=1, source_target_pairs={{0,64},{1,65},{2,66},{3,67},{4,68},{5,69},{6,70},{7,71},{8,72},{9,... | collective-permute-start | bytes 24584 | tf_op jit(solution)/shard_map/ppermute | solution.py:46
  41.9 3.2 %collective-permute-start.10 = (bf16[1024,256]{1,0:T(8,128)(2,1)}, bf16[1024,256]{1,0:T(8,128)(2,1)S(1)}, u32[]{:S(2)}, u32[]{:S(2)}) collective-permute-start(bf16[1024,256]{1,0:T(8,128)(2,1)} %collective-permute-done.5.rest_6_), channel_id=1, source_target_pairs={{0,48},{1,49},{2,50},{3,51},{4,52},{5,53},{6,54},{7,55},{8,56},{9,... | collective-permute-start | bytes 1572872 | tf_op jit(solution)/shard_map/ppermute | solution.py:46
  45.0 2.4 %collective-permute-done.12 = s32[16,128]{1,0:T(8,128)S(1)} collective-permute-done((s32[16,128]{1,0:T(8,128)S(1)}, s32[16,128]{1,0:T(8,128)S(1)}, u32[]{:S(2)}, u32[]{:S(2)}) %collective-permute-start.12) | collective-permute-done | bytes 8224 | tf_op jit(solution)/shard_map/ppermute | solution.py:46
  47.9 6.0 %collective-permute-done.9.rest_8_ = bf16[1024,256]{1,0:T(8,128)(2,1)S(1)} collective-permute-done((bf16[1024,256]{1,0:T(8,128)(2,1)}, bf16[1024,256]{1,0:T(8,128)(2,1)S(1)}, u32[]{:S(2)}, u32[]{:S(2)}) %collective-permute-start.9) | collective-permute-done | bytes 524320 | tf_op jit(solution)/shard_map/ppermute | solution.py:46
  54.8 1.3 %collective-permute-done.16.rest_7_ = bf16[1024,256]{1,0:T(8,128)(2,1)S(1)} collective-permute-done((bf16[1024,256]{1,0:T(8,128)(2,1)}, bf16[1024,256]{1,0:T(8,128)(2,1)S(1)}, u32[]{:S(2)}, u32[]{:S(2)}) %collective-permute-start.16) | collective-permute-done | bytes 524320 | tf_op jit(solution)/shard_map/ppermute | solution.py:46
  56.6 1.4 %collective-permute-done.17.rest_9_ = bf16[1024,256]{1,0:T(8,128)(2,1)S(1)} collective-permute-done((bf16[1024,256]{1,0:T(8,128)(2,1)S(1)}, bf16[1024,256]{1,0:T(8,128)(2,1)S(1)}, u32[]{:S(2)}, u32[]{:S(2)}) %collective-permute-start.17) | collective-permute-done | bytes 524320 | tf_op jit(solution)/shard_map/ppermute | solution.py:46
  59.8 9.8 %attend.1 = (bf16[512,128]{1,0:T(8,128)(2,1)S(1)}, bf16[512,128]{1,0:T(8,128)(2,1)S(1)}, bf16[512,128]{1,0:T(8,128)(2,1)S(1)}, bf16[512,128]{1,0:T(8,128)(2,1)S(1)}) custom-call(s32[32,32]{1,0:T(8,128)S(1)} %get-tuple-element.81.list_ref, s32[32]{0:T(128)S(1)} %slice_reduce_fusion.count_ref, s32[32]{0:T(128)S(1)} %get-tuple-element.83.order_ref, ...), custom_call_target="tpu_custom_call" | custom-call | flops 2147483648 | bytes 10485760 | tf_op jit(solution)/shard_map/attend/pallas_call | solution.py:181
  69.6 2.7 %collective-permute-start.20 = (bf16[512,128]{1,0:T(8,128)(2,1)S(1)}, bf16[512,128]{1,0:T(8,128)(2,1)S(1)}, u32[]{:S(2)}, u32[]{:S(2)}) collective-permute-start(bf16[512,128]{1,0:T(8,128)(2,1)S(1)} %get-tuple-element.99.c0), channel_id=1, source_target_pairs={{0,1},{1,0},{2,3},{3,2},{4,5},{5,4},{6,7},{7,6},{8,9},{9,8},{10,11... | collective-permute-start | bytes 393224 | tf_op jit(solution)/shard_map/ppermute | solution.py:46
  73.1 3.8 %collective-permute-start.27 = (bf16[512,128]{1,0:T(8,128)(2,1)S(1)}, bf16[512,128]{1,0:T(8,128)(2,1)S(1)}, u32[]{:S(2)}, u32[]{:S(2)}) collective-permute-start(bf16[512,128]{1,0:T(8,128)(2,1)S(1)} %get-tuple-element.110.c0), channel_id=1, source_target_pairs={{0,1},{1,0},{2,3},{3,2},{4,5},{5,4},{6,7},{7,6},{8,9},{9,8},{10,11... | collective-permute-start | bytes 393224 | tf_op jit(solution)/shard_map/ppermute | solution.py:46
  78.1 1.6 %collective-permute-done.21.c3 = bf16[512,128]{1,0:T(8,128)(2,1)S(1)} collective-permute-done((bf16[512,128]{1,0:T(8,128)(2,1)S(1)}, bf16[512,128]{1,0:T(8,128)(2,1)S(1)}, u32[]{:S(2)}, u32[]{:S(2)}) %collective-permute-start.21) | collective-permute-done | bytes 131104 | tf_op jit(solution)/shard_map/ppermute | solution.py:46
  81.0 1.6 %collective-permute-start.23 = (bf16[256,256]{1,0:T(8,128)(2,1)S(1)}, bf16[256,256]{1,0:T(8,128)(2,1)S(1)}, u32[]{:S(2)}, u32[]{:S(2)}) collective-permute-start(bf16[256,256]{1,0:T(8,128)(2,1)S(1)} %get-tuple-element.107), channel_id=1, source_target_pairs={{0,6},{1,7},{2,0},{3,1},{4,2},{5,3},{6,4},{7,5},{8,14},{9,15},{10,... | collective-permute-start | bytes 393224 | tf_op jit(solution)/shard_map/ppermute | solution.py:46
  83.4 3.2 %collective-permute-done.28.c3 = bf16[512,128]{1,0:T(8,128)(2,1)S(1)} collective-permute-done((bf16[512,128]{1,0:T(8,128)(2,1)S(1)}, bf16[512,128]{1,0:T(8,128)(2,1)S(1)}, u32[]{:S(2)}, u32[]{:S(2)}) %collective-permute-start.28) | collective-permute-done | bytes 131104 | tf_op jit(solution)/shard_map/ppermute | solution.py:46
  87.9 1.5 %collective-permute-start.30 = (bf16[256,256]{1,0:T(8,128)(2,1)S(1)}, bf16[256,256]{1,0:T(8,128)(2,1)S(1)}, u32[]{:S(2)}, u32[]{:S(2)}) collective-permute-start(bf16[256,256]{1,0:T(8,128)(2,1)S(1)} %get-tuple-element.116), channel_id=1, source_target_pairs={{0,6},{1,7},{2,0},{3,1},{4,2},{5,3},{6,4},{7,5},{8,14},{9,15},{10,... | collective-permute-start | bytes 393224 | tf_op jit(solution)/shard_map/ppermute | solution.py:46
  89.5 1.8 %collective-permute-start.24 = (bf16[512,256]{1,0:T(8,128)(2,1)S(1)}, bf16[512,256]{1,0:T(8,128)(2,1)S(1)}, u32[]{:S(2)}, u32[]{:S(2)}) collective-permute-start(bf16[512,256]{1,0:T(8,128)(2,1)S(1)} %get-tuple-element.108), channel_id=1, source_target_pairs={{0,2},{1,3},{2,4},{3,5},{4,6},{5,7},{6,0},{7,1},{8,10},{9,11},{10,... | collective-permute-start | bytes 786440 | tf_op jit(solution)/shard_map/ppermute | solution.py:46
  91.6 2.1 %collective-permute-done.29.up_ref = bf16[256,256]{1,0:T(8,128)(2,1)S(1)} collective-permute-done((bf16[256,256]{1,0:T(8,128)(2,1)S(1)}, bf16[256,256]{1,0:T(8,128)(2,1)S(1)}, u32[]{:S(2)}, u32[]{:S(2)}) %collective-permute-start.29) | collective-permute-done | bytes 131104 | tf_op jit(solution)/shard_map/ppermute | solution.py:46
  94.5 1.2 %collective-permute-start.31 = (bf16[512,256]{1,0:T(8,128)(2,1)S(1)}, bf16[512,256]{1,0:T(8,128)(2,1)S(1)}, u32[]{:S(2)}, u32[]{:S(2)}) collective-permute-start(bf16[512,256]{1,0:T(8,128)(2,1)S(1)} %get-tuple-element.117), channel_id=1, source_target_pairs={{0,2},{1,3},{2,4},{3,5},{4,6},{5,7},{6,0},{7,1},{8,10},{9,11},{10,... | collective-permute-start | bytes 786440 | tf_op jit(solution)/shard_map/ppermute | solution.py:46
  96.6 2.7 %collective-permute-done.24.refs_1_ = bf16[512,256]{1,0:T(8,128)(2,1)S(1)} collective-permute-done((bf16[512,256]{1,0:T(8,128)(2,1)S(1)}, bf16[512,256]{1,0:T(8,128)(2,1)S(1)}, u32[]{:S(2)}, u32[]{:S(2)}) %collective-permute-start.24) | collective-permute-done | bytes 262176 | tf_op jit(solution)/shard_map/ppermute | solution.py:46
  99.3 2.4 %collective-permute-done.25.refs_2_ = bf16[512,256]{1,0:T(8,128)(2,1)S(1)} collective-permute-done((bf16[512,256]{1,0:T(8,128)(2,1)S(1)}, bf16[512,256]{1,0:T(8,128)(2,1)S(1)}, u32[]{:S(2)}, u32[]{:S(2)}) %collective-permute-start.25) | collective-permute-done | bytes 262176 | tf_op jit(solution)/shard_map/ppermute | solution.py:46
  101.7 2.6 %collective-permute-done.31.refs_4_ = bf16[512,256]{1,0:T(8,128)(2,1)S(1)} collective-permute-done((bf16[512,256]{1,0:T(8,128)(2,1)S(1)}, bf16[512,256]{1,0:T(8,128)(2,1)S(1)}, u32[]{:S(2)}, u32[]{:S(2)}) %collective-permute-start.31) | collective-permute-done | bytes 262176 | tf_op jit(solution)/shard_map/ppermute | solution.py:46
  104.2 1.4 %collective-permute-done.32.refs_5_ = bf16[512,256]{1,0:T(8,128)(2,1)S(1)} collective-permute-done((bf16[512,256]{1,0:T(8,128)(2,1)S(1)}, bf16[512,256]{1,0:T(8,128)(2,1)S(1)}, u32[]{:S(2)}, u32[]{:S(2)}) %collective-permute-start.32) | collective-permute-done | bytes 262176 | tf_op jit(solution)/shard_map/ppermute | solution.py:46
  (73 shorter events, 16.1 us)
Async XLA Ops:
  6.5 14.0 %collective-permute-start.3 = (bf16[1024,256]{1,0:T(8,128)(2,1)}, bf16[1024,256]{1,0:T(8,128)(2,1)}, u32[]{:S(2)}, u32[]{:S(2)}) collective-permute-start(bf16[1024,256]{1,0:T(8,128)(2,1)} %get-tuple-element.63), channel_id=1, source_target_pairs={{0,64},{1,65},{2,66},{3,67},{4,68},{5,69},{6,70},{7,71},{8,72},{9,... | collective-permute-start | bytes 1572872 | tf_op jit(solution)/shard_map/ppermute | solution.py:46
  9.2 18.5 %collective-permute-start.2 = (bf16[1024,256]{1,0:T(8,128)(2,1)}, bf16[1024,256]{1,0:T(8,128)(2,1)}, u32[]{:S(2)}, u32[]{:S(2)}) collective-permute-start(bf16[1024,256]{1,0:T(8,128)(2,1)} %get-tuple-element.76.rest_0_), channel_id=1, source_target_pairs={{0,48},{1,49},{2,50},{3,51},{4,52},{5,53},{6,54},{7,55},{8,56},{9,... | collective-permute-start | bytes 1572872 | tf_op jit(solution)/shard_map/ppermute | solution.py:46
  13.2 16.3 %collective-permute-start.1 = (bf16[1024,256]{1,0:T(8,128)(2,1)}, bf16[1024,256]{1,0:T(8,128)(2,1)}, u32[]{:S(2)}, u32[]{:S(2)}) collective-permute-start(bf16[1024,256]{1,0:T(8,128)(2,1)} %get-tuple-element.76.rest_0_), channel_id=1, source_target_pairs={{0,16},{1,17},{2,18},{3,19},{4,20},{5,21},{6,22},{7,23},{8,24},{9,... | collective-permute-start | bytes 1572872 | tf_op jit(solution)/shard_map/ppermute | solution.py:46
  20.5 18.4 %collective-permute-start.5 = (bf16[1024,256]{1,0:T(8,128)(2,1)}, bf16[1024,256]{1,0:T(8,128)(2,1)}, u32[]{:S(2)}, u32[]{:S(2)}) collective-permute-start(bf16[1024,256]{1,0:T(8,128)(2,1)} %collective-permute-done.3.rest_2_), channel_id=1, source_target_pairs={{0,48},{1,49},{2,50},{3,51},{4,52},{5,53},{6,54},{7,55},{8,56},{9,... | collective-permute-start | bytes 1572872 | tf_op jit(solution)/shard_map/ppermute | solution.py:46
  24.5 15.2 %collective-permute-start.4 = (bf16[1024,256]{1,0:T(8,128)(2,1)}, bf16[1024,256]{1,0:T(8,128)(2,1)}, u32[]{:S(2)}, u32[]{:S(2)}) collective-permute-start(bf16[1024,256]{1,0:T(8,128)(2,1)} %collective-permute-done.3.rest_2_), channel_id=1, source_target_pairs={{0,16},{1,17},{2,18},{3,19},{4,20},{5,21},{6,22},{7,23},{8,24},{9,... | collective-permute-start | bytes 1572872 | tf_op jit(solution)/shard_map/ppermute | solution.py:46
  24.5 14.3 %collective-permute-start.8 = (bf16[256,1024]{1,0:T(8,128)(2,1)}, bf16[256,1024]{1,0:T(8,128)(2,1)}, u32[]{:S(2)}, u32[]{:S(2)}) collective-permute-start(bf16[256,1024]{1,0:T(8,128)(2,1)} %pack_weight.2), channel_id=1, source_target_pairs={{0,1},{1,0},{2,3},{3,2},{4,5},{5,4},{6,7},{7,6},{8,9},{9,8},{10,11... | collective-permute-start | bytes 1572872 | tf_op jit(solution)/shard_map/ppermute | solution.py:46
  27.7 12.0 %collective-permute-start.7 = (bf16[1024,256]{1,0:T(8,128)(2,1)}, bf16[1024,256]{1,0:T(8,128)(2,1)}, u32[]{:S(2)}, u32[]{:S(2)}) collective-permute-start(bf16[1024,256]{1,0:T(8,128)(2,1)} %collective-permute-done.2.rest_4_), channel_id=1, source_target_pairs={{0,8},{1,9},{2,10},{3,11},{4,12},{5,13},{6,14},{7,15},{8,0},{9,1},... | collective-permute-start | bytes 1572872 | tf_op jit(solution)/shard_map/ppermute | solution.py:46
  29.5 10.2 %collective-permute-start.6 = (bf16[1024,256]{1,0:T(8,128)(2,1)}, bf16[1024,256]{1,0:T(8,128)(2,1)}, u32[]{:S(2)}, u32[]{:S(2)}) collective-permute-start(bf16[1024,256]{1,0:T(8,128)(2,1)} %collective-permute-done.1.rest_12_), channel_id=1, source_target_pairs={{0,8},{1,9},{2,10},{3,11},{4,12},{5,13},{6,14},{7,15},{8,0},{9,1},... | collective-permute-start | bytes 1572872 | tf_op jit(solution)/shard_map/ppermute | solution.py:46
  39.7 14.2 %collective-permute-start.9 = (bf16[1024,256]{1,0:T(8,128)(2,1)}, bf16[1024,256]{1,0:T(8,128)(2,1)S(1)}, u32[]{:S(2)}, u32[]{:S(2)}) collective-permute-start(bf16[1024,256]{1,0:T(8,128)(2,1)} %collective-permute-done.1.rest_12_), channel_id=1, source_target_pairs={{0,16},{1,17},{2,18},{3,19},{4,20},{5,21},{6,22},{7,23},{8,24},{9,... | collective-permute-start | bytes 1572872 | tf_op jit(solution)/shard_map/ppermute | solution.py:46
  39.7 7.6 %collective-permute-start.11 = (bf16[1024,128]{1,0:T(8,128)(2,1)}, bf16[1024,128]{1,0:T(8,128)(2,1)S(1)}, u32[]{:S(2)}, u32[]{:S(2)}) collective-permute-start(bf16[1024,128]{1,0:T(8,128)(2,1)} %copy-done.6), channel_id=1, source_target_pairs={{0,64},{1,65},{2,66},{3,67},{4,68},{5,69},{6,70},{7,71},{8,72},{9,... | collective-permute-start | bytes 786440 | tf_op jit(solution)/shard_map/ppermute | solution.py:46
  40.6 6.8 %collective-permute-start.12 = (s32[16,128]{1,0:T(8,128)S(1)}, s32[16,128]{1,0:T(8,128)S(1)}, u32[]{:S(2)}, u32[]{:S(2)}) collective-permute-start(s32[16,128]{1,0:T(8,128)S(1)} %add_add_fusion), channel_id=1, source_target_pairs={{0,64},{1,65},{2,66},{3,67},{4,68},{5,69},{6,70},{7,71},{8,72},{9,... | collective-permute-start | bytes 24584 | tf_op jit(solution)/shard_map/ppermute | solution.py:46
  41.9 12.9 %collective-permute-start.10 = (bf16[1024,256]{1,0:T(8,128)(2,1)}, bf16[1024,256]{1,0:T(8,128)(2,1)S(1)}, u32[]{:S(2)}, u32[]{:S(2)}) collective-permute-start(bf16[1024,256]{1,0:T(8,128)(2,1)} %collective-permute-done.5.rest_6_), channel_id=1, source_target_pairs={{0,48},{1,49},{2,50},{3,51},{4,52},{5,53},{6,54},{7,55},{8,56},{9,... | collective-permute-start | bytes 1572872 | tf_op jit(solution)/shard_map/ppermute | solution.py:46
  47.4 7.4 %collective-permute-start.13 = (bf16[1024,256]{1,0:T(8,128)(2,1)}, bf16[1024,256]{1,0:T(8,128)(2,1)S(1)}, u32[]{:S(2)}, u32[]{:S(2)}) collective-permute-start(bf16[1024,256]{1,0:T(8,128)(2,1)} %get-tuple-element.76.rest_0_), channel_id=1, source_target_pairs={{0,8},{1,9},{2,10},{3,11},{4,12},{5,13},{6,14},{7,15},{8,0},{9,1},... | collective-permute-start | bytes 1572872 | tf_op jit(solution)/shard_map/ppermute | solution.py:46
  47.4 7.4 %collective-permute-start.14 = (bf16[1024,256]{1,0:T(8,128)(2,1)}, bf16[1024,256]{1,0:T(8,128)(2,1)S(1)}, u32[]{:S(2)}, u32[]{:S(2)}) collective-permute-start(bf16[1024,256]{1,0:T(8,128)(2,1)} %collective-permute-done.3.rest_2_), channel_id=1, source_target_pairs={{0,8},{1,9},{2,10},{3,11},{4,12},{5,13},{6,14},{7,15},{8,0},{9,1},... | collective-permute-start | bytes 1572872 | tf_op jit(solution)/shard_map/ppermute | solution.py:46
  47.9 6.9 %collective-permute-start.15 = (bf16[1024,256]{1,0:T(8,128)(2,1)}, bf16[1024,256]{1,0:T(8,128)(2,1)S(1)}, u32[]{:S(2)}, u32[]{:S(2)}) collective-permute-start(bf16[1024,256]{1,0:T(8,128)(2,1)} %collective-permute-done.4.rest_14_), channel_id=1, source_target_pairs={{0,8},{1,9},{2,10},{3,11},{4,12},{5,13},{6,14},{7,15},{8,0},{9,1},... | collective-permute-start | bytes 1572872 | tf_op jit(solution)/shard_map/ppermute | solution.py:46
  54.0 2.1 %collective-permute-start.16 = (bf16[1024,256]{1,0:T(8,128)(2,1)}, bf16[1024,256]{1,0:T(8,128)(2,1)S(1)}, u32[]{:S(2)}, u32[]{:S(2)}) collective-permute-start(bf16[1024,256]{1,0:T(8,128)(2,1)} %collective-permute-done.5.rest_6_), channel_id=1, source_target_pairs={{0,8},{1,9},{2,10},{3,11},{4,12},{5,13},{6,14},{7,15},{8,0},{9,1},... | collective-permute-start | bytes 1572872 | tf_op jit(solution)/shard_map/ppermute | solution.py:46
  56.1 1.9 %collective-permute-start.17 = (bf16[1024,256]{1,0:T(8,128)(2,1)S(1)}, bf16[1024,256]{1,0:T(8,128)(2,1)S(1)}, u32[]{:S(2)}, u32[]{:S(2)}) collective-permute-start(bf16[1024,256]{1,0:T(8,128)(2,1)S(1)} %collective-permute-done.9.rest_8_), channel_id=1, source_target_pairs={{0,8},{1,9},{2,10},{3,11},{4,12},{5,13},{6,14},{7,15},{8,0},{9,1},... | collective-permute-start | bytes 1572872 | tf_op jit(solution)/shard_map/ppermute | solution.py:46
  56.2 2.5 %collective-permute-start.18 = (bf16[1024,256]{1,0:T(8,128)(2,1)S(1)}, bf16[1024,256]{1,0:T(8,128)(2,1)S(1)}, u32[]{:S(2)}, u32[]{:S(2)}) collective-permute-start(bf16[1024,256]{1,0:T(8,128)(2,1)S(1)} %collective-permute-done.10.rest_10_), channel_id=1, source_target_pairs={{0,8},{1,9},{2,10},{3,11},{4,12},{5,13},{6,14},{7,15},{8,0},{9,1},... | collective-permute-start | bytes 1572872 | tf_op jit(solution)/shard_map/ppermute | solution.py:46
  69.6 7.4 %collective-permute-start.20 = (bf16[512,128]{1,0:T(8,128)(2,1)S(1)}, bf16[512,128]{1,0:T(8,128)(2,1)S(1)}, u32[]{:S(2)}, u32[]{:S(2)}) collective-permute-start(bf16[512,128]{1,0:T(8,128)(2,1)S(1)} %get-tuple-element.99.c0), channel_id=1, source_target_pairs={{0,1},{1,0},{2,3},{3,2},{4,5},{5,4},{6,7},{7,6},{8,9},{9,8},{10,11... | collective-permute-start | bytes 393224 | tf_op jit(solution)/shard_map/ppermute | solution.py:46
  72.2 7.5 %collective-permute-start.21 = (bf16[512,128]{1,0:T(8,128)(2,1)S(1)}, bf16[512,128]{1,0:T(8,128)(2,1)S(1)}, u32[]{:S(2)}, u32[]{:S(2)}) collective-permute-start(bf16[512,128]{1,0:T(8,128)(2,1)S(1)} %get-tuple-element.100), channel_id=1, source_target_pairs={{0,65},{1,64},{2,67},{3,66},{4,69},{5,68},{6,71},{7,70},{8,73},{9,... | collective-permute-start | bytes 393224 | tf_op jit(solution)/shard_map/ppermute | solution.py:46
  72.2 7.5 %collective-permute-start.19 = (bf16[512,128]{1,0:T(8,128)(2,1)S(1)}, bf16[512,128]{1,0:T(8,128)(2,1)S(1)}, u32[]{:S(2)}, u32[]{:S(2)}) collective-permute-start(bf16[512,128]{1,0:T(8,128)(2,1)S(1)} %get-tuple-element.100), channel_id=1, source_target_pairs={{0,64},{1,65},{2,66},{3,67},{4,68},{5,69},{6,70},{7,71},{8,72},{9,... | collective-permute-start | bytes 393224 | tf_op jit(solution)/shard_map/ppermute | solution.py:46
  73.1 10.3 %collective-permute-start.27 = (bf16[512,128]{1,0:T(8,128)(2,1)S(1)}, bf16[512,128]{1,0:T(8,128)(2,1)S(1)}, u32[]{:S(2)}, u32[]{:S(2)}) collective-permute-start(bf16[512,128]{1,0:T(8,128)(2,1)S(1)} %get-tuple-element.110.c0), channel_id=1, source_target_pairs={{0,1},{1,0},{2,3},{3,2},{4,5},{5,4},{6,7},{7,6},{8,9},{9,8},{10,11... | collective-permute-start | bytes 393224 | tf_op jit(solution)/shard_map/ppermute | solution.py:46
  76.9 9.7 %collective-permute-start.28 = (bf16[512,128]{1,0:T(8,128)(2,1)S(1)}, bf16[512,128]{1,0:T(8,128)(2,1)S(1)}, u32[]{:S(2)}, u32[]{:S(2)}) collective-permute-start(bf16[512,128]{1,0:T(8,128)(2,1)S(1)} %get-tuple-element.111), channel_id=1, source_target_pairs={{0,65},{1,64},{2,67},{3,66},{4,69},{5,68},{6,71},{7,70},{8,73},{9,... | collective-permute-start | bytes 393224 | tf_op jit(solution)/shard_map/ppermute | solution.py:46
  76.9 9.6 %collective-permute-start.26 = (bf16[512,128]{1,0:T(8,128)(2,1)S(1)}, bf16[512,128]{1,0:T(8,128)(2,1)S(1)}, u32[]{:S(2)}, u32[]{:S(2)}) collective-permute-start(bf16[512,128]{1,0:T(8,128)(2,1)S(1)} %get-tuple-element.111), channel_id=1, source_target_pairs={{0,64},{1,65},{2,66},{3,67},{4,68},{5,69},{6,70},{7,71},{8,72},{9,... | collective-permute-start | bytes 393224 | tf_op jit(solution)/shard_map/ppermute | solution.py:46
  80.4 8.9 %collective-permute-start.22 = (bf16[256,256]{1,0:T(8,128)(2,1)S(1)}, bf16[256,256]{1,0:T(8,128)(2,1)S(1)}, u32[]{:S(2)}, u32[]{:S(2)}) collective-permute-start(bf16[256,256]{1,0:T(8,128)(2,1)S(1)} %get-tuple-element.106), channel_id=1, source_target_pairs={{0,2},{1,3},{2,4},{3,5},{4,6},{5,7},{6,0},{7,1},{8,10},{9,11},{10,... | collective-permute-start | bytes 393224 | tf_op jit(solution)/shard_map/ppermute | solution.py:46
  81.0 8.4 %collective-permute-start.23 = (bf16[256,256]{1,0:T(8,128)(2,1)S(1)}, bf16[256,256]{1,0:T(8,128)(2,1)S(1)}, u32[]{:S(2)}, u32[]{:S(2)}) collective-permute-start(bf16[256,256]{1,0:T(8,128)(2,1)S(1)} %get-tuple-element.107), channel_id=1, source_target_pairs={{0,6},{1,7},{2,0},{3,1},{4,2},{5,3},{6,4},{7,5},{8,14},{9,15},{10,... | collective-permute-start | bytes 393224 | tf_op jit(solution)/shard_map/ppermute | solution.py:46
  87.3 6.4 %collective-permute-start.29 = (bf16[256,256]{1,0:T(8,128)(2,1)S(1)}, bf16[256,256]{1,0:T(8,128)(2,1)S(1)}, u32[]{:S(2)}, u32[]{:S(2)}) collective-permute-start(bf16[256,256]{1,0:T(8,128)(2,1)S(1)} %get-tuple-element.115), channel_id=1, source_target_pairs={{0,2},{1,3},{2,4},{3,5},{4,6},{5,7},{6,0},{7,1},{8,10},{9,11},{10,... | collective-permute-start | bytes 393224 | tf_op jit(solution)/shard_map/ppermute | solution.py:46
  87.9 6.6 %collective-permute-start.30 = (bf16[256,256]{1,0:T(8,128)(2,1)S(1)}, bf16[256,256]{1,0:T(8,128)(2,1)S(1)}, u32[]{:S(2)}, u32[]{:S(2)}) collective-permute-start(bf16[256,256]{1,0:T(8,128)(2,1)S(1)} %get-tuple-element.116), channel_id=1, source_target_pairs={{0,6},{1,7},{2,0},{3,1},{4,2},{5,3},{6,4},{7,5},{8,14},{9,15},{10,... | collective-permute-start | bytes 393224 | tf_op jit(solution)/shard_map/ppermute | solution.py:46
  89.5 9.8 %collective-permute-start.24 = (bf16[512,256]{1,0:T(8,128)(2,1)S(1)}, bf16[512,256]{1,0:T(8,128)(2,1)S(1)}, u32[]{:S(2)}, u32[]{:S(2)}) collective-permute-start(bf16[512,256]{1,0:T(8,128)(2,1)S(1)} %get-tuple-element.108), channel_id=1, source_target_pairs={{0,2},{1,3},{2,4},{3,5},{4,6},{5,7},{6,0},{7,1},{8,10},{9,11},{10,... | collective-permute-start | bytes 786440 | tf_op jit(solution)/shard_map/ppermute | solution.py:46
  91.2 10.5 %collective-permute-start.25 = (bf16[512,256]{1,0:T(8,128)(2,1)S(1)}, bf16[512,256]{1,0:T(8,128)(2,1)S(1)}, u32[]{:S(2)}, u32[]{:S(2)}) collective-permute-start(bf16[512,256]{1,0:T(8,128)(2,1)S(1)} %get-tuple-element.109), channel_id=1, source_target_pairs={{0,6},{1,7},{2,0},{3,1},{4,2},{5,3},{6,4},{7,5},{8,14},{9,15},{10,... | collective-permute-start | bytes 786440 | tf_op jit(solution)/shard_map/ppermute | solution.py:46
  94.5 9.7 %collective-permute-start.31 = (bf16[512,256]{1,0:T(8,128)(2,1)S(1)}, bf16[512,256]{1,0:T(8,128)(2,1)S(1)}, u32[]{:S(2)}, u32[]{:S(2)}) collective-permute-start(bf16[512,256]{1,0:T(8,128)(2,1)S(1)} %get-tuple-element.117), channel_id=1, source_target_pairs={{0,2},{1,3},{2,4},{3,5},{4,6},{5,7},{6,0},{7,1},{8,10},{9,11},{10,... | collective-permute-start | bytes 786440 | tf_op jit(solution)/shard_map/ppermute | solution.py:46
  95.7 10.0 %collective-permute-start.32 = (bf16[512,256]{1,0:T(8,128)(2,1)S(1)}, bf16[512,256]{1,0:T(8,128)(2,1)S(1)}, u32[]{:S(2)}, u32[]{:S(2)}) collective-permute-start(bf16[512,256]{1,0:T(8,128)(2,1)S(1)} %get-tuple-element.118), channel_id=1, source_target_pairs={{0,6},{1,7},{2,0},{3,1},{4,2},{5,3},{6,4},{7,5},{8,14},{9,15},{10,... | collective-permute-start | bytes 786440 | tf_op jit(solution)/shard_map/ppermute | solution.py:46
  (10 other events, 111.2 us)

commit v6 on v5

--- a/solution.py
+++ b/solution.py
@@ -150,7 +150,7 @@
     for copy in copies:
         copy.start()
     q_ref[:rows, :] = qm_ref[...]
-    q_ref[rows:, :] = qp_ref[...]
+    q_ref[rows:, :] = qp_ref[:rows, :]
     for copy in copies:
         copy.wait()
     tiles = q_ref.shape[0] // TILE
@@ -340,7 +340,7 @@
     kvp = move(kvo, dyl=1)
     first, kvo = barrier((selected_count, kvo))
     kvm, first = barrier((kvm, move(first, dc=1)))
-    up_m, down_m = move(kvm, dz=1), move(kvm, dz=-1)
+    up_m, down_m, core_m = move(kvm, dz=1), move(kvm, dz=-1), move(kvm, dc=1)
     kvp, sent_weight, first = barrier((kvp, sent_weight, first))
     up_p, down_p = move(kvp, dz=1), move(kvp, dz=-1)
     other_weight = move(sent_weight, dyh=1)
@@ -349,18 +349,20 @@
     packed = jnp.concatenate(
         [selected_tiles, counts[:, None], jnp.zeros((rows_here, 95), jnp.int32)], axis=1
     )
-    up_m, down_m, up_p, down_p, qo, packed, core_up_m, core_down_m, other_weight = barrier(
-        (up_m, down_m, up_p, down_p, qo, packed, core_up_m, core_down_m, other_weight)
+    sent_queries = jnp.concatenate([qo, packed.astype(jnp.bfloat16)], axis=0)
+    up_m, down_m, up_p, down_p, sent_queries, core_m, core_up_m, core_down_m, other_weight = barrier(
+        (up_m, down_m, up_p, down_p, sent_queries, core_m, core_up_m, core_down_m, other_weight)
     )
     far_m, far_p = move(up_m, dz=1), move(down_p, dz=-1)
-    qp, packed_p = move(qo, dyl=1), move(packed, dyl=1)
-    qp, packed_p, up_p, down_p, own_m, own_p = barrier((qp, packed_p, up_p, down_p, kvm, kvp))
-    core_m, core_p = move(own_m, dc=1), move(own_p, dc=1)
+    qp = move(sent_queries, dyl=1)
+    qp, up_p, down_p, own_p = barrier((qp, up_p, down_p, kvp))
+    packed_p = qp[qo.shape[0] :].astype(jnp.int32)
+    core_p = move(own_p, dc=1)
     core_up_p, core_down_p = move(up_p, dc=1), move(down_p, dc=1)
     packed = jnp.concatenate([packed, packed_p], axis=0)
     lists, counts, order = place_lists(packed[:, :SEL], packed[:, SEL], yl, z, core)
-    far_m, far_p, core_m, core_p, core_up_p, core_down_p, lists, counts, order = barrier(
-        (far_m, far_p, core_m, core_p, core_up_p, core_down_p, lists, counts, order)
+    far_m, far_p, core_p, core_up_p, core_down_p, lists, counts, order = barrier(
+        (far_m, far_p, core_p, core_up_p, core_down_p, lists, counts, order)
     )
     core_far_m, core_far_p = move(far_m, dc=1), move(far_p, dc=1)
     parts = attend(

time: 107 us -> 103 us (0.963)
  waiting for transfers between devices: 41.8 us -> 38.9 us
  other arithmetic: 0.49 us -> 2.25 us
  local copies, waits for them, and re-layouts: 5.52 us -> 4.39 us
  Pallas kernels: 23.8 us -> 22.7 us
    ppermute x33 -> x32, waiting for transfers between devices: 41.8 us -> 38.9 us  [move(): return lax.ppermute(array, AXES, pairs)]
    concatenate x1 -> x2, other arithmetic: 0.08 us -> 1.75 us  [the longest x1 1.67 us: per_device(): sent_queries = jnp.concatenate([qo, packed.astype(jnp.bfloat16)], axis=0)]
    pallas_call x1, Pallas kernels: 9.77 us -> 8.66 us  [attend(): pl.pallas_call(attend_kernel, out_shape=[part] * (2 * CHUNKS), in_specs=[...]
    unnamed x19 -> x18, local copies, waits for them, and re-layouts: 5.17 us -> 4.12 us
    ppermute x33 -> x32, starting transfers between devices: 34.9 us -> 34.5 us  [move(): return lax.ppermute(array, AXES, pairs)]
  transfers between devices with their start and end apart: 33 -> 32, of which waited for: 20 -> 17; matrix products, arithmetic and copies ran while one was open for 1% -> 2% of each run, Pallas kernels for 6% -> 6%
where the time goes in v6:
time: 103 us
  waiting for transfers between devices  38.9 us (38%)
  starting transfers between devices  34.5 us (33%)
  Pallas kernels  22.7 us (22%)
  local copies, waits for them, and re-layouts  4.39 us (4%)
  other arithmetic  2.25 us (2%)
    ppermute x32, waiting for transfers between devices, move(): return lax.ppermute(array, AXES, pairs)  38.9 us
    ppermute x32, starting transfers between devices, move(): return lax.ppermute(array, AXES, pairs)  34.5 us
    pallas_call x2, Pallas kernels, project(): pl.pallas_call(kernel, grid_spec=pltpu.PrefetchScalarGridSpec(num_scalar_...  8.97 us
    pallas_call x1, Pallas kernels, attend(): pl.pallas_call(attend_kernel, out_shape=[part] * (2 * CHUNKS), in_specs=[...  8.66 us
    unnamed x18, local copies, waits for them, and re-layouts  4.12 us
    pallas_call x2, Pallas kernels, pack_weight(): pl.pallas_call(kernel, in_specs=[SM] + [VM] * (1 + len(extra)), out_specs...  2.57 us
  transfers between devices with their start and end apart: 32, of which 17 were waited for; matrix products, arithmetic and copies ran while one was open for 2% of the time, Pallas kernels for 6%

profile of v6, /device:TPU:6, one launch (start us, length us, event | category | flops | bytes accessed | tf_op | source)
XLA Modules:
  0.0 102.9 jit_solution(6743223673329353372)
XLA Ops:
  0.0 6.5 %project.2 = (bf16[1024,256]{1,0:T(8,128)(2,1)}, bf16[1024,256]{1,0:T(8,128)(2,1)}) custom-call(s32[1]{0:T(128)} %bitcast.half_ref, bf16[1024,2048]{1,0:T(8,128)(2,1)} %h_ref.3, f32[1,2048]{1,0:T(1,128)} %bitcast.6, bf16[3,2048,256]{2,1,0:T(8,128)(2,1)} %qo.1, bf16[3,2048,256]{2,1,0:T(8,128)(2,1)} %qo.1, bf16[3,2048,256]{2,1,0:T(8,128)(2,1)} %qo.1, ...), custom_call_target="tpu_custom_call" | custom-call | flops 1024 | bytes 1024 | tf_op jit(solution)/shard_map/project/pallas_call | solution.py:81
  6.5 1.6 %collective-permute-start.3 = (bf16[1024,256]{1,0:T(8,128)(2,1)}, bf16[1024,256]{1,0:T(8,128)(2,1)}, u32[]{:S(2)}, u32[]{:S(2)}) collective-permute-start(bf16[1024,256]{1,0:T(8,128)(2,1)} %get-tuple-element.60), channel_id=1, source_target_pairs={{0,64},{1,65},{2,66},{3,67},{4,68},{5,69},{6,70},{7,71},{8,72},{9,... | collective-permute-start | bytes 1572872 | tf_op jit(solution)/shard_map/ppermute | solution.py:46
  9.4 4.0 %collective-permute-start.2 = (bf16[1024,256]{1,0:T(8,128)(2,1)}, bf16[1024,256]{1,0:T(8,128)(2,1)}, u32[]{:S(2)}, u32[]{:S(2)}) collective-permute-start(bf16[1024,256]{1,0:T(8,128)(2,1)} %get-tuple-element.62.rest_0_), channel_id=1, source_target_pairs={{0,48},{1,49},{2,50},{3,51},{4,52},{5,53},{6,54},{7,55},{8,56},{9,... | collective-permute-start | bytes 1572872 | tf_op jit(solution)/shard_map/ppermute | solution.py:46
  13.5 2.2 %copy-done.1 = bf16[1024,2048]{1,0:T(8,128)(2,1)S(1)} copy-done((bf16[1024,2048]{1,0:T(8,128)(2,1)S(1)}, bf16[1024,2048]{1,0:T(8,128)(2,1)}, u32[]{:S(2)}) %copy-start.1) | copy-done | bytes 4194328
  15.6 2.5 %project.3 = (bf16[1024,128]{1,0:T(8,128)(2,1)S(1)}, bf16[1024,128]{1,0:T(8,128)(2,1)S(1)}) custom-call(s32[1]{0:T(128)} %bitcast.half_ref, bf16[1024,2048]{1,0:T(8,128)(2,1)S(1)} %copy-done.1, f32[1,2048]{1,0:T(1,128)S(1)} %bitcast.7, bf16[3,2048,256]{2,1,0:T(8,128)(2,1)S(1)} %copy-done, bf16[3,2048,256]{2,1,0:T(8,128)(2,1)S(1)} %copy-done), custom_call_target="tpu_custom_call" | custom-call | flops 1024 | bytes 1024 | tf_op jit(solution)/shard_map/project/pallas_call | solution.py:81
  18.9 1.2 %copy-done.2 = bf16[256,2048]{1,0:T(8,128)(2,1)S(1)} copy-done((bf16[256,2048]{1,0:T(8,128)(2,1)S(1)}, bf16[256,2048]{1,0:T(8,128)(2,1)}, u32[]{:S(2)}) %copy-start.2) | copy-done | bytes 1048600
  20.2 1.4 %pack_weight.2 = bf16[256,1024]{1,0:T(8,128)(2,1)} custom-call(s32[3]{0:T(128)S(1)} %pad_add_fusion.1.spot_ref, bf16[256,2048]{1,0:T(8,128)(2,1)S(1)} %copy-done.2), custom_call_target="tpu_custom_call" | custom-call | flops 1024 | bytes 1024 | tf_op jit(solution)/shard_map/pack_weight/pallas_call | solution.py:217
  21.6 3.2 %collective-permute-start.5 = (bf16[1024,256]{1,0:T(8,128)(2,1)}, bf16[1024,256]{1,0:T(8,128)(2,1)S(1)}, u32[]{:S(2)}, u32[]{:S(2)}) collective-permute-start(bf16[1024,256]{1,0:T(8,128)(2,1)} %collective-permute-done.3.rest_2_), channel_id=1, source_target_pairs={{0,48},{1,49},{2,50},{3,51},{4,52},{5,53},{6,54},{7,55},{8,56},{9,... | collective-permute-start | bytes 1572872 | tf_op jit(solution)/shard_map/ppermute | solution.py:46
  24.8 2.9 %collective-permute-start.9 = (bf16[256,1024]{1,0:T(8,128)(2,1)}, bf16[256,1024]{1,0:T(8,128)(2,1)}, u32[]{:S(2)}, u32[]{:S(2)}) collective-permute-start(bf16[256,1024]{1,0:T(8,128)(2,1)} %pack_weight.2), channel_id=1, source_target_pairs={{0,1},{1,0},{2,3},{3,2},{4,5},{5,4},{6,7},{7,6},{8,9},{9,8},{10,11... | collective-permute-start | bytes 1572872 | tf_op jit(solution)/shard_map/ppermute | solution.py:46
  27.7 1.5 %collective-permute-done.1.rest_12_ = bf16[1024,256]{1,0:T(8,128)(2,1)} collective-permute-done((bf16[1024,256]{1,0:T(8,128)(2,1)}, bf16[1024,256]{1,0:T(8,128)(2,1)}, u32[]{:S(2)}, u32[]{:S(2)}) %collective-permute-start.1) | collective-permute-done | bytes 524320 | tf_op jit(solution)/shard_map/ppermute | solution.py:46
  29.3 1.7 %pad_maximum_fusion = bf16[1040,128]{1,0:T(8,128)(2,1)} fusion(bf16[16,128]{1,0:T(8,128)(2,1)S(1)} %add_convert_fusion, bf16[1024,128]{1,0:T(8,128)(2,1)} %copy-done.5), kind=kLoop, calls=%fused_computation | loop fusion | flops 532480 | bytes 532480 | tf_op jit(solution)/shard_map/concatenate | solution.py:352
  31.0 8.9 %collective-permute-done.9.refs_0_ = bf16[256,1024]{1,0:T(8,128)(2,1)} collective-permute-done((bf16[256,1024]{1,0:T(8,128)(2,1)}, bf16[256,1024]{1,0:T(8,128)(2,1)}, u32[]{:S(2)}, u32[]{:S(2)}) %collective-permute-start.9) | collective-permute-done | bytes 524320 | tf_op jit(solution)/shard_map/ppermute | solution.py:46
  40.5 3.2 %collective-permute-start.11 = (bf16[1024,256]{1,0:T(8,128)(2,1)S(1)}, bf16[1024,256]{1,0:T(8,128)(2,1)S(1)}, u32[]{:S(2)}, u32[]{:S(2)}) collective-permute-start(bf16[1024,256]{1,0:T(8,128)(2,1)S(1)} %collective-permute-done.5.rest_6_), channel_id=1, source_target_pairs={{0,48},{1,49},{2,50},{3,51},{4,52},{5,53},{6,54},{7,55},{8,56},{9,... | collective-permute-start | bytes 1572872 | tf_op jit(solution)/shard_map/ppermute | solution.py:46
  43.7 3.8 %collective-permute-done.12.qp_ref = bf16[1040,128]{1,0:T(8,128)(2,1)S(1)} collective-permute-done((bf16[1040,128]{1,0:T(8,128)(2,1)}, bf16[1040,128]{1,0:T(8,128)(2,1)S(1)}, u32[]{:S(2)}, u32[]{:S(2)}) %collective-permute-start.12) | collective-permute-done | bytes 266272 | tf_op jit(solution)/shard_map/ppermute | solution.py:46
  48.6 5.7 %collective-permute-done.10.rest_8_ = bf16[1024,256]{1,0:T(8,128)(2,1)S(1)} collective-permute-done((bf16[1024,256]{1,0:T(8,128)(2,1)}, bf16[1024,256]{1,0:T(8,128)(2,1)S(1)}, u32[]{:S(2)}, u32[]{:S(2)}) %collective-permute-start.10) | collective-permute-done | bytes 524320 | tf_op jit(solution)/shard_map/ppermute | solution.py:46
  55.0 1.4 %collective-permute-done.16.rest_9_ = bf16[1024,256]{1,0:T(8,128)(2,1)S(1)} collective-permute-done((bf16[1024,256]{1,0:T(8,128)(2,1)S(1)}, bf16[1024,256]{1,0:T(8,128)(2,1)S(1)}, u32[]{:S(2)}, u32[]{:S(2)}) %collective-permute-start.16) | collective-permute-done | bytes 524320 | tf_op jit(solution)/shard_map/ppermute | solution.py:46
  57.2 8.7 %attend.1 = (bf16[512,128]{1,0:T(8,128)(2,1)S(1)}, bf16[512,128]{1,0:T(8,128)(2,1)S(1)}, bf16[512,128]{1,0:T(8,128)(2,1)S(1)}, bf16[512,128]{1,0:T(8,128)(2,1)S(1)}) custom-call(s32[32,32]{1,0:T(8,128)S(1)} %get-tuple-element.76.list_ref, s32[32]{0:T(128)S(1)} %slice_reduce_fusion.count_ref, s32[32]{0:T(128)S(1)} %get-tuple-element.78.order_ref, ...), custom_call_target="tpu_custom_call" | custom-call | flops 2147483648 | bytes 10485760 | tf_op jit(solution)/shard_map/attend/pallas_call | solution.py:181
  65.8 2.9 %collective-permute-start.19 = (bf16[512,128]{1,0:T(8,128)(2,1)S(1)}, bf16[512,128]{1,0:T(8,128)(2,1)S(1)}, u32[]{:S(2)}, u32[]{:S(2)}) collective-permute-start(bf16[512,128]{1,0:T(8,128)(2,1)S(1)} %get-tuple-element.93.c0), channel_id=1, source_target_pairs={{0,1},{1,0},{2,3},{3,2},{4,5},{5,4},{6,7},{7,6},{8,9},{9,8},{10,11... | collective-permute-start | bytes 393224 | tf_op jit(solution)/shard_map/ppermute | solution.py:46
  68.7 1.5 %collective-permute-start.20 = (bf16[512,128]{1,0:T(8,128)(2,1)S(1)}, bf16[512,128]{1,0:T(8,128)(2,1)S(1)}, u32[]{:S(2)}, u32[]{:S(2)}) collective-permute-start(bf16[512,128]{1,0:T(8,128)(2,1)S(1)} %get-tuple-element.94), channel_id=1, source_target_pairs={{0,65},{1,64},{2,67},{3,66},{4,69},{5,68},{6,71},{7,70},{8,73},{9,... | collective-permute-start | bytes 393224 | tf_op jit(solution)/shard_map/ppermute | solution.py:46
  70.2 3.2 %collective-permute-start.26 = (bf16[512,128]{1,0:T(8,128)(2,1)S(1)}, bf16[512,128]{1,0:T(8,128)(2,1)S(1)}, u32[]{:S(2)}, u32[]{:S(2)}) collective-permute-start(bf16[512,128]{1,0:T(8,128)(2,1)S(1)} %get-tuple-element.104.c0), channel_id=1, source_target_pairs={{0,1},{1,0},{2,3},{3,2},{4,5},{5,4},{6,7},{7,6},{8,9},{9,8},{10,11... | collective-permute-start | bytes 393224 | tf_op jit(solution)/shard_map/ppermute | solution.py:46
  73.4 1.5 %collective-permute-start.27 = (bf16[512,128]{1,0:T(8,128)(2,1)S(1)}, bf16[512,128]{1,0:T(8,128)(2,1)S(1)}, u32[]{:S(2)}, u32[]{:S(2)}) collective-permute-start(bf16[512,128]{1,0:T(8,128)(2,1)S(1)} %get-tuple-element.105), channel_id=1, source_target_pairs={{0,65},{1,64},{2,67},{3,66},{4,69},{5,68},{6,71},{7,70},{8,73},{9,... | collective-permute-start | bytes 393224 | tf_op jit(solution)/shard_map/ppermute | solution.py:46
  75.1 1.2 %pack_weight.3.weight_ref = bf16[512,1024]{1,0:T(8,128)(2,1)S(1)} custom-call(s32[3]{0:T(128)S(1)} %pad_add_fusion.1.spot_ref, bf16[256,2048]{1,0:T(8,128)(2,1)S(1)} %copy-done.3, bf16[256,1024]{1,0:T(8,128)(2,1)} %collective-permute-done.9.refs_0_), custom_call_target="tpu_custom_call" | custom-call | flops 1024 | bytes 1024 | tf_op jit(solution)/shard_map/pack_weight/pallas_call | solution.py:217
  77.9 1.5 %collective-permute-start.22 = (bf16[256,256]{1,0:T(8,128)(2,1)S(1)}, bf16[256,256]{1,0:T(8,128)(2,1)S(1)}, u32[]{:S(2)}, u32[]{:S(2)}) collective-permute-start(bf16[256,256]{1,0:T(8,128)(2,1)S(1)} %get-tuple-element.101), channel_id=1, source_target_pairs={{0,6},{1,7},{2,0},{3,1},{4,2},{5,3},{6,4},{7,5},{8,14},{9,15},{10,... | collective-permute-start | bytes 393224 | tf_op jit(solution)/shard_map/ppermute | solution.py:46
  80.6 2.6 %collective-permute-done.27.c3 = bf16[512,128]{1,0:T(8,128)(2,1)S(1)} collective-permute-done((bf16[512,128]{1,0:T(8,128)(2,1)S(1)}, bf16[512,128]{1,0:T(8,128)(2,1)S(1)}, u32[]{:S(2)}, u32[]{:S(2)}) %collective-permute-start.27) | collective-permute-done | bytes 131104 | tf_op jit(solution)/shard_map/ppermute | solution.py:46
  84.4 1.5 %collective-permute-start.29 = (bf16[256,256]{1,0:T(8,128)(2,1)S(1)}, bf16[256,256]{1,0:T(8,128)(2,1)S(1)}, u32[]{:S(2)}, u32[]{:S(2)}) collective-permute-start(bf16[256,256]{1,0:T(8,128)(2,1)S(1)} %get-tuple-element.110), channel_id=1, source_target_pairs={{0,6},{1,7},{2,0},{3,1},{4,2},{5,3},{6,4},{7,5},{8,14},{9,15},{10,... | collective-permute-start | bytes 393224 | tf_op jit(solution)/shard_map/ppermute | solution.py:46
  86.1 1.8 %collective-permute-start.23 = (bf16[512,256]{1,0:T(8,128)(2,1)S(1)}, bf16[512,256]{1,0:T(8,128)(2,1)S(1)}, u32[]{:S(2)}, u32[]{:S(2)}) collective-permute-start(bf16[512,256]{1,0:T(8,128)(2,1)S(1)} %get-tuple-element.102), channel_id=1, source_target_pairs={{0,2},{1,3},{2,4},{3,5},{4,6},{5,7},{6,0},{7,1},{8,10},{9,11},{10,... | collective-permute-start | bytes 786440 | tf_op jit(solution)/shard_map/ppermute | solution.py:46
  88.2 2.2 %collective-permute-done.28.up_ref = bf16[256,256]{1,0:T(8,128)(2,1)S(1)} collective-permute-done((bf16[256,256]{1,0:T(8,128)(2,1)S(1)}, bf16[256,256]{1,0:T(8,128)(2,1)S(1)}, u32[]{:S(2)}, u32[]{:S(2)}) %collective-permute-start.28) | collective-permute-done | bytes 131104 | tf_op jit(solution)/shard_map/ppermute | solution.py:46
  90.7 1.4 %collective-permute-start.30 = (bf16[512,256]{1,0:T(8,128)(2,1)S(1)}, bf16[512,256]{1,0:T(8,128)(2,1)S(1)}, u32[]{:S(2)}, u32[]{:S(2)}) collective-permute-start(bf16[512,256]{1,0:T(8,128)(2,1)S(1)} %get-tuple-element.111), channel_id=1, source_target_pairs={{0,2},{1,3},{2,4},{3,5},{4,6},{5,7},{6,0},{7,1},{8,10},{9,11},{10,... | collective-permute-start | bytes 786440 | tf_op jit(solution)/shard_map/ppermute | solution.py:46
  92.8 3.1 %collective-permute-done.23.refs_1_ = bf16[512,256]{1,0:T(8,128)(2,1)S(1)} collective-permute-done((bf16[512,256]{1,0:T(8,128)(2,1)S(1)}, bf16[512,256]{1,0:T(8,128)(2,1)S(1)}, u32[]{:S(2)}, u32[]{:S(2)}) %collective-permute-start.23) | collective-permute-done | bytes 262176 | tf_op jit(solution)/shard_map/ppermute | solution.py:46
  95.9 2.3 %collective-permute-done.24.refs_2_ = bf16[512,256]{1,0:T(8,128)(2,1)S(1)} collective-permute-done((bf16[512,256]{1,0:T(8,128)(2,1)S(1)}, bf16[512,256]{1,0:T(8,128)(2,1)S(1)}, u32[]{:S(2)}, u32[]{:S(2)}) %collective-permute-start.24) | collective-permute-done | bytes 262176 | tf_op jit(solution)/shard_map/ppermute | solution.py:46
  98.3 2.2 %collective-permute-done.30.refs_4_ = bf16[512,256]{1,0:T(8,128)(2,1)S(1)} collective-permute-done((bf16[512,256]{1,0:T(8,128)(2,1)S(1)}, bf16[512,256]{1,0:T(8,128)(2,1)S(1)}, u32[]{:S(2)}, u32[]{:S(2)}) %collective-permute-start.30) | collective-permute-done | bytes 262176 | tf_op jit(solution)/shard_map/ppermute | solution.py:46
  100.5 1.4 %collective-permute-done.31.refs_5_ = bf16[512,256]{1,0:T(8,128)(2,1)S(1)} collective-permute-done((bf16[512,256]{1,0:T(8,128)(2,1)S(1)}, bf16[512,256]{1,0:T(8,128)(2,1)S(1)}, u32[]{:S(2)}, u32[]{:S(2)}) %collective-permute-start.31) | collective-permute-done | bytes 262176 | tf_op jit(solution)/shard_map/ppermute | solution.py:46
  (71 shorter events, 12.1 us)
Async XLA Ops:
  6.5 15.1 %collective-permute-start.3 = (bf16[1024,256]{1,0:T(8,128)(2,1)}, bf16[1024,256]{1,0:T(8,128)(2,1)}, u32[]{:S(2)}, u32[]{:S(2)}) collective-permute-start(bf16[1024,256]{1,0:T(8,128)(2,1)} %get-tuple-element.60), channel_id=1, source_target_pairs={{0,64},{1,65},{2,66},{3,67},{4,68},{5,69},{6,70},{7,71},{8,72},{9,... | collective-permute-start | bytes 1572872 | tf_op jit(solution)/shard_map/ppermute | solution.py:46
  8.1 1.1 %collective-permute-start = (s32[16]{0:T(128)S(1)}, s32[16]{0:T(128)S(1)}, u32[]{:S(2)}, u32[]{:S(2)}) collective-permute-start(s32[16]{0:T(128)S(1)} %copy-done.8), channel_id=1, source_target_pairs={{0,8},{1,9},{2,10},{3,11},{4,12},{5,13},{6,14},{7,15},{8,0},{9,1},... | collective-permute-start | bytes 200 | tf_op jit(solution)/shard_map/ppermute | solution.py:46
  9.2 15.6 %collective-permute-start.6 = (bf16[1024,256]{1,0:T(8,128)(2,1)}, bf16[1024,256]{1,0:T(8,128)(2,1)}, u32[]{:S(2)}, u32[]{:S(2)}) collective-permute-start(bf16[1024,256]{1,0:T(8,128)(2,1)} %get-tuple-element.62.rest_0_), channel_id=1, source_target_pairs={{0,8},{1,9},{2,10},{3,11},{4,12},{5,13},{6,14},{7,15},{8,0},{9,1},... | collective-permute-start | bytes 1572872 | tf_op jit(solution)/shard_map/ppermute | solution.py:46
  9.4 18.3 %collective-permute-start.2 = (bf16[1024,256]{1,0:T(8,128)(2,1)}, bf16[1024,256]{1,0:T(8,128)(2,1)}, u32[]{:S(2)}, u32[]{:S(2)}) collective-permute-start(bf16[1024,256]{1,0:T(8,128)(2,1)} %get-tuple-element.62.rest_0_), channel_id=1, source_target_pairs={{0,48},{1,49},{2,50},{3,51},{4,52},{5,53},{6,54},{7,55},{8,56},{9,... | collective-permute-start | bytes 1572872 | tf_op jit(solution)/shard_map/ppermute | solution.py:46
  13.4 15.7 %collective-permute-start.1 = (bf16[1024,256]{1,0:T(8,128)(2,1)}, bf16[1024,256]{1,0:T(8,128)(2,1)}, u32[]{:S(2)}, u32[]{:S(2)}) collective-permute-start(bf16[1024,256]{1,0:T(8,128)(2,1)} %get-tuple-element.62.rest_0_), channel_id=1, source_target_pairs={{0,16},{1,17},{2,18},{3,19},{4,20},{5,21},{6,22},{7,23},{8,24},{9,... | collective-permute-start | bytes 1572872 | tf_op jit(solution)/shard_map/ppermute | solution.py:46
  21.6 18.3 %collective-permute-start.5 = (bf16[1024,256]{1,0:T(8,128)(2,1)}, bf16[1024,256]{1,0:T(8,128)(2,1)S(1)}, u32[]{:S(2)}, u32[]{:S(2)}) collective-permute-start(bf16[1024,256]{1,0:T(8,128)(2,1)} %collective-permute-done.3.rest_2_), channel_id=1, source_target_pairs={{0,48},{1,49},{2,50},{3,51},{4,52},{5,53},{6,54},{7,55},{8,56},{9,... | collective-permute-start | bytes 1572872 | tf_op jit(solution)/shard_map/ppermute | solution.py:46
  24.8 15.1 %collective-permute-start.4 = (bf16[1024,256]{1,0:T(8,128)(2,1)}, bf16[1024,256]{1,0:T(8,128)(2,1)S(1)}, u32[]{:S(2)}, u32[]{:S(2)}) collective-permute-start(bf16[1024,256]{1,0:T(8,128)(2,1)} %collective-permute-done.3.rest_2_), channel_id=1, source_target_pairs={{0,16},{1,17},{2,18},{3,19},{4,20},{5,21},{6,22},{7,23},{8,24},{9,... | collective-permute-start | bytes 1572872 | tf_op jit(solution)/shard_map/ppermute | solution.py:46
  24.8 15.1 %collective-permute-start.9 = (bf16[256,1024]{1,0:T(8,128)(2,1)}, bf16[256,1024]{1,0:T(8,128)(2,1)}, u32[]{:S(2)}, u32[]{:S(2)}) collective-permute-start(bf16[256,1024]{1,0:T(8,128)(2,1)} %pack_weight.2), channel_id=1, source_target_pairs={{0,1},{1,0},{2,3},{3,2},{4,5},{5,4},{6,7},{7,6},{8,9},{9,8},{10,11... | collective-permute-start | bytes 1572872 | tf_op jit(solution)/shard_map/ppermute | solution.py:46
  27.7 12.2 %collective-permute-start.8 = (bf16[1024,256]{1,0:T(8,128)(2,1)}, bf16[1024,256]{1,0:T(8,128)(2,1)S(1)}, u32[]{:S(2)}, u32[]{:S(2)}) collective-permute-start(bf16[1024,256]{1,0:T(8,128)(2,1)} %collective-permute-done.2.rest_4_), channel_id=1, source_target_pairs={{0,8},{1,9},{2,10},{3,11},{4,12},{5,13},{6,14},{7,15},{8,0},{9,1},... | collective-permute-start | bytes 1572872 | tf_op jit(solution)/shard_map/ppermute | solution.py:46
  29.2 10.8 %collective-permute-start.7 = (bf16[1024,256]{1,0:T(8,128)(2,1)}, bf16[1024,256]{1,0:T(8,128)(2,1)S(1)}, u32[]{:S(2)}, u32[]{:S(2)}) collective-permute-start(bf16[1024,256]{1,0:T(8,128)(2,1)} %collective-permute-done.1.rest_12_), channel_id=1, source_target_pairs={{0,8},{1,9},{2,10},{3,11},{4,12},{5,13},{6,14},{7,15},{8,0},{9,1},... | collective-permute-start | bytes 1572872 | tf_op jit(solution)/shard_map/ppermute | solution.py:46
  39.9 7.6 %collective-permute-start.12 = (bf16[1040,128]{1,0:T(8,128)(2,1)}, bf16[1040,128]{1,0:T(8,128)(2,1)S(1)}, u32[]{:S(2)}, u32[]{:S(2)}) collective-permute-start(bf16[1040,128]{1,0:T(8,128)(2,1)} %pad_maximum_fusion), channel_id=1, source_target_pairs={{0,64},{1,65},{2,66},{3,67},{4,68},{5,69},{6,70},{7,71},{8,72},{9,... | collective-permute-start | bytes 798728 | tf_op jit(solution)/shard_map/ppermute | solution.py:46
  40.5 13.9 %collective-permute-start.10 = (bf16[1024,256]{1,0:T(8,128)(2,1)}, bf16[1024,256]{1,0:T(8,128)(2,1)S(1)}, u32[]{:S(2)}, u32[]{:S(2)}) collective-permute-start(bf16[1024,256]{1,0:T(8,128)(2,1)} %collective-permute-done.1.rest_12_), channel_id=1, source_target_pairs={{0,16},{1,17},{2,18},{3,19},{4,20},{5,21},{6,22},{7,23},{8,24},{9,... | collective-permute-start | bytes 1572872 | tf_op jit(solution)/shard_map/ppermute | solution.py:46
  40.5 13.9 %collective-permute-start.11 = (bf16[1024,256]{1,0:T(8,128)(2,1)S(1)}, bf16[1024,256]{1,0:T(8,128)(2,1)S(1)}, u32[]{:S(2)}, u32[]{:S(2)}) collective-permute-start(bf16[1024,256]{1,0:T(8,128)(2,1)S(1)} %collective-permute-done.5.rest_6_), channel_id=1, source_target_pairs={{0,48},{1,49},{2,50},{3,51},{4,52},{5,53},{6,54},{7,55},{8,56},{9,... | collective-permute-start | bytes 1572872 | tf_op jit(solution)/shard_map/ppermute | solution.py:46
  47.5 6.9 %collective-permute-start.13 = (bf16[1024,256]{1,0:T(8,128)(2,1)}, bf16[1024,256]{1,0:T(8,128)(2,1)S(1)}, u32[]{:S(2)}, u32[]{:S(2)}) collective-permute-start(bf16[1024,256]{1,0:T(8,128)(2,1)} %collective-permute-done.3.rest_2_), channel_id=1, source_target_pairs={{0,8},{1,9},{2,10},{3,11},{4,12},{5,13},{6,14},{7,15},{8,0},{9,1},... | collective-permute-start | bytes 1572872 | tf_op jit(solution)/shard_map/ppermute | solution.py:46
  47.5 6.9 %collective-permute-start.14 = (bf16[1024,256]{1,0:T(8,128)(2,1)S(1)}, bf16[1024,256]{1,0:T(8,128)(2,1)S(1)}, u32[]{:S(2)}, u32[]{:S(2)}) collective-permute-start(bf16[1024,256]{1,0:T(8,128)(2,1)S(1)} %collective-permute-done.4.rest_14_), channel_id=1, source_target_pairs={{0,8},{1,9},{2,10},{3,11},{4,12},{5,13},{6,14},{7,15},{8,0},{9,1},... | collective-permute-start | bytes 1572872 | tf_op jit(solution)/shard_map/ppermute | solution.py:46
  48.0 6.4 %collective-permute-start.15 = (bf16[1024,256]{1,0:T(8,128)(2,1)S(1)}, bf16[1024,256]{1,0:T(8,128)(2,1)S(1)}, u32[]{:S(2)}, u32[]{:S(2)}) collective-permute-start(bf16[1024,256]{1,0:T(8,128)(2,1)S(1)} %collective-permute-done.5.rest_6_), channel_id=1, source_target_pairs={{0,8},{1,9},{2,10},{3,11},{4,12},{5,13},{6,14},{7,15},{8,0},{9,1},... | collective-permute-start | bytes 1572872 | tf_op jit(solution)/shard_map/ppermute | solution.py:46
  54.4 2.0 %collective-permute-start.16 = (bf16[1024,256]{1,0:T(8,128)(2,1)S(1)}, bf16[1024,256]{1,0:T(8,128)(2,1)S(1)}, u32[]{:S(2)}, u32[]{:S(2)}) collective-permute-start(bf16[1024,256]{1,0:T(8,128)(2,1)S(1)} %collective-permute-done.10.rest_8_), channel_id=1, source_target_pairs={{0,8},{1,9},{2,10},{3,11},{4,12},{5,13},{6,14},{7,15},{8,0},{9,1},... | collective-permute-start | bytes 1572872 | tf_op jit(solution)/shard_map/ppermute | solution.py:46
  54.5 2.6 %collective-permute-start.17 = (bf16[1024,256]{1,0:T(8,128)(2,1)S(1)}, bf16[1024,256]{1,0:T(8,128)(2,1)S(1)}, u32[]{:S(2)}, u32[]{:S(2)}) collective-permute-start(bf16[1024,256]{1,0:T(8,128)(2,1)S(1)} %collective-permute-done.11.rest_10_), channel_id=1, source_target_pairs={{0,8},{1,9},{2,10},{3,11},{4,12},{5,13},{6,14},{7,15},{8,0},{9,1},... | collective-permute-start | bytes 1572872 | tf_op jit(solution)/shard_map/ppermute | solution.py:46
  65.8 9.1 %collective-permute-start.19 = (bf16[512,128]{1,0:T(8,128)(2,1)S(1)}, bf16[512,128]{1,0:T(8,128)(2,1)S(1)}, u32[]{:S(2)}, u32[]{:S(2)}) collective-permute-start(bf16[512,128]{1,0:T(8,128)(2,1)S(1)} %get-tuple-element.93.c0), channel_id=1, source_target_pairs={{0,1},{1,0},{2,3},{3,2},{4,5},{5,4},{6,7},{7,6},{8,9},{9,8},{10,11... | collective-permute-start | bytes 393224 | tf_op jit(solution)/shard_map/ppermute | solution.py:46
  68.7 7.9 %collective-permute-start.20 = (bf16[512,128]{1,0:T(8,128)(2,1)S(1)}, bf16[512,128]{1,0:T(8,128)(2,1)S(1)}, u32[]{:S(2)}, u32[]{:S(2)}) collective-permute-start(bf16[512,128]{1,0:T(8,128)(2,1)S(1)} %get-tuple-element.94), channel_id=1, source_target_pairs={{0,65},{1,64},{2,67},{3,66},{4,69},{5,68},{6,71},{7,70},{8,73},{9,... | collective-permute-start | bytes 393224 | tf_op jit(solution)/shard_map/ppermute | solution.py:46
  70.2 6.4 %collective-permute-start.18 = (bf16[512,128]{1,0:T(8,128)(2,1)S(1)}, bf16[512,128]{1,0:T(8,128)(2,1)S(1)}, u32[]{:S(2)}, u32[]{:S(2)}) collective-permute-start(bf16[512,128]{1,0:T(8,128)(2,1)S(1)} %get-tuple-element.94), channel_id=1, source_target_pairs={{0,64},{1,65},{2,66},{3,67},{4,68},{5,69},{6,70},{7,71},{8,72},{9,... | collective-permute-start | bytes 393224 | tf_op jit(solution)/shard_map/ppermute | solution.py:46
  70.2 10.4 %collective-permute-start.26 = (bf16[512,128]{1,0:T(8,128)(2,1)S(1)}, bf16[512,128]{1,0:T(8,128)(2,1)S(1)}, u32[]{:S(2)}, u32[]{:S(2)}) collective-permute-start(bf16[512,128]{1,0:T(8,128)(2,1)S(1)} %get-tuple-element.104.c0), channel_id=1, source_target_pairs={{0,1},{1,0},{2,3},{3,2},{4,5},{5,4},{6,7},{7,6},{8,9},{9,8},{10,11... | collective-permute-start | bytes 393224 | tf_op jit(solution)/shard_map/ppermute | solution.py:46
  73.4 9.8 %collective-permute-start.27 = (bf16[512,128]{1,0:T(8,128)(2,1)S(1)}, bf16[512,128]{1,0:T(8,128)(2,1)S(1)}, u32[]{:S(2)}, u32[]{:S(2)}) collective-permute-start(bf16[512,128]{1,0:T(8,128)(2,1)S(1)} %get-tuple-element.105), channel_id=1, source_target_pairs={{0,65},{1,64},{2,67},{3,66},{4,69},{5,68},{6,71},{7,70},{8,73},{9,... | collective-permute-start | bytes 393224 | tf_op jit(solution)/shard_map/ppermute | solution.py:46
  74.9 8.3 %collective-permute-start.25 = (bf16[512,128]{1,0:T(8,128)(2,1)S(1)}, bf16[512,128]{1,0:T(8,128)(2,1)S(1)}, u32[]{:S(2)}, u32[]{:S(2)}) collective-permute-start(bf16[512,128]{1,0:T(8,128)(2,1)S(1)} %get-tuple-element.105), channel_id=1, source_target_pairs={{0,64},{1,65},{2,66},{3,67},{4,68},{5,69},{6,70},{7,71},{8,72},{9,... | collective-permute-start | bytes 393224 | tf_op jit(solution)/shard_map/ppermute | solution.py:46
  77.3 8.6 %collective-permute-start.21 = (bf16[256,256]{1,0:T(8,128)(2,1)S(1)}, bf16[256,256]{1,0:T(8,128)(2,1)S(1)}, u32[]{:S(2)}, u32[]{:S(2)}) collective-permute-start(bf16[256,256]{1,0:T(8,128)(2,1)S(1)} %get-tuple-element.100), channel_id=1, source_target_pairs={{0,2},{1,3},{2,4},{3,5},{4,6},{5,7},{6,0},{7,1},{8,10},{9,11},{10,... | collective-permute-start | bytes 393224 | tf_op jit(solution)/shard_map/ppermute | solution.py:46
  77.9 8.1 %collective-permute-start.22 = (bf16[256,256]{1,0:T(8,128)(2,1)S(1)}, bf16[256,256]{1,0:T(8,128)(2,1)S(1)}, u32[]{:S(2)}, u32[]{:S(2)}) collective-permute-start(bf16[256,256]{1,0:T(8,128)(2,1)S(1)} %get-tuple-element.101), channel_id=1, source_target_pairs={{0,6},{1,7},{2,0},{3,1},{4,2},{5,3},{6,4},{7,5},{8,14},{9,15},{10,... | collective-permute-start | bytes 393224 | tf_op jit(solution)/shard_map/ppermute | solution.py:46
  83.9 6.4 %collective-permute-start.28 = (bf16[256,256]{1,0:T(8,128)(2,1)S(1)}, bf16[256,256]{1,0:T(8,128)(2,1)S(1)}, u32[]{:S(2)}, u32[]{:S(2)}) collective-permute-start(bf16[256,256]{1,0:T(8,128)(2,1)S(1)} %get-tuple-element.109), channel_id=1, source_target_pairs={{0,2},{1,3},{2,4},{3,5},{4,6},{5,7},{6,0},{7,1},{8,10},{9,11},{10,... | collective-permute-start | bytes 393224 | tf_op jit(solution)/shard_map/ppermute | solution.py:46
  84.4 6.2 %collective-permute-start.29 = (bf16[256,256]{1,0:T(8,128)(2,1)S(1)}, bf16[256,256]{1,0:T(8,128)(2,1)S(1)}, u32[]{:S(2)}, u32[]{:S(2)}) collective-permute-start(bf16[256,256]{1,0:T(8,128)(2,1)S(1)} %get-tuple-element.110), channel_id=1, source_target_pairs={{0,6},{1,7},{2,0},{3,1},{4,2},{5,3},{6,4},{7,5},{8,14},{9,15},{10,... | collective-permute-start | bytes 393224 | tf_op jit(solution)/shard_map/ppermute | solution.py:46
  86.1 9.9 %collective-permute-start.23 = (bf16[512,256]{1,0:T(8,128)(2,1)S(1)}, bf16[512,256]{1,0:T(8,128)(2,1)S(1)}, u32[]{:S(2)}, u32[]{:S(2)}) collective-permute-start(bf16[512,256]{1,0:T(8,128)(2,1)S(1)} %get-tuple-element.102), channel_id=1, source_target_pairs={{0,2},{1,3},{2,4},{3,5},{4,6},{5,7},{6,0},{7,1},{8,10},{9,11},{10,... | collective-permute-start | bytes 786440 | tf_op jit(solution)/shard_map/ppermute | solution.py:46
  87.8 10.5 %collective-permute-start.24 = (bf16[512,256]{1,0:T(8,128)(2,1)S(1)}, bf16[512,256]{1,0:T(8,128)(2,1)S(1)}, u32[]{:S(2)}, u32[]{:S(2)}) collective-permute-start(bf16[512,256]{1,0:T(8,128)(2,1)S(1)} %get-tuple-element.103), channel_id=1, source_target_pairs={{0,6},{1,7},{2,0},{3,1},{4,2},{5,3},{6,4},{7,5},{8,14},{9,15},{10,... | collective-permute-start | bytes 786440 | tf_op jit(solution)/shard_map/ppermute | solution.py:46
  90.7 9.7 %collective-permute-start.30 = (bf16[512,256]{1,0:T(8,128)(2,1)S(1)}, bf16[512,256]{1,0:T(8,128)(2,1)S(1)}, u32[]{:S(2)}, u32[]{:S(2)}) collective-permute-start(bf16[512,256]{1,0:T(8,128)(2,1)S(1)} %get-tuple-element.111), channel_id=1, source_target_pairs={{0,2},{1,3},{2,4},{3,5},{4,6},{5,7},{6,0},{7,1},{8,10},{9,11},{10,... | collective-permute-start | bytes 786440 | tf_op jit(solution)/shard_map/ppermute | solution.py:46
  92.2 9.8 %collective-permute-start.31 = (bf16[512,256]{1,0:T(8,128)(2,1)S(1)}, bf16[512,256]{1,0:T(8,128)(2,1)S(1)}, u32[]{:S(2)}, u32[]{:S(2)}) collective-permute-start(bf16[512,256]{1,0:T(8,128)(2,1)S(1)} %get-tuple-element.112), channel_id=1, source_target_pairs={{0,6},{1,7},{2,0},{3,1},{4,2},{5,3},{6,4},{7,5},{8,14},{9,15},{10,... | collective-permute-start | bytes 786440 | tf_op jit(solution)/shard_map/ppermute | solution.py:46
  (9 other events, 112.1 us)
